TPU v7x, 256 devices: a whole 4x4x8 slice. The times are simulated.
256 devices in a mesh: leaf: 32 (over x, y, core), rhs: 8 (over z).
Axes of the slice: x: 4, y: 4, z: 8, core: 2. Of those that a mesh axis runs over, the one named last changes fastest.
Arguments:
- currents: bfloat16 [32, 1024, 256], P('rhs', 'leaf'), may hold values from -6 to 6
- counts: int32 [1024], P('leaf'), may hold values from 16 to 128, as said below
- neighbours: int32 [1024, 9], P('leaf'), may hold values from 0 to 1023, as said below
- source_maps: int32 [1024, 32], P('leaf'), may hold values from 0 to 127
- target_maps: int32 [1024, 1024], P(None, 'leaf'), may hold values from 0 to 127
- source_bases: bfloat16 [1024, 2, 128, 64], P('leaf'), may hold values from -0.375 to 0.375
- level_one: bfloat16 [128, 2, 64, 64], replicated, may hold values from -0.5 to 0.5
- level_two: bfloat16 [128, 2, 64, 64], replicated, may hold values from -0.015625 to 0.015625
- target_bases: bfloat16 [1024, 2, 128, 64], P('leaf'), may hold values from -0.5 to 0.5
- near_blocks: bfloat16 [1024, 9, 2, 128, 128], P('leaf', None, None, 'rhs'), may hold values from -0.125 to 0.125
Outputs:
- fields: float32 [32, 1024, 256], P('rhs', 'leaf')
Inputs may be any that keep to these rules, and one draw needn't show every extreme that they name: `counts`: each box has at least 16 live unknowns; some box has exactly 128. `neighbours`: row t begins with t itself; its other entries are distinct boxes other than t, each at most 8 boxes away from t in box order.
All inputs are finite; a program needn't handle non-finite values.
Results may differ from a plain program's by a relative error of at most 0.0029.
Values may be sent and summed in bfloat16 or wider, within the bound.
No kernel may reach another device: no remote copies, remote signals or barrier semaphores. Data moves between devices by JAX's collectives and lax.ppermute only.
A program may use at most 128 MiB of HBM per device.

v0:
```python
import jax
import jax.numpy as jnp
from jax import lax
from jax.sharding import PartitionSpec as P

SPAN = 8


def extended(cells, sides, width):
    for axis, dim in sides:
        count = lax.axis_size(axis)
        ends = count - 1
        head = lax.slice_in_dim(cells, 0, width, axis=dim)
        tail = lax.slice_in_dim(cells, cells.shape[dim] - width, cells.shape[dim], axis=dim)
        cells = jnp.concatenate(
            [
                lax.ppermute(tail, axis, [(i, (i + 1) % count) for i in range(ends)]),
                cells,
                lax.ppermute(head, axis, [((i + 1) % count, i) for i in range(ends)]),
            ],
            axis=dim,
        )
    return cells


def combine(x):
    return jnp.stack([x[..., 0, 0, :] - x[..., 1, 1, :], x[..., 0, 1, :] + x[..., 1, 0, :]], -2)


def near_rows(picked, blocks):
    raw = jnp.einsum("atncp,tndqp->atcdq", picked, blocks, preferred_element_type=jnp.float32)
    return jnp.stack([raw[:, :, 0, 0] - raw[:, :, 1, 1], raw[:, :, 0, 1] + raw[:, :, 1, 0]], 2)


def shards(
    currents,
    counts,
    neighbours,
    source_maps,
    target_maps,
    source_bases,
    level_one,
    level_two,
    target_bases,
    near_blocks,
):
    high = lax.Precision.HIGHEST
    angles, boxes, doubled = currents.shape
    points = doubled // 2
    rank = level_one.shape[2]
    kernel_count = level_one.shape[0]
    nearby = neighbours.shape[1]
    start = lax.axis_index("leaf") * boxes
    live = jnp.arange(points)[None, :] < counts[:, None]
    masked = currents.reshape(angles, boxes, 2, points) * live[None, :, None, :].astype(
        jnp.bfloat16
    )
    flat = masked.reshape(angles, boxes, doubled)
    window = extended(flat, (("leaf", 1),), SPAN)
    local_ids = (neighbours - start + SPAN).reshape(-1)
    every_angle = lax.all_gather(window, "rhs", axis=0, tiled=True)
    picked = jnp.take(every_angle, local_ids, axis=1).reshape(
        every_angle.shape[0], boxes, nearby, 2, points
    )
    partial_rows = near_rows(picked, near_blocks)
    near = lax.all_to_all(partial_rows, "rhs", split_axis=0, concat_axis=3, tiled=True)
    coef_raw = jnp.einsum(
        "abcp,bdpr->abcdr", masked, source_bases, preferred_element_type=jnp.float32
    )
    coef = combine(coef_raw).astype(jnp.bfloat16)
    selector = (
        target_maps[:, :, None] == jnp.arange(kernel_count, dtype=jnp.int32)[None, None, :]
    ).astype(jnp.bfloat16)
    kernels_two = level_two.astype(jnp.float32)
    bases_out = target_bases.astype(jnp.float32)
    lifted = jnp.einsum("abcr,kdrs->abkcds", coef, level_one, preferred_element_type=jnp.float32)
    every_kernel = combine(lifted).reshape(angles, boxes, kernel_count, 2 * rank)
    pieces = jnp.take_along_axis(every_kernel, source_maps[None, :, :, None], axis=2).astype(
        jnp.bfloat16
    )
    incoming = lax.all_to_all(pieces, "leaf", split_axis=2, concat_axis=1, tiled=True)[:, :, 0, :]
    summed = jnp.einsum("asr,stk->atkr", incoming, selector, preferred_element_type=jnp.float32)
    summed = summed.reshape(incoming.shape[0], boxes, kernel_count, 2, rank)
    far_coef = combine(jnp.einsum("atkcr,kdrs->atcds", summed, kernels_two, precision=high))
    far = combine(jnp.einsum("atcr,tdqr->atcdq", far_coef, bases_out, precision=high))
    total = (near + far) * live[None, :, None, :].astype(jnp.float32)
    return total.reshape(angles, boxes, doubled)


def solution(mesh):
    placed = (
        P("rhs", "leaf", None),
        P("leaf"),
        P("leaf", None),
        P("leaf", None),
        P(None, "leaf"),
        P("leaf", None, None, None),
        P(),
        P(),
        P("leaf", None, None, None),
        P("leaf", None, None, "rhs", None),
    )
    return jax.shard_map(
        shards, mesh=mesh, in_specs=placed, out_specs=P("rhs", "leaf", None), check_vma=False
    )
```

profile of v0, /device:TPU:1, one launch (start us, length us, event | category | flops | bytes accessed | tf_op | source)
XLA Modules:
  0.0 165.1 jit_solution(9380503668601350351)
XLA Ops:
  0.0 0.9 fusion.47
  0.9 0.8 broadcast_multiply_fusion
  1.8 0.6 fusion.51
  2.4 4.6 %collective-permute-start = (bf16[4,8,256]{2,1,0:T(8,128)(2,1)}, bf16[4,8,256]{2,1,0:T(8,128)(2,1)S(1)}, u32[]{:S(2)}, u32[]{:S(2)}) collective-permute-start(bf16[4,8,256]{2,1,0:T(8,128)(2,1)} %get-tuple-element.5), channel_id=1, source_target_pairs={{0,8},{8,16},{16,24},{24,32},{32,40},{40,48},{48,56},{56,64},{64,7... | collective-permute-start | bytes 49160 | tf_op jit(solution)/shard_map/ppermute | solution.py:17
  7.0 1.9 %collective-permute-start.1 = (bf16[4,8,256]{2,1,0:T(8,128)(2,1)S(1)}, bf16[4,8,256]{2,1,0:T(8,128)(2,1)S(1)}, u32[]{:S(2)}, u32[]{:S(2)}) collective-permute-start(bf16[4,8,256]{2,1,0:T(8,128)(2,1)S(1)} %get-tuple-element.6), channel_id=1, source_target_pairs={{8,0},{16,8},{24,16},{32,24},{40,32},{48,40},{56,48},{64,56},{72,6... | collective-permute-start | bytes 49160 | tf_op jit(solution)/shard_map/ppermute | solution.py:19
  8.9 0.9 reshape.296
  9.8 2.1 %convolution_bitcast_fusion.1 = f32[4,32,2,2,64]{4,0,3,2,1:T(4,128)S(1)} fusion(bf16[32,2,128,64]{2,3,1,0:T(8,128)(2,1)} %param.15, bf16[4,32,2,128]{3,2,1,0:T(2,128)(2,1)S(1)} %reshape.296, bf16[32,128]{1,0:T(8,128)(2,1)S(1)} %get-tuple-element.8), kind=kOutput, calls=%fused_computation.26 | convolution fusion | flops 8519680 | bytes 1253376 | tf_op jit(solution)/shard_map/abcp,bdpr->abcdr/dot_general | solution.py:67
  12.0 4.0 %convolution_bitcast_fusion = f32[4,32,128,2,2,64]{2,1,5,4,3,0:T(8,128)S(1)} fusion(bf16[128,2,64,64,1,1]{0,3,2,1,5,4:T(8,128)(2,1)} %bitcast.173, bf16[4,32,2,64,1,1]{3,0,1,2,5,4:T(4,128)(2,1)S(1)} %maximum_bitcast_fusion.1), kind=kOutput, calls=%fused_computation.5 | convolution fusion | flops 536870912 | bytes 18907136 | tf_op jit(solution)/shard_map/abcr,kdrs->abkcds/dot_general | solution.py:76
  16.0 2.4 %fusion.11 = bf16[4,32,128,1,64]{2,1,4,0,3:T(8,128)(2,1)} fusion(f32[4,32,128,2,2,64]{2,1,5,4,3,0:T(8,128)S(1)} %convolution_bitcast_fusion), kind=kLoop, calls=%fused_computation.18 | loop fusion | flops 2097152 | bytes 10485760 | tf_op jit(solution)/shard_map/sub | solution.py:27
  18.4 2.4 %fusion.9 = bf16[4,32,128,1,64]{2,1,4,0,3:T(8,128)(2,1)} fusion(f32[4,32,128,2,2,64]{2,1,5,4,3,0:T(8,128)S(1)} %convolution_bitcast_fusion), kind=kLoop, calls=%fused_computation.15 | loop fusion | flops 2097152 | bytes 10485760 | tf_op jit(solution)/shard_map/add | solution.py:27
  21.0 2.6 %pad_maximum_fusion = bf16[4,32,128,2,64]{2,1,4,0,3:T(8,128)(2,1)S(1)} fusion(bf16[4,32,128,1,64]{2,1,4,0,3:T(8,128)(2,1)} %fusion.9, bf16[4,32,128,1,64]{2,1,4,0,3:T(8,128)(2,1)} %fusion.11), kind=kLoop, calls=%fused_computation.6 | loop fusion | flops 2097152 | bytes 8388608 | tf_op jit(solution)/shard_map/stack | solution.py:27
  23.7 3.6 %copy.143 = bf16[4,32,128,2,64]{2,4,3,1,0:T(8,128)(2,1)} copy(bf16[4,32,128,2,64]{2,1,4,0,3:T(8,128)(2,1)S(1)} %pad_maximum_fusion) | data formatting | bytes 8388608 | tf_op jit(solution)/shard_map/stack | solution.py:27
  27.2 7.5 %copy.144 = bf16[4,32,128,128]{3,0,2,1:T(4,128)(2,1)} copy(bf16[4,32,128,128]{2,3,1,0:T(8,128)(2,1)} %bitcast.170) | data formatting | bytes 8388608 | tf_op jit(solution)/shard_map/reshape | solution.py:77
  34.8 6.7 %gather_fusion.1 = bf16[1024,4,128]{2,1,0:T(4,128)(2,1)S(1)} fusion(bf16[4,32,128,128]{3,0,2,1:T(4,128)(2,1)} %copy.144, s32[1024]{0:T(1024)S(1)} %reshape.308), kind=kCustom, calls=%fused_computation.1 | custom fusion | bytes 2105344 | tf_op jit(solution)/shard_map/jit(take_along_axis)/gather | solution.py:78
  41.5 1.1 copy.145
  42.7 24.6 %all_gather.3 = bf16[32,48,256]{2,1,0:T(8,128)(2,1)S(1)} all-gather(bf16[4,48,256]{2,1,0:T(8,128)(2,1)S(1)} %pad_maximum_fusion.3), channel_id=1, replica_groups=mesh['leaf'=32,'rhs'=8] {'rhs'}, dimensions={0}, use_global_device_ids=true | all-gather | bytes 884736 | tf_op jit(solution)/shard_map/all_gather | solution.py:61
  67.6 13.3 %gather_fusion = bf16[288,32,256]{2,1,0:T(8,128)(2,1)} fusion(bf16[32,48,256]{2,0,1:T(8,128)(2,1)S(1)} %copy.129, s32[1024]{0:T(1024)S(1)} %pad_clamp_fusion), kind=kCustom, calls=%fused_computation | custom fusion | bytes 9438336 | tf_op jit(solution)/shard_map/jit(_take)/gather | solution.py:62
  80.9 7.7 %gather.11 = bf16[32,32,9,2,128]{4,3,0,2,1:T(2,128)(2,1)} reshape(bf16[32,288,256]{2,0,1:T(8,128)(2,1)} %bitcast.169) | data formatting | bytes 9437184 | tf_op jit(solution)/shard_map/jit(_take)/gather | solution.py:62
  88.7 6.1 %fusion.16 = f32[32,32,2,2,16]{0,4,3,2,1:T(8,128)S(1)} fusion(bf16[32,32,9,2,128]{4,3,0,2,1:T(2,128)(2,1)} %gather.11, pred[32,9]{1,0:T(8,128)(4,1)S(1)} %copy.127, bf16[32,9,2,16,128]{4,3,2,1,0:T(8,128)(2,1)S(1)} %copy-done), kind=kOutput, calls=%fused_computation.25 | convolution fusion | flops 153354240 | bytes 7340320 | tf_op jit(solution)/shard_map/atncp,tndqp->atcdq/dot_general | solution.py:31
  94.9 0.5 copy.134
  95.5 0.9 reshape.334
  96.4 3.8 %all-to-all-start = ((f32[8,1,4096]{2,1,0:T(1,128)}), f32[8,1,4096]{2,1,0:T(1,128)S(1)}, u32[]{:S(2)}, u32[]{:S(2)}) async-start(f32[8,1,4096]{2,1,0:T(1,128)} %reshape.334), calls=%async_computation | async-start | bytes 262144 | tf_op jit(solution)/shard_map/all_to_all | solution.py:66
  100.5 1.4 copy.146
  101.8 6.2 %all-to-all-done = f32[8,1,4096]{2,1,0:T(1,128)S(1)} async-done(((f32[8,1,4096]{2,1,0:T(1,128)}), f32[8,1,4096]{2,1,0:T(1,128)S(1)}, u32[]{:S(2)}, u32[]{:S(2)}) %all-to-all-start) | async-done | bytes 131104 | tf_op jit(solution)/shard_map/all_to_all | solution.py:66
  108.1 15.3 %all-to-all-start.1 = ((bf16[4,32,32,128]{3,1,0,2:T(8,128)(2,1)}), bf16[4,32,32,128]{3,1,0,2:T(8,128)(2,1)S(1)}, u32[]{:S(2)}, u32[]{:S(2)}) async-start(bf16[4,32,32,128]{3,1,0,2:T(8,128)(2,1)} %copy.146), calls=%async_computation.1 | async-start | bytes 2097152 | tf_op jit(solution)/shard_map/all_to_all | solution.py:81
  123.4 0.5 broadcast.95
  123.9 1.0 reduce.2
  125.3 15.0 %all-to-all-done.1 = bf16[4,32,32,128]{3,1,0,2:T(8,128)(2,1)S(1)} async-done(((bf16[4,32,32,128]{3,1,0,2:T(8,128)(2,1)}), bf16[4,32,32,128]{3,1,0,2:T(8,128)(2,1)S(1)}, u32[]{:S(2)}, u32[]{:S(2)}) %all-to-all-start.1) | async-done | bytes 1048608 | tf_op jit(solution)/shard_map/all_to_all | solution.py:81
  140.4 14.1 %fusion.1 = f32[32,128,4,128]{1,3,2,0:T(8,128)S(1)} fusion(bf16[4,1024,128,1]{2,1,0,3:T(8,128)(2,1)S(1)} %bitcast.177, s32[1024,32]{0,1:T(8,128)S(1)} %copy-done.7), kind=kOutput, calls=%fused_computation.4 | convolution fusion | flops 4299161600 | bytes 9568256 | tf_op jit(solution)/shard_map/asr,stk->atkr/dot_general | solution.py:82
  154.6 8.8 %fusion.21 = f32[4,32,2,2,64]{4,1,3,2,0:T(8,128)S(1)} fusion(bf16[128,2,64,64]{0,3,2,1:T(8,128)(2,1)S(1)} %copy-done.3, f32[4,32,128,2,64,1]{2,4,3,0,1,5:T(8,128)S(1)} %bitcast.171), kind=kOutput, calls=%fused_computation.28 | convolution fusion | flops 3221225472 | bytes 10616832 | tf_op jit(solution)/shard_map/atkcr,kdrs->atcds/dot_general | solution.py:84
  163.5 0.6 convolution_bitcast_fusion.2
  164.4 0.7 add_multiply_fusion
  (53 shorter events, 2.1 us)
Async XLA Ops:
  0.0 88.7 %copy-start = (bf16[32,9,2,16,128]{4,3,2,1,0:T(8,128)(2,1)S(1)}, bf16[32,9,2,16,128]{4,3,2,1,0:T(8,128)(2,1)}, u32[]{:S(2)}) copy-start(bf16[32,9,2,16,128]{4,3,2,1,0:T(8,128)(2,1)} %param.19) | copy-start | bytes 7077892
  2.4 40.3 %collective-permute-start = (bf16[4,8,256]{2,1,0:T(8,128)(2,1)}, bf16[4,8,256]{2,1,0:T(8,128)(2,1)S(1)}, u32[]{:S(2)}, u32[]{:S(2)}) collective-permute-start(bf16[4,8,256]{2,1,0:T(8,128)(2,1)} %get-tuple-element.5), channel_id=1, source_target_pairs={{0,8},{8,16},{16,24},{24,32},{32,40},{40,48},{48,56},{56,64},{64,7... | collective-permute-start | bytes 49160 | tf_op jit(solution)/shard_map/ppermute | solution.py:17
  7.0 35.7 %collective-permute-start.1 = (bf16[4,8,256]{2,1,0:T(8,128)(2,1)S(1)}, bf16[4,8,256]{2,1,0:T(8,128)(2,1)S(1)}, u32[]{:S(2)}, u32[]{:S(2)}) collective-permute-start(bf16[4,8,256]{2,1,0:T(8,128)(2,1)S(1)} %get-tuple-element.6), channel_id=1, source_target_pairs={{8,0},{16,8},{24,16},{32,24},{40,32},{48,40},{56,48},{64,56},{72,6... | collective-permute-start | bytes 49160 | tf_op jit(solution)/shard_map/ppermute | solution.py:19
  18.4 2.4 %copy-start.5 = (s32[32,32]{1,0:T(8,128)S(1)}, s32[32,32]{1,0:T(8,128)}, u32[]{:S(2)}) copy-start(s32[32,32]{1,0:T(8,128)} %param.13) | copy-start | bytes 12292
  18.4 2.4 %copy-start.6 = (s32[32,9]{0,1:T(8,128)S(1)}, s32[32,9]{0,1:T(8,128)}, u32[]{:S(2)}) copy-start(s32[32,9]{0,1:T(8,128)} %param.12) | copy-start | bytes 3460
  94.8 5.3 %copy-start.2 = (bf16[1024,4,128]{2,0,1:T(8,128)(2,1)S(1)}, bf16[1024,4,128]{2,0,1:T(8,128)(2,1)}, u32[]{:S(2)}) copy-start(bf16[1024,4,128]{2,0,1:T(8,128)(2,1)} %copy.145) | copy-start | bytes 3145732
  96.4 11.7 %all-to-all-start = ((f32[8,1,4096]{2,1,0:T(1,128)}), f32[8,1,4096]{2,1,0:T(1,128)S(1)}, u32[]{:S(2)}, u32[]{:S(2)}) async-start(f32[8,1,4096]{2,1,0:T(1,128)} %reshape.334), calls=%async_computation | async-start | bytes 262144 | tf_op jit(solution)/shard_map/all_to_all | solution.py:66
  100.4 39.9 %copy-start.7 = (s32[1024,32]{0,1:T(8,128)S(1)}, s32[1024,32]{0,1:T(8,128)}, u32[]{:S(2)}) copy-start(s32[1024,32]{0,1:T(8,128)} %param.14) | copy-start | bytes 393220
  108.1 32.2 %all-to-all-start.1 = ((bf16[4,32,32,128]{3,1,0,2:T(8,128)(2,1)}), bf16[4,32,32,128]{3,1,0,2:T(8,128)(2,1)S(1)}, u32[]{:S(2)}, u32[]{:S(2)}) async-start(bf16[4,32,32,128]{3,1,0,2:T(8,128)(2,1)} %copy.146), calls=%async_computation.1 | async-start | bytes 2097152 | tf_op jit(solution)/shard_map/all_to_all | solution.py:81
  140.4 14.2 %copy-start.3 = (bf16[128,2,64,64]{0,3,2,1:T(8,128)(2,1)S(1)}, bf16[128,2,64,64]{0,3,2,1:T(8,128)(2,1)}, u32[]{:S(2)}) copy-start(bf16[128,2,64,64]{0,3,2,1:T(8,128)(2,1)} %param.17) | copy-start | bytes 6291460
  154.5 8.9 %copy-start.4 = (bf16[32,2,128,64]{2,3,1,0:T(8,128)(2,1)S(1)}, bf16[32,2,128,64]{2,3,1,0:T(8,128)(2,1)}, u32[]{:S(2)}) copy-start(bf16[32,2,128,64]{2,3,1,0:T(8,128)(2,1)} %param.18) | copy-start | bytes 3145732
  154.6 10.5 %copy-start.1 = (bf16[32,9,2,16,128]{4,3,2,1,0:T(8,128)(2,1)S(1)}, bf16[32,9,2,16,128]{4,3,2,1,0:T(8,128)(2,1)}, u32[]{:S(2)}) copy-start(bf16[32,9,2,16,128]{4,3,2,1,0:T(8,128)(2,1)} %param.19) | copy-start | bytes 7077892
where the time goes:
time: 166 us; the launch traced here: 165 us
  local copies, waits for them, and re-layouts  46.1 us (28%)
  matrix products  35.8 us (22%)
  starting transfers between devices  25.6 us (15%)
  blocking collectives  24.6 us (15%)
  waiting for transfers between devices  21.2 us (13%)
  other arithmetic  11.4 us (7%)
    all_gather x1, blocking collectives, shards(): every_angle = lax.all_gather(window, 'rhs', axis=0, tiled=True)  24.6 us
    gather x2, local copies, waits for them, and re-layouts, shards(): jnp.take(every_angle, local_ids, axis=1)  21.1 us
    all_to_all x1, starting transfers between devices, shards(): lax.all_to_all(pieces, 'leaf', split_axis=2, concat_axis=1, tiled=True)  15.3 us
    all_to_all x1, waiting for transfers between devices, shards(): lax.all_to_all(pieces, 'leaf', split_axis=2, concat_axis=1, tiled=True)  15 us
    dot_general x1, matrix products, shards(): jnp.einsum('asr,stk->atkr', incoming, selector, preferred_element_type=jn...  14.1 us
    dot_general x1, matrix products, shards(): jnp.einsum('atkcr,kdrs->atcds', summed, kernels_two, precision=high)  8.82 us
    gather x3, local copies, waits for them, and re-layouts, shards(): jnp.take_along_axis(every_kernel, source_maps[None, :, :, None], axis=2)  7.84 us
    reshape x1, local copies, waits for them, and re-layouts, shards(): combine(lifted).reshape(angles, boxes, kernel_count, 2 * rank)  7.53 us
  transfers between devices with their start and end apart: 4, of which 2 were waited for; matrix products, arithmetic and copies ran while one was open for 23% of the time, Pallas kernels for 0%

commit v1 on v0

v1 whole, which is shorter than its diff:
```python
import jax
import jax.numpy as jnp
from jax import lax
from jax.experimental import pallas as pl
from jax.experimental.pallas import tpu as pltpu
from jax.sharding import PartitionSpec as P

SPAN = 8
PITCH = 129
F32 = jnp.float32
BF16 = jnp.bfloat16
VMEM = pl.BlockSpec(memory_space=pltpu.VMEM)
SMEM = pl.BlockSpec(memory_space=pltpu.SMEM)
NT = (((1,), (1,)), ((), ()))


def params(mib):
    return pltpu.CompilerParams(vmem_limit_bytes=mib * 2**20)


def live_lanes(counts_ref, boxes, points):
    row = lax.broadcasted_iota(jnp.int32, (boxes, points), 0)
    limit = jnp.zeros((boxes, points), jnp.int32)
    for box in range(boxes):
        limit = jnp.where(row == box, counts_ref[box], limit)
    lane = lax.broadcasted_iota(jnp.int32, (boxes, points), 1)
    return lane < limit


def mask_kernel(counts_ref, currents_ref, masked_ref, copies_ref):
    angles, boxes, doubled = currents_ref.shape
    points = doubled // 2
    live = live_lanes(counts_ref, boxes, points)
    for a in range(angles):
        for c in range(2):
            lanes = slice(c * points, (c + 1) * points)
            kept = jnp.where(live, currents_ref[a, :, lanes].astype(F32), 0.0).astype(BF16)
            masked_ref[a, :, lanes] = kept
            for z in range(copies_ref.shape[0]):
                copies_ref[z, a, :, lanes] = kept


def beside(*parts):
    return jnp.concatenate(parts, axis=1)


def above(*parts):
    return jnp.concatenate(parts, axis=0)


def turn_kernels(kernels_ref, turned):
    _, rank, _, kernel_count = kernels_ref.shape

    def one(r, _):
        real, imag = kernels_ref[0, r], kernels_ref[1, r]
        turned[pl.ds(r, kernel_count, stride=PITCH), :] = above(real, imag).T.astype(F32)
        turned[pl.ds(rank + r, kernel_count, stride=PITCH), :] = above(-imag, real).T.astype(F32)
        return 0

    lax.fori_loop(0, rank, one, 0, unroll=4)


def lift_kernel(maps_ref, masked_ref, bases_ref, kernels_ref, out_ref, rows, raws, turned, lifted, staged):
    angles, boxes, doubled = masked_ref.shape
    points = doubled // 2
    _, rank, _, kernel_count = kernels_ref.shape
    groups = out_ref.shape[0]
    wide = 2 * rank
    each = 2 * angles
    for a in range(angles):
        for c in range(2):
            rows[pl.ds(c * angles + a, boxes, stride=each), :] = masked_ref[
                a, :, c * points : (c + 1) * points
            ].astype(F32)
    for box in range(boxes):
        x = rows[each * box : each * (box + 1), :].astype(BF16)
        raws[each * box : each * (box + 1), :] = lax.dot_general(
            x, above(bases_ref[box, 0], bases_ref[box, 1]), NT, preferred_element_type=F32
        )
    raw = raws[...].reshape(boxes, 2, angles, wide)
    crossed = pltpu.roll(raw[:, 1].reshape(boxes * angles, wide), rank, 1)
    lane = lax.broadcasted_iota(jnp.int32, crossed.shape, 1)
    straight = raw[:, 0].reshape(boxes * angles, wide)
    coef = (straight + jnp.where(lane < rank, -crossed, crossed)).astype(BF16)
    turn_kernels(kernels_ref, turned)

    def pair(step, _):
        k = 2 * step
        weights = beside(turned[pl.ds(k * PITCH, wide), :], turned[pl.ds((k + 1) * PITCH, wide), :])
        both = jnp.dot(coef, weights.astype(BF16), preferred_element_type=F32)
        lifted[k] = both[:, :wide]
        lifted[k + 1] = both[:, wide:]
        return 0

    lax.fori_loop(0, kernel_count // 2, pair, 0, unroll=16)
    pitch = boxes + 1

    def one_group(g, slot):
        for box in range(boxes):
            k = maps_ref[box, g]
            staged[slot, pl.ds(box, angles, stride=pitch), :] = lifted[
                k, angles * box : angles * (box + 1), :
            ]
        for a in range(angles):
            out_ref[g, :, a * wide : (a + 1) * wide] = staged[
                slot, a * pitch : a * pitch + boxes, :
            ].astype(BF16)

    def two_groups(step, _):
        one_group(2 * step, 0)
        one_group(2 * step + 1, 1)
        return 0

    lax.fori_loop(0, groups // 2, two_groups, 0)


def pack_kernel(every_ref, out_ref, head_ref, tail_ref, spread):
    parts, angles, boxes, doubled = every_ref.shape
    points = doubled // 2
    total = parts * angles
    pitch = total + 1
    for z in range(parts):
        for a in range(angles):
            for c in range(2):
                spread[c, pl.ds(a * parts + z, boxes, stride=pitch), :] = every_ref[
                    z, a, :, c * points : (c + 1) * points
                ].astype(F32)
    for box in range(boxes):
        for c in range(2):
            lanes = slice(c * points, (c + 1) * points)
            rows = spread[c, box * pitch : box * pitch + total, :].astype(BF16)
            out_ref[box, :, lanes] = rows
            if box < SPAN:
                head_ref[box, :, lanes] = rows
            if box >= boxes - SPAN:
                tail_ref[box - (boxes - SPAN), :, lanes] = rows


def near_rows(sources, ids, blocks_ref, t, total, angles):
    nearby, _, owned, points = blocks_ref.shape[1:]
    parts = total // angles
    held, weights = [], []
    for n in range(nearby):
        held.append(sources[ids[n]])
        real, imag = blocks_ref[t, n, 0], blocks_ref[t, n, 1]
        weights.append(above(beside(real, -imag), beside(imag, real)))
    summed = lax.dot_general(beside(*held), beside(*weights), NT, preferred_element_type=F32)
    return beside(*[summed[a * parts : (a + 1) * parts] for a in range(angles)])


def inner_kernel(neighbours_ref, own_ref, blocks_ref, out_ref, rows):
    boxes, total, _ = own_ref.shape
    parts, inner, lanes = out_ref.shape
    angles = total // parts
    pitch = inner + 1

    def target(step, _):
        t = SPAN + step
        ids = [t + neighbours_ref[n, t] - neighbours_ref[0, t] for n in range(blocks_ref.shape[1])]
        rows[pl.ds(step, parts, stride=pitch), :] = near_rows(own_ref, ids, blocks_ref, t, total, angles)
        return 0

    lax.fori_loop(0, inner, target, 0, unroll=4)
    for z in range(parts):
        out_ref[z] = rows[z * pitch : z * pitch + inner, :].astype(BF16)


def outer_kernel(neighbours_ref, own_ref, before_ref, after_ref, inner_ref, blocks_ref, out_ref, window, rows):
    boxes, total, _ = own_ref.shape
    parts, _, lanes = out_ref.shape
    angles = total // parts
    pitch = boxes + 1
    window[:SPAN] = before_ref[...]
    window[SPAN : 3 * SPAN] = own_ref[: 2 * SPAN]
    window[3 * SPAN : 5 * SPAN] = own_ref[boxes - 2 * SPAN :]
    window[5 * SPAN :] = after_ref[...]

    def target(step, _):
        late = step // SPAN
        t = step + late * (boxes - 2 * SPAN)
        base = step + SPAN + late * 2 * SPAN - neighbours_ref[0, t]
        ids = [base + neighbours_ref[n, t] for n in range(blocks_ref.shape[1])]
        rows[pl.ds(t, parts, stride=pitch), :] = near_rows(window, ids, blocks_ref, t, total, angles)
        return 0

    lax.fori_loop(0, 2 * SPAN, target, 0, unroll=4)
    for z in range(parts):
        out_ref[z, :SPAN] = rows[z * pitch : z * pitch + SPAN, :].astype(BF16)
        out_ref[z, SPAN : boxes - SPAN] = inner_ref[z]
        out_ref[z, boxes - SPAN :] = rows[z * pitch + boxes - SPAN : z * pitch + boxes, :].astype(BF16)


CHUNK = 32


def far_kernel(maps_ref, pieces_ref, kernels_ref, bases_ref, out_ref, table, turned, total_ref):
    sources, lanes = pieces_ref.shape
    _, rank, _, kernel_count = kernels_ref.shape
    boxes, _, _, points = bases_ref.shape
    wide = 2 * rank
    angles = lanes // wide
    turn_kernels(kernels_ref, turned)
    table[...] = maps_ref[...].astype(F32).astype(BF16)
    total_ref[...] = jnp.zeros_like(total_ref)
    one, zero = jnp.ones((), BF16), jnp.zeros((), BF16)

    def chunk(step, _):
        first = step * CHUNK
        maps = table[...]
        chosen = above(*[jnp.where(maps == (first + i).astype(BF16), one, zero) for i in range(CHUNK)])
        summed = jnp.dot(chosen, pieces_ref[...], preferred_element_type=F32)
        xs, weights = [], []
        for i in range(CHUNK):
            x = above(
                *[summed[i * boxes : (i + 1) * boxes, a * wide : (a + 1) * wide] for a in range(angles)]
            )
            w = turned[pl.ds((first + i) * PITCH, wide), :].astype(BF16)
            high = x.astype(BF16)
            xs += [high, (x - high.astype(F32)).astype(BF16)]
            weights += [w, w]
        total_ref[...] += jnp.dot(beside(*xs), above(*weights), preferred_element_type=F32)
        return 0

    lax.fori_loop(0, kernel_count // CHUNK, chunk, 0)
    for t in range(boxes):
        x = total_ref[pl.ds(t, angles, stride=boxes), :]
        high = x.astype(BF16).astype(F32)
        both = above(high, x - high).astype(BF16)
        real, imag = bases_ref[t, 0], bases_ref[t, 1]
        weights = beside(above(real, -imag), above(imag, real))
        far = jnp.dot(both, weights, preferred_element_type=F32)
        far = far[:angles] + far[angles:]
        for c in range(2):
            out_ref[c, pl.ds(t, angles, stride=boxes), :] = far[:, c * points : (c + 1) * points]


def finish_kernel(counts_ref, near_ref, far_ref, out_ref):
    parts, boxes, lanes = near_ref.shape
    angles, _, doubled = out_ref.shape
    points = doubled // 2
    owned = points // parts
    live = live_lanes(counts_ref, boxes, points)
    block = lax.broadcasted_iota(jnp.int32, (boxes, points), 1) // owned
    near = [near_ref[z].astype(F32) for z in range(parts)]
    for a in range(angles):
        for c in range(2):
            place = (a * 2 + c) * owned
            joined = jnp.zeros((boxes, points), F32)
            for z in range(parts):
                shift = (z * owned - place) % lanes
                moved = near[z] if shift == 0 else pltpu.roll(near[z], shift, 1)
                joined = jnp.where(block == z, moved, joined)
            lanes_out = slice(c * points, (c + 1) * points)
            far = far_ref[c, a * boxes : (a + 1) * boxes, :]
            out_ref[a, :, lanes_out] = jnp.where(live, joined + far, 0.0)


def shards(
    currents,
    counts,
    neighbours,
    source_maps,
    target_maps,
    source_bases,
    level_one,
    level_two,
    target_bases,
    near_blocks,
):
    angles, boxes, doubled = currents.shape
    points = doubled // 2
    kernel_count, _, rank, _ = level_one.shape
    wide = 2 * rank
    leaves, parts = lax.axis_size("leaf"), lax.axis_size("rhs")
    owned = near_blocks.shape[3]

    lines = lambda x: jnp.swapaxes(x, -1, -2)
    kernels_one = level_one.transpose(1, 2, 3, 0)
    kernels_two = level_two.transpose(1, 2, 3, 0)

    masked, copies = pl.pallas_call(
        mask_kernel,
        out_shape=(
            jax.ShapeDtypeStruct((angles, boxes, doubled), BF16),
            jax.ShapeDtypeStruct((parts, angles, boxes, doubled), BF16),
        ),
        in_specs=[SMEM, VMEM],
        out_specs=(VMEM, VMEM),
        name="mask",
    )(counts, currents)
    every = lax.all_to_all(copies, "rhs", split_axis=0, concat_axis=0, tiled=True)

    pieces = pl.pallas_call(
        lift_kernel,
        out_shape=jax.ShapeDtypeStruct((leaves, boxes, angles * wide), BF16),
        in_specs=[SMEM, VMEM, VMEM, VMEM],
        out_specs=VMEM,
        scratch_shapes=[
            pltpu.VMEM((boxes * 2 * angles, points), F32),
            pltpu.VMEM((boxes * 2 * angles, wide), F32),
            pltpu.VMEM((kernel_count * PITCH, wide), F32),
            pltpu.VMEM((kernel_count, boxes * angles, wide), F32),
            pltpu.VMEM((2, angles * (boxes + 1) + angles, wide), F32),
        ],
        compiler_params=params(32),
        cost_estimate=pl.CostEstimate(flops=2**33, bytes_accessed=8 * 2**20, transcendentals=0),
        name="lift",
    )(source_maps, masked, lines(source_bases), kernels_one)
    incoming = lax.all_to_all(pieces, "leaf", split_axis=0, concat_axis=0, tiled=True)

    total = parts * angles
    own, head, tail = pl.pallas_call(
        pack_kernel,
        out_shape=(
            jax.ShapeDtypeStruct((boxes, total, doubled), BF16),
            jax.ShapeDtypeStruct((SPAN, total, doubled), BF16),
            jax.ShapeDtypeStruct((SPAN, total, doubled), BF16),
        ),
        in_specs=[VMEM],
        out_specs=(VMEM, VMEM, VMEM),
        scratch_shapes=[pltpu.VMEM((2, boxes * (total + 1) + total, points), F32)],
        compiler_params=params(16),
        name="pack",
    )(every)
    before = lax.ppermute(tail, "leaf", [(i, (i + 1) % leaves) for i in range(leaves)])
    after = lax.ppermute(head, "leaf", [((i + 1) % leaves, i) for i in range(leaves)])

    near_ids = neighbours.T
    inner = boxes - 2 * SPAN
    inner_rows = pl.pallas_call(
        inner_kernel,
        out_shape=jax.ShapeDtypeStruct((parts, inner, angles * 2 * owned), BF16),
        in_specs=[SMEM, VMEM, VMEM],
        out_specs=VMEM,
        scratch_shapes=[pltpu.VMEM((parts * (inner + 1) + parts, angles * 2 * owned), F32)],
        compiler_params=params(16),
        cost_estimate=pl.CostEstimate(flops=2**31, bytes_accessed=2**21, transcendentals=0),
        name="inner",
    )(near_ids, own, near_blocks)
    rows = pl.pallas_call(
        outer_kernel,
        out_shape=jax.ShapeDtypeStruct((parts, boxes, angles * 2 * owned), BF16),
        in_specs=[SMEM] + [VMEM] * 5,
        out_specs=VMEM,
        scratch_shapes=[
            pltpu.VMEM((6 * SPAN, total, doubled), BF16),
            pltpu.VMEM((parts * (boxes + 1) + parts, angles * 2 * owned), F32),
        ],
        compiler_params=params(16),
        name="outer",
    )(near_ids, own, before, after, inner_rows, near_blocks)
    near = lax.all_to_all(rows, "rhs", split_axis=0, concat_axis=0, tiled=True)

    far = pl.pallas_call(
        far_kernel,
        out_shape=jax.ShapeDtypeStruct((2, angles * boxes, points), F32),
        in_specs=[VMEM, VMEM, VMEM, VMEM],
        out_specs=VMEM,
        scratch_shapes=[
            pltpu.VMEM((boxes, leaves * boxes), BF16),
            pltpu.VMEM((kernel_count * PITCH, wide), F32),
            pltpu.VMEM((angles * boxes, wide), F32),
        ],
        compiler_params=params(40),
        cost_estimate=pl.CostEstimate(flops=2**33, bytes_accessed=8 * 2**20, transcendentals=0),
        name="far",
    )(target_maps.T, incoming.reshape(leaves * boxes, angles * wide), kernels_two, lines(target_bases))

    return pl.pallas_call(
        finish_kernel,
        out_shape=jax.ShapeDtypeStruct((angles, boxes, doubled), F32),
        in_specs=[SMEM, VMEM, VMEM],
        out_specs=VMEM,
        name="finish",
    )(counts, near, far)


def solution(mesh):
    placed = (
        P("rhs", "leaf", None),
        P("leaf"),
        P("leaf", None),
        P("leaf", None),
        P(None, "leaf"),
        P("leaf", None, None, None),
        P(),
        P(),
        P("leaf", None, None, None),
        P("leaf", None, None, "rhs", None),
    )
    return jax.shard_map(
        shards, mesh=mesh, in_specs=placed, out_specs=P("rhs", "leaf", None), check_vma=False
    )
```

time: 166 us -> 77.5 us (0.47)
  the two profiles are of different devices: /device:TPU:1 before, /device:TPU:32 now
where the time goes in v1:
time: 77.5 us; the launch traced here: 76.9 us
  Pallas kernels  26.3 us (34%)
  starting transfers between devices  25.9 us (33%)
  waiting for transfers between devices  15.2 us (20%)
  local copies, waits for them, and re-layouts  9.43 us (12%)
    ppermute x1, waiting for transfers between devices, shards(): lax.ppermute(tail, 'leaf', [(i, (i + 1) % leaves) for i in range(leaves)])  11.3 us
    pallas_call x1, Pallas kernels, shards(): pl.pallas_call(far_kernel, out_shape=jax.ShapeDtypeStruct((2, angles * bo...  10.8 us
    unnamed x24, local copies, waits for them, and re-layouts  9.43 us
    all_to_all x1, starting transfers between devices, shards(): lax.all_to_all(copies, 'rhs', split_axis=0, concat_axis=0, tiled=True)  8.57 us
    all_to_all x1, starting transfers between devices, shards(): lax.all_to_all(pieces, 'leaf', split_axis=0, concat_axis=0, tiled=True)  7.45 us
    pallas_call x1, Pallas kernels, shards(): pl.pallas_call(lift_kernel, out_shape=jax.ShapeDtypeStruct((leaves, boxes...  6.8 us
    ppermute x1, starting transfers between devices, shards(): lax.ppermute(head, 'leaf', [((i + 1) % leaves, i) for i in range(leaves)])  4.87 us
    all_to_all x1, starting transfers between devices, shards(): near = lax.all_to_all(rows, 'rhs', split_axis=0, concat_axis=0, tiled=True)  4.72 us
  transfers between devices with their start and end apart: 5, of which 2 were waited for; matrix products, arithmetic and copies ran while one was open for 0% of the time, Pallas kernels for 30%

profile of v1, /device:TPU:32, one launch (start us, length us, event | category | flops | bytes accessed | tf_op | source)
XLA Modules:
  0.0 76.9 jit_solution(10998863799913935380)
XLA Ops:
  0.0 1.8 %mask.1 = (bf16[4,32,256]{2,1,0:T(8,128)(2,1)}, bf16[8,4,32,256]{3,2,1,0:T(8,128)(2,1)}) custom-call(s32[32]{0:T(128)} %counts_ref.3, bf16[4,32,256]{2,1,0:T(8,128)(2,1)} %currents_ref.1), custom_call_target="tpu_custom_call" | custom-call | tf_op jit(solution)/shard_map/mask/pallas_call | solution.py:281
  1.8 8.6 %all-to-all-start = ((bf16[8,4,32,256]{3,2,1,0:T(8,128)(2,1)}), bf16[8,4,32,256]{3,2,1,0:T(8,128)(2,1)S(1)}, u32[]{:S(2)}, u32[]{:S(2)}) async-start(bf16[8,4,32,256]{3,2,1,0:T(8,128)(2,1)} %get-tuple-element.10), calls=%async_computation | async-start | bytes 1048576 | tf_op jit(solution)/shard_map/all_to_all | solution.py:291
  10.3 0.0 copy-start.4
  10.3 1.6 %copy-done.4 = bf16[128,2,64,64]{0,3,2,1:T(8,128)(2,1)S(1)} copy-done((bf16[128,2,64,64]{0,3,2,1:T(8,128)(2,1)S(1)}, bf16[128,2,64,64]{0,3,2,1:T(8,128)(2,1)}, u32[]{:S(2)}) %copy-start.4) | copy-done | bytes 2097176
  11.9 1.2 %copy-done.6 = bf16[32,2,128,64]{2,3,1,0:T(8,128)(2,1)S(1)} copy-done((bf16[32,2,128,64]{2,3,1,0:T(8,128)(2,1)S(1)}, bf16[32,2,128,64]{2,3,1,0:T(8,128)(2,1)}, u32[]{:S(2)}) %copy-start.6) | copy-done | bytes 1048600
  13.2 0.8 %copy-done.9 = bf16[4,32,256]{2,1,0:T(8,128)(2,1)S(1)} copy-done((bf16[4,32,256]{2,1,0:T(8,128)(2,1)S(1)}, bf16[4,32,256]{2,1,0:T(8,128)(2,1)}, u32[]{:S(2)}) %copy-start.9) | copy-done | bytes 65560
  14.0 0.7 copy-done.10
  14.7 6.8 %lift.1 = bf16[32,32,512]{2,1,0:T(8,128)(2,1)S(1)} custom-call(s32[32,32]{1,0:T(8,128)S(1)} %copy-done.10, bf16[4,32,256]{2,1,0:T(8,128)(2,1)S(1)} %copy-done.9, bf16[32,2,64,128]{3,2,1,0:T(8,128)(2,1)S(1)} %bitcast.11, bf16[2,64,64,128]{3,2,1,0:T(8,128)(2,1)S(1)} %bitcast.9), custom_call_target="tpu_custom_call" | custom-call | flops 8589934592 | bytes 8388608 | tf_op jit(solution)/shard_map/lift/pallas_call | solution.py:293
  21.5 1.0 %copy-done.1 = bf16[32,32,512]{2,1,0:T(8,128)(2,1)} copy-done((bf16[32,32,512]{2,1,0:T(8,128)(2,1)}, bf16[32,32,512]{2,1,0:T(8,128)(2,1)S(1)}, u32[]{:S(2)}) %copy-start.1) | copy-done | bytes 1048600
  22.5 3.9 %all-to-all-done.every_ref = bf16[8,4,32,256]{3,2,1,0:T(8,128)(2,1)S(1)} async-done(((bf16[8,4,32,256]{3,2,1,0:T(8,128)(2,1)}), bf16[8,4,32,256]{3,2,1,0:T(8,128)(2,1)S(1)}, u32[]{:S(2)}, u32[]{:S(2)}) %all-to-all-start) | async-done | bytes 524320 | tf_op jit(solution)/shard_map/all_to_all | solution.py:291
  26.4 7.4 %all-to-all-start.2 = ((bf16[32,32,512]{2,1,0:T(8,128)(2,1)}), bf16[32,32,512]{2,1,0:T(8,128)(2,1)}, u32[]{:S(2)}, u32[]{:S(2)}) async-start(bf16[32,32,512]{2,1,0:T(8,128)(2,1)} %copy-done.1), calls=%async_computation.2 | async-start | bytes 2097152 | tf_op jit(solution)/shard_map/all_to_all | solution.py:309
  33.8 0.2 pack.1
  34.0 0.3 collective-permute-start
  34.3 4.9 %collective-permute-start.1 = (bf16[8,32,256]{2,1,0:T(8,128)(2,1)S(1)}, bf16[8,32,256]{2,1,0:T(8,128)(2,1)S(1)}, u32[]{:S(2)}, u32[]{:S(2)}) collective-permute-start(bf16[8,32,256]{2,1,0:T(8,128)(2,1)S(1)} %get-tuple-element.13), channel_id=1, source_target_pairs={{8,0},{16,8},{24,16},{32,24},{40,32},{48,40},{56,48},{64,56},{72,6... | collective-permute-start | bytes 393224 | tf_op jit(solution)/shard_map/ppermute | solution.py:326
  39.2 0.0 copy-done
  39.2 0.0 copy-done.3
  39.2 2.1 %inner.1.inner_ref = bf16[8,16,128]{2,1,0:T(8,128)(2,1)S(1)} custom-call(s32[9,32]{1,0:T(8,128)S(1)} %bitcast.7, bf16[32,32,256]{2,1,0:T(8,128)(2,1)S(1)} %get-tuple-element.11.own_ref, bf16[32,9,2,16,128]{4,3,2,1,0:T(8,128)(2,1)S(1)} %copy-done), custom_call_target="tpu_custom_call" | custom-call | flops 2147483648 | bytes 2097152 | tf_op jit(solution)/shard_map/inner/pallas_call | solution.py:330
  41.3 0.0 copy-start.8
  41.3 11.3 %collective-permute-done.before_ref = bf16[8,32,256]{2,1,0:T(8,128)(2,1)S(1)} collective-permute-done((bf16[8,32,256]{2,1,0:T(8,128)(2,1)S(1)}, bf16[8,32,256]{2,1,0:T(8,128)(2,1)S(1)}, u32[]{:S(2)}, u32[]{:S(2)}) %collective-permute-start) | collective-permute-done | bytes 131104 | tf_op jit(solution)/shard_map/ppermute | solution.py:325
  52.6 0.0 collective-permute-done.1.after_ref
  52.6 2.9 %outer.1 = bf16[8,32,128]{2,1,0:T(8,128)(2,1)} custom-call(s32[9,32]{1,0:T(8,128)S(1)} %bitcast.8, bf16[32,32,256]{2,1,0:T(8,128)(2,1)S(1)} %get-tuple-element.11.own_ref, bf16[8,32,256]{2,1,0:T(8,128)(2,1)S(1)} %collective-permute-done.before_ref, bf16[8,32,256]{2,1,0:T(8,128)(2,1)S(1)} %collective-permute-done.1.after_ref, ...), custom_call_target="tpu_custom_call" | custom-call | tf_op jit(solution)/shard_map/outer/pallas_call | solution.py:340
  55.5 0.0 all-to-all-done.2
  55.5 4.7 %all-to-all-start.1 = ((bf16[8,32,128]{2,1,0:T(8,128)(2,1)}), bf16[8,32,128]{2,1,0:T(8,128)(2,1)S(1)}, u32[]{:S(2)}, u32[]{:S(2)}) async-start(bf16[8,32,128]{2,1,0:T(8,128)(2,1)} %outer.1), calls=%async_computation.1 | async-start | bytes 131072 | tf_op jit(solution)/shard_map/all_to_all | solution.py:352
  60.2 0.0 copy-done.8
  60.2 1.6 %copy-done.5 = bf16[128,2,64,64]{0,3,2,1:T(8,128)(2,1)S(1)} copy-done((bf16[128,2,64,64]{0,3,2,1:T(8,128)(2,1)S(1)}, bf16[128,2,64,64]{0,3,2,1:T(8,128)(2,1)}, u32[]{:S(2)}) %copy-start.5) | copy-done | bytes 2097176
  61.8 1.2 %copy-done.7 = bf16[32,2,128,64]{2,3,1,0:T(8,128)(2,1)S(1)} copy-done((bf16[32,2,128,64]{2,3,1,0:T(8,128)(2,1)S(1)}, bf16[32,2,128,64]{2,3,1,0:T(8,128)(2,1)}, u32[]{:S(2)}) %copy-start.7) | copy-done | bytes 1048600
  63.0 10.8 %far.1.far_ref = f32[2,128,128]{2,1,0:T(8,128)S(1)} custom-call(s32[32,1024]{1,0:T(8,128)S(1)} %bitcast.13, bf16[1024,512]{1,0:T(8,128)(2,1)} %bitcast.4.pieces_ref, bf16[2,64,64,128]{3,2,1,0:T(8,128)(2,1)S(1)} %bitcast.10, bf16[32,2,64,128]{3,2,1,0:T(8,128)(2,1)S(1)} %bitcast.12), custom_call_target="tpu_custom_call" | custom-call | flops 8589934592 | bytes 8388608 | tf_op jit(solution)/shard_map/far/pallas_call | solution.py:354
  73.8 0.0 copy-start.2
  73.8 0.6 copy-done.2
  74.5 0.0 all-to-all-done.1.near_ref
  74.5 0.6 copy-done.11
  75.1 1.8 %finish.1 = f32[4,32,256]{2,1,0:T(8,128)} custom-call(s32[32]{0:T(128)} %counts_ref.3, bf16[8,32,128]{2,1,0:T(8,128)(2,1)} %copy-done.11, f32[2,128,128]{2,1,0:T(8,128)} %copy-done.2), custom_call_target="tpu_custom_call" | custom-call | tf_op jit(solution)/shard_map/finish/pallas_call | solution.py:369
  (9 shorter events, 0.0 us)
Async XLA Ops:
  1.8 24.6 %all-to-all-start = ((bf16[8,4,32,256]{3,2,1,0:T(8,128)(2,1)}), bf16[8,4,32,256]{3,2,1,0:T(8,128)(2,1)S(1)}, u32[]{:S(2)}, u32[]{:S(2)}) async-start(bf16[8,4,32,256]{3,2,1,0:T(8,128)(2,1)} %get-tuple-element.10), calls=%async_computation | async-start | bytes 1048576 | tf_op jit(solution)/shard_map/all_to_all | solution.py:291
  10.3 1.6 %copy-start.4 = (bf16[128,2,64,64]{0,3,2,1:T(8,128)(2,1)S(1)}, bf16[128,2,64,64]{0,3,2,1:T(8,128)(2,1)}, u32[]{:S(2)}) copy-start(bf16[128,2,64,64]{0,3,2,1:T(8,128)(2,1)} %param.16) | copy-start | bytes 6291460
  11.9 1.2 %copy-start.6 = (bf16[32,2,128,64]{2,3,1,0:T(8,128)(2,1)S(1)}, bf16[32,2,128,64]{2,3,1,0:T(8,128)(2,1)}, u32[]{:S(2)}) copy-start(bf16[32,2,128,64]{2,3,1,0:T(8,128)(2,1)} %param.15) | copy-start | bytes 3145732
  13.2 0.8 %copy-start.9 = (bf16[4,32,256]{2,1,0:T(8,128)(2,1)S(1)}, bf16[4,32,256]{2,1,0:T(8,128)(2,1)}, u32[]{:S(2)}) copy-start(bf16[4,32,256]{2,1,0:T(8,128)(2,1)} %get-tuple-element.14.masked_ref) | copy-start | bytes 196612
  14.0 0.7 copy-start.10
  21.5 1.0 %copy-start.1 = (bf16[32,32,512]{2,1,0:T(8,128)(2,1)}, bf16[32,32,512]{2,1,0:T(8,128)(2,1)S(1)}, u32[]{:S(2)}) copy-start(bf16[32,32,512]{2,1,0:T(8,128)(2,1)S(1)} %lift.1) | copy-start | bytes 3145732
  22.5 16.7 %copy-start = (bf16[32,9,2,16,128]{4,3,2,1,0:T(8,128)(2,1)S(1)}, bf16[32,9,2,16,128]{4,3,2,1,0:T(8,128)(2,1)}, u32[]{:S(2)}) copy-start(bf16[32,9,2,16,128]{4,3,2,1,0:T(8,128)(2,1)} %blocks_ref.3) | copy-start | bytes 7077892
  22.5 16.7 %copy-start.3 = (s32[32,9]{0,1:T(8,128)S(1)}, s32[32,9]{0,1:T(8,128)}, u32[]{:S(2)}) copy-start(s32[32,9]{0,1:T(8,128)} %param.12) | copy-start | bytes 3460
  26.4 29.1 %all-to-all-start.2 = ((bf16[32,32,512]{2,1,0:T(8,128)(2,1)}), bf16[32,32,512]{2,1,0:T(8,128)(2,1)}, u32[]{:S(2)}, u32[]{:S(2)}) async-start(bf16[32,32,512]{2,1,0:T(8,128)(2,1)} %copy-done.1), calls=%async_computation.2 | async-start | bytes 2097152 | tf_op jit(solution)/shard_map/all_to_all | solution.py:309
  34.0 18.6 %collective-permute-start = (bf16[8,32,256]{2,1,0:T(8,128)(2,1)S(1)}, bf16[8,32,256]{2,1,0:T(8,128)(2,1)S(1)}, u32[]{:S(2)}, u32[]{:S(2)}) collective-permute-start(bf16[8,32,256]{2,1,0:T(8,128)(2,1)S(1)} %get-tuple-element.12), channel_id=1, source_target_pairs={{0,8},{8,16},{16,24},{24,32},{32,40},{40,48},{48,56},{56,64},{64,7... | collective-permute-start | bytes 393224 | tf_op jit(solution)/shard_map/ppermute | solution.py:325
  34.3 18.3 %collective-permute-start.1 = (bf16[8,32,256]{2,1,0:T(8,128)(2,1)S(1)}, bf16[8,32,256]{2,1,0:T(8,128)(2,1)S(1)}, u32[]{:S(2)}, u32[]{:S(2)}) collective-permute-start(bf16[8,32,256]{2,1,0:T(8,128)(2,1)S(1)} %get-tuple-element.13), channel_id=1, source_target_pairs={{8,0},{16,8},{24,16},{32,24},{40,32},{48,40},{56,48},{64,56},{72,6... | collective-permute-start | bytes 393224 | tf_op jit(solution)/shard_map/ppermute | solution.py:326
  41.3 18.9 %copy-start.8 = (s32[1024,32]{0,1:T(8,128)S(1)}, s32[1024,32]{0,1:T(8,128)}, u32[]{:S(2)}) copy-start(s32[1024,32]{0,1:T(8,128)} %param.14) | copy-start | bytes 393220
  55.5 19.0 %all-to-all-start.1 = ((bf16[8,32,128]{2,1,0:T(8,128)(2,1)}), bf16[8,32,128]{2,1,0:T(8,128)(2,1)S(1)}, u32[]{:S(2)}, u32[]{:S(2)}) async-start(bf16[8,32,128]{2,1,0:T(8,128)(2,1)} %outer.1), calls=%async_computation.1 | async-start | bytes 131072 | tf_op jit(solution)/shard_map/all_to_all | solution.py:352
  60.2 1.6 %copy-start.5 = (bf16[128,2,64,64]{0,3,2,1:T(8,128)(2,1)S(1)}, bf16[128,2,64,64]{0,3,2,1:T(8,128)(2,1)}, u32[]{:S(2)}) copy-start(bf16[128,2,64,64]{0,3,2,1:T(8,128)(2,1)} %param.17) | copy-start | bytes 6291460
  61.8 1.2 %copy-start.7 = (bf16[32,2,128,64]{2,3,1,0:T(8,128)(2,1)S(1)}, bf16[32,2,128,64]{2,3,1,0:T(8,128)(2,1)}, u32[]{:S(2)}) copy-start(bf16[32,2,128,64]{2,3,1,0:T(8,128)(2,1)} %param.18) | copy-start | bytes 3145732
  73.8 0.7 copy-start.2
  74.5 0.6 copy-start.11

commit v2 on v1

--- a/solution.py
+++ b/solution.py
@@ -11,6 +11,7 @@
 BF16 = jnp.bfloat16
 VMEM = pl.BlockSpec(memory_space=pltpu.VMEM)
 SMEM = pl.BlockSpec(memory_space=pltpu.SMEM)
+ANY = pl.BlockSpec(memory_space=pl.ANY)
 NT = (((1,), (1,)), ((), ()))
 
 
@@ -27,7 +28,7 @@
     return lane < limit
 
 
-def mask_kernel(counts_ref, currents_ref, masked_ref, copies_ref):
+def mask_kernel(counts_ref, currents_ref, masked_ref):
     angles, boxes, doubled = currents_ref.shape
     points = doubled // 2
     live = live_lanes(counts_ref, boxes, points)
@@ -36,8 +37,6 @@
             lanes = slice(c * points, (c + 1) * points)
             kept = jnp.where(live, currents_ref[a, :, lanes].astype(F32), 0.0).astype(BF16)
             masked_ref[a, :, lanes] = kept
-            for z in range(copies_ref.shape[0]):
-                copies_ref[z, a, :, lanes] = kept
 
 
 def beside(*parts):
@@ -60,7 +59,13 @@
     lax.fori_loop(0, rank, one, 0, unroll=4)
 
 
-def lift_kernel(maps_ref, masked_ref, bases_ref, kernels_ref, out_ref, rows, raws, turned, lifted, staged):
+def lift_kernel(
+    maps_ref, masked_ref, bases_hbm, kernels_hbm, out_ref, bases_ref, kernels_ref, rows, raws, turned, lifted, staged, arrived
+):
+    load_bases = pltpu.make_async_copy(bases_hbm, bases_ref, arrived.at[0])
+    load_kernels = pltpu.make_async_copy(kernels_hbm, kernels_ref, arrived.at[1])
+    load_bases.start()
+    load_kernels.start()
     angles, boxes, doubled = masked_ref.shape
     points = doubled // 2
     _, rank, _, kernel_count = kernels_ref.shape
@@ -72,6 +77,7 @@
             rows[pl.ds(c * angles + a, boxes, stride=each), :] = masked_ref[
                 a, :, c * points : (c + 1) * points
             ].astype(F32)
+    load_bases.wait()
     for box in range(boxes):
         x = rows[each * box : each * (box + 1), :].astype(BF16)
         raws[each * box : each * (box + 1), :] = lax.dot_general(
@@ -82,6 +88,7 @@
     lane = lax.broadcasted_iota(jnp.int32, crossed.shape, 1)
     straight = raw[:, 0].reshape(boxes * angles, wide)
     coef = (straight + jnp.where(lane < rank, -crossed, crossed)).astype(BF16)
+    load_kernels.wait()
     turn_kernels(kernels_ref, turned)
 
     def pair(step, _):
@@ -114,17 +121,24 @@
     lax.fori_loop(0, groups // 2, two_groups, 0)
 
 
-def pack_kernel(every_ref, out_ref, head_ref, tail_ref, spread):
-    parts, angles, boxes, doubled = every_ref.shape
+def pack_kernel(*refs):
+    every, (out_ref, head_ref, tail_ref, spread) = refs[:7], refs[-4:]
+    angles, boxes, doubled = every[0].shape
     points = doubled // 2
-    total = parts * angles
+    total = out_ref.shape[1]
+    parts = total // angles
     pitch = total + 1
-    for z in range(parts):
-        for a in range(angles):
-            for c in range(2):
-                spread[c, pl.ds(a * parts + z, boxes, stride=pitch), :] = every_ref[
-                    z, a, :, c * points : (c + 1) * points
-                ].astype(F32)
+    me = lax.axis_index("rhs")
+    back = 0
+    for ref in every:
+        for group in range(ref.shape[0] // angles):
+            z = lax.rem(me + parts - back, parts)
+            back += 1
+            for a in range(angles):
+                for c in range(2):
+                    spread[c, pl.ds(a * parts + z, boxes, stride=pitch), :] = ref[
+                        group * angles + a, :, c * points : (c + 1) * points
+                    ].astype(F32)
     for box in range(boxes):
         for c in range(2):
             lanes = slice(c * points, (c + 1) * points)
@@ -190,16 +204,37 @@
         out_ref[z, boxes - SPAN :] = rows[z * pitch + boxes - SPAN : z * pitch + boxes, :].astype(BF16)
 
 
+def turn_kernel(kernels_ref, out_ref, turned):
+    turn_kernels(kernels_ref, turned)
+    wide = out_ref.shape[1]
+
+    def one(k, _):
+        out_ref[k] = turned[pl.ds(k * PITCH, wide), :].astype(BF16)
+        return 0
+
+    lax.fori_loop(0, out_ref.shape[0], one, 0, unroll=8)
+
+
 CHUNK = 32
 
 
-def far_kernel(maps_ref, pieces_ref, kernels_ref, bases_ref, out_ref, table, turned, total_ref):
+def far_kernel(
+    maps_ref, pieces_ref, kernels_hbm, bases_hbm, out_ref, table, kernels_ref, bases_ref, total_ref, arrived
+):
     sources, lanes = pieces_ref.shape
-    _, rank, _, kernel_count = kernels_ref.shape
-    boxes, _, _, points = bases_ref.shape
-    wide = 2 * rank
+    kernel_count, wide, _ = kernels_hbm.shape
+    boxes, _, _, points = bases_hbm.shape
     angles = lanes // wide
-    turn_kernels(kernels_ref, turned)
+    chunks = kernel_count // CHUNK
+
+    def load_kernels(step):
+        part = pl.ds(step * CHUNK, CHUNK)
+        return pltpu.make_async_copy(kernels_hbm.at[part], kernels_ref.at[part], arrived.at[step])
+
+    load_bases = pltpu.make_async_copy(bases_hbm, bases_ref, arrived.at[chunks])
+    for step in range(chunks):
+        load_kernels(step).start()
+    load_bases.start()
     table[...] = maps_ref[...].astype(F32).astype(BF16)
     total_ref[...] = jnp.zeros_like(total_ref)
     one, zero = jnp.ones((), BF16), jnp.zeros((), BF16)
@@ -209,19 +244,21 @@
         maps = table[...]
         chosen = above(*[jnp.where(maps == (first + i).astype(BF16), one, zero) for i in range(CHUNK)])
         summed = jnp.dot(chosen, pieces_ref[...], preferred_element_type=F32)
+        load_kernels(step).wait()
         xs, weights = [], []
         for i in range(CHUNK):
             x = above(
                 *[summed[i * boxes : (i + 1) * boxes, a * wide : (a + 1) * wide] for a in range(angles)]
             )
-            w = turned[pl.ds((first + i) * PITCH, wide), :].astype(BF16)
+            w = kernels_ref[first + i]
             high = x.astype(BF16)
             xs += [high, (x - high.astype(F32)).astype(BF16)]
             weights += [w, w]
         total_ref[...] += jnp.dot(beside(*xs), above(*weights), preferred_element_type=F32)
         return 0
 
-    lax.fori_loop(0, kernel_count // CHUNK, chunk, 0)
+    lax.fori_loop(0, chunks, chunk, 0)
+    load_bases.wait()
     for t in range(boxes):
         x = total_ref[pl.ds(t, angles, stride=boxes), :]
         high = x.astype(BF16).astype(F32)
@@ -278,31 +315,40 @@
     kernels_one = level_one.transpose(1, 2, 3, 0)
     kernels_two = level_two.transpose(1, 2, 3, 0)
 
-    masked, copies = pl.pallas_call(
+    masked = pl.pallas_call(
         mask_kernel,
-        out_shape=(
-            jax.ShapeDtypeStruct((angles, boxes, doubled), BF16),
-            jax.ShapeDtypeStruct((parts, angles, boxes, doubled), BF16),
-        ),
+        out_shape=jax.ShapeDtypeStruct((angles, boxes, doubled), BF16),
         in_specs=[SMEM, VMEM],
-        out_specs=(VMEM, VMEM),
+        out_specs=VMEM,
+        compiler_params=params(60),
         name="mask",
     )(counts, currents)
-    every = lax.all_to_all(copies, "rhs", split_axis=0, concat_axis=0, tiled=True)
+
+    def passed(x, steps):
+        return lax.ppermute(x, "rhs", [(i, (i + steps) % parts) for i in range(parts)])
+
+    back1, ahead1 = passed(masked, 1), passed(masked, -1)
+    back2, ahead2 = passed(masked, 2), passed(masked, -2)
+    back34 = passed(jnp.concatenate([back1, back2], axis=0), 2)
+    ahead3 = passed(ahead1, -2)
+    every = (masked, back1, back2, back34, ahead3, ahead2, ahead1)
 
     pieces = pl.pallas_call(
         lift_kernel,
         out_shape=jax.ShapeDtypeStruct((leaves, boxes, angles * wide), BF16),
-        in_specs=[SMEM, VMEM, VMEM, VMEM],
+        in_specs=[SMEM, VMEM, ANY, ANY],
         out_specs=VMEM,
         scratch_shapes=[
+            pltpu.VMEM((boxes, 2, rank, points), BF16),
+            pltpu.VMEM((2, rank, rank, kernel_count), BF16),
             pltpu.VMEM((boxes * 2 * angles, points), F32),
             pltpu.VMEM((boxes * 2 * angles, wide), F32),
             pltpu.VMEM((kernel_count * PITCH, wide), F32),
             pltpu.VMEM((kernel_count, boxes * angles, wide), F32),
             pltpu.VMEM((2, angles * (boxes + 1) + angles, wide), F32),
+            pltpu.SemaphoreType.DMA((2,)),
         ],
-        compiler_params=params(32),
+        compiler_params=params(60),
         cost_estimate=pl.CostEstimate(flops=2**33, bytes_accessed=8 * 2**20, transcendentals=0),
         name="lift",
     )(source_maps, masked, lines(source_bases), kernels_one)
@@ -316,12 +362,12 @@
             jax.ShapeDtypeStruct((SPAN, total, doubled), BF16),
             jax.ShapeDtypeStruct((SPAN, total, doubled), BF16),
         ),
-        in_specs=[VMEM],
+        in_specs=[VMEM] * len(every),
         out_specs=(VMEM, VMEM, VMEM),
         scratch_shapes=[pltpu.VMEM((2, boxes * (total + 1) + total, points), F32)],
-        compiler_params=params(16),
+        compiler_params=params(6),
         name="pack",
-    )(every)
+    )(*every)
     before = lax.ppermute(tail, "leaf", [(i, (i + 1) % leaves) for i in range(leaves)])
     after = lax.ppermute(head, "leaf", [((i + 1) % leaves, i) for i in range(leaves)])
 
@@ -333,7 +379,7 @@
         in_specs=[SMEM, VMEM, VMEM],
         out_specs=VMEM,
         scratch_shapes=[pltpu.VMEM((parts * (inner + 1) + parts, angles * 2 * owned), F32)],
-        compiler_params=params(16),
+        compiler_params=params(4),
         cost_estimate=pl.CostEstimate(flops=2**31, bytes_accessed=2**21, transcendentals=0),
         name="inner",
     )(near_ids, own, near_blocks)
@@ -346,31 +392,46 @@
             pltpu.VMEM((6 * SPAN, total, doubled), BF16),
             pltpu.VMEM((parts * (boxes + 1) + parts, angles * 2 * owned), F32),
         ],
-        compiler_params=params(16),
+        compiler_params=params(6),
+        cost_estimate=pl.CostEstimate(flops=2**36, bytes_accessed=2**21, transcendentals=0),
         name="outer",
     )(near_ids, own, before, after, inner_rows, near_blocks)
     near = lax.all_to_all(rows, "rhs", split_axis=0, concat_axis=0, tiled=True)
 
+    turned = pl.pallas_call(
+        turn_kernel,
+        out_shape=jax.ShapeDtypeStruct((kernel_count, wide, wide), BF16),
+        in_specs=[VMEM],
+        out_specs=VMEM,
+        scratch_shapes=[pltpu.VMEM((kernel_count * PITCH, wide), F32)],
+        compiler_params=params(60),
+        cost_estimate=pl.CostEstimate(flops=2**31, bytes_accessed=6 * 2**20, transcendentals=0),
+        name="turn",
+    )(kernels_two)
+
     far = pl.pallas_call(
         far_kernel,
         out_shape=jax.ShapeDtypeStruct((2, angles * boxes, points), F32),
-        in_specs=[VMEM, VMEM, VMEM, VMEM],
+        in_specs=[VMEM, VMEM, ANY, ANY],
         out_specs=VMEM,
         scratch_shapes=[
             pltpu.VMEM((boxes, leaves * boxes), BF16),
-            pltpu.VMEM((kernel_count * PITCH, wide), F32),
+            pltpu.VMEM((kernel_count, wide, wide), BF16),
+            pltpu.VMEM((boxes, 2, rank, points), BF16),
             pltpu.VMEM((angles * boxes, wide), F32),
+            pltpu.SemaphoreType.DMA((kernel_count // CHUNK + 1,)),
         ],
-        compiler_params=params(40),
+        compiler_params=params(60),
         cost_estimate=pl.CostEstimate(flops=2**33, bytes_accessed=8 * 2**20, transcendentals=0),
         name="far",
-    )(target_maps.T, incoming.reshape(leaves * boxes, angles * wide), kernels_two, lines(target_bases))
+    )(target_maps.T, incoming.reshape(leaves * boxes, angles * wide), turned, lines(target_bases))
 
     return pl.pallas_call(
         finish_kernel,
         out_shape=jax.ShapeDtypeStruct((angles, boxes, doubled), F32),
         in_specs=[SMEM, VMEM, VMEM],
         out_specs=VMEM,
+        compiler_params=params(4),
         name="finish",
     )(counts, near, far)
 

time: 77.5 us -> 67.1 us (0.87)
  waiting for transfers between devices: 15.2 us -> 1.06 us
  local copies, waits for them, and re-layouts: 9.43 us -> 0.91 us
  Pallas kernels: 26.3 us -> 33.6 us
  starting transfers between devices: 25.9 us -> 31 us
    ppermute x0 -> x6, starting transfers between devices: none -> 11.7 us  [passed(): lax.ppermute(x, 'rhs', [(i, (i + steps) % parts) for i in range(parts)])]
    ppermute x1, waiting for transfers between devices: 11.3 us -> 0.64 us  [shards(): lax.ppermute(tail, 'leaf', [(i, (i + 1) % leaves) for i in range(leaves)])]
    all_to_all x1 -> x0, starting transfers between devices: 8.57 us -> none  [shards(): lax.all_to_all(copies, 'rhs', split_axis=0, concat_axis=0, tiled=True)]
    unnamed x24 -> x10, local copies, waits for them, and re-layouts: 9.43 us -> 0.91 us
    pallas_call x1 -> x2, Pallas kernels: 1.77 us -> 7.66 us  [the longest x1 6.16 us: shards(): pl.pallas_call(turn_kernel, out_shape=jax.ShapeDtypeStruct((kernel_count,...]
    all_to_all x1 -> x0, waiting for transfers between devices: 3.87 us -> none  [shards(): lax.all_to_all(copies, 'rhs', split_axis=0, concat_axis=0, tiled=True)]
    pallas_call x1, Pallas kernels: 6.8 us -> 9.18 us  [shards(): pl.pallas_call(lift_kernel, out_shape=jax.ShapeDtypeStruct((leaves, boxes...]
    all_to_all x1, starting transfers between devices: 4.72 us -> 6.66 us  [shards(): near = lax.all_to_all(rows, 'rhs', split_axis=0, concat_axis=0, tiled=True)]
  transfers between devices with their start and end apart: 5 -> 10, of which waited for: 2 -> 2; matrix products, arithmetic and copies ran while one was open for 0% -> 0% of each run, Pallas kernels for 30% -> 46%
where the time goes in v2:
time: 67.1 us; the launch traced here: 66.7 us
  Pallas kernels  33.6 us (50%)
  starting transfers between devices  31 us (46%)
  waiting for transfers between devices  1.06 us (2%)
  local copies, waits for them, and re-layouts  0.91 us (1%)
    ppermute x6, starting transfers between devices, passed(): lax.ppermute(x, 'rhs', [(i, (i + steps) % parts) for i in range(parts)])  11.7 us
    pallas_call x1, Pallas kernels, shards(): pl.pallas_call(far_kernel, out_shape=jax.ShapeDtypeStruct((2, angles * bo...  10.2 us
    pallas_call x1, Pallas kernels, shards(): pl.pallas_call(lift_kernel, out_shape=jax.ShapeDtypeStruct((leaves, boxes...  9.18 us
    all_to_all x1, starting transfers between devices, shards(): lax.all_to_all(pieces, 'leaf', split_axis=0, concat_axis=0, tiled=True)  7.46 us
    all_to_all x1, starting transfers between devices, shards(): near = lax.all_to_all(rows, 'rhs', split_axis=0, concat_axis=0, tiled=True)  6.66 us
    pallas_call x1, Pallas kernels, shards(): pl.pallas_call(turn_kernel, out_shape=jax.ShapeDtypeStruct((kernel_count,...  6.16 us
    ppermute x1, starting transfers between devices, shards(): lax.ppermute(head, 'leaf', [((i + 1) % leaves, i) for i in range(leaves)])  5.05 us
    pallas_call x1, Pallas kernels, shards(): pl.pallas_call(outer_kernel, out_shape=jax.ShapeDtypeStruct((parts, boxes...  2.85 us
  transfers between devices with their start and end apart: 10, of which 2 were waited for; matrix products, arithmetic and copies ran while one was open for 0% of the time, Pallas kernels for 46%

profile of v2, /device:TPU:32, one launch (start us, length us, event | category | flops | bytes accessed | tf_op | source)
XLA Modules:
  0.0 66.7 jit_solution(5270975467319559398)
XLA Ops:
  0.0 1.5 %mask.1.refs_0_.masked_ref = bf16[4,32,256]{2,1,0:T(8,128)(2,1)} custom-call(s32[32]{0:T(128)} %counts_ref.3, bf16[4,32,256]{2,1,0:T(8,128)(2,1)} %currents_ref.1), custom_call_target="tpu_custom_call" | custom-call | tf_op jit(solution)/shard_map/mask/pallas_call | solution.py:318
  1.5 5.4 %collective-permute-start.5 = (bf16[4,32,256]{2,1,0:T(8,128)(2,1)}, bf16[4,32,256]{2,1,0:T(8,128)(2,1)S(1)}, u32[]{:S(2)}, u32[]{:S(2)}) collective-permute-start(bf16[4,32,256]{2,1,0:T(8,128)(2,1)} %mask.1.refs_0_.masked_ref), channel_id=1, source_target_pairs={{0,6},{1,7},{2,0},{3,1},{4,2},{5,3},{6,4},{7,5},{8,14},{9,15},{10,... | collective-permute-start | bytes 196616 | tf_op jit(solution)/shard_map/ppermute | solution.py:328
  6.9 1.0 %collective-permute-start.3 = (bf16[4,32,256]{2,1,0:T(8,128)(2,1)}, bf16[4,32,256]{2,1,0:T(8,128)(2,1)S(1)}, u32[]{:S(2)}, u32[]{:S(2)}) collective-permute-start(bf16[4,32,256]{2,1,0:T(8,128)(2,1)} %mask.1.refs_0_.masked_ref), channel_id=1, source_target_pairs={{0,7},{1,0},{2,1},{3,2},{4,3},{5,4},{6,5},{7,6},{8,15},{9,8},{10,9... | collective-permute-start | bytes 196616 | tf_op jit(solution)/shard_map/ppermute | solution.py:328
  7.9 0.0 collective-permute-start.1
  7.9 1.0 %collective-permute-start = (bf16[4,32,256]{2,1,0:T(8,128)(2,1)}, bf16[4,32,256]{2,1,0:T(8,128)(2,1)S(1)}, u32[]{:S(2)}, u32[]{:S(2)}) collective-permute-start(bf16[4,32,256]{2,1,0:T(8,128)(2,1)} %mask.1.refs_0_.masked_ref), channel_id=1, source_target_pairs={{0,1},{1,2},{2,3},{3,4},{4,5},{5,6},{6,7},{7,0},{8,9},{9,10},{10,1... | collective-permute-start | bytes 196616 | tf_op jit(solution)/shard_map/ppermute | solution.py:328
  8.9 9.2 %lift.1 = bf16[32,32,512]{2,1,0:T(8,128)(2,1)} custom-call(s32[32,32]{1,0:T(8,128)} %maps_ref.1, bf16[4,32,256]{2,1,0:T(8,128)(2,1)} %mask.1.refs_0_.masked_ref, bf16[32,2,64,128]{3,2,1,0:T(8,128)(2,1)} %bitcast.11, bf16[2,64,64,128]{3,2,1,0:T(8,128)(2,1)} %bitcast.9), custom_call_target="tpu_custom_call" | custom-call | flops 8589934592 | bytes 8388608 | tf_op jit(solution)/shard_map/lift/pallas_call | solution.py:336
  18.1 7.5 %all-to-all-start.1 = ((bf16[32,32,512]{2,1,0:T(8,128)(2,1)}), bf16[32,32,512]{2,1,0:T(8,128)(2,1)}, u32[]{:S(2)}, u32[]{:S(2)}) async-start(bf16[32,32,512]{2,1,0:T(8,128)(2,1)} %lift.1), calls=%async_computation.1 | async-start | bytes 2097152 | tf_op jit(solution)/shard_map/all_to_all | solution.py:355
  25.6 0.0 collective-permute-done.1.refs_2_
  25.6 0.0 collective-permute-done.refs_1_
  25.6 2.1 %collective-permute-start.2 = (bf16[8,32,256]{2,1,0:T(8,128)(2,1)S(1)}, bf16[8,32,256]{2,1,0:T(8,128)(2,1)S(1)}, u32[]{:S(2)}, u32[]{:S(2)}) collective-permute-start(bf16[8,32,256]{2,1,0:T(8,128)(2,1)S(1)} %pad_maximum_fusion), channel_id=1, source_target_pairs={{0,2},{1,3},{2,4},{3,5},{4,6},{5,7},{6,0},{7,1},{8,10},{9,11},{10,... | collective-permute-start | bytes 393224 | tf_op jit(solution)/shard_map/ppermute | solution.py:328
  27.7 0.0 collective-permute-done.3.refs_6_
  27.7 2.2 %collective-permute-start.4 = (bf16[4,32,256]{2,1,0:T(8,128)(2,1)S(1)}, bf16[4,32,256]{2,1,0:T(8,128)(2,1)S(1)}, u32[]{:S(2)}, u32[]{:S(2)}) collective-permute-start(bf16[4,32,256]{2,1,0:T(8,128)(2,1)S(1)} %collective-permute-done.3.refs_6_), channel_id=1, source_target_pairs={{0,6},{1,7},{2,0},{3,1},{4,2},{5,3},{6,4},{7,5},{8,14},{9,15},{10,... | collective-permute-start | bytes 196616 | tf_op jit(solution)/shard_map/ppermute | solution.py:328
  30.0 6.2 %turn.1.kernels_hbm = bf16[128,128,128]{2,1,0:T(8,128)(2,1)} custom-call(bf16[2,64,64,128]{3,2,1,0:T(8,128)(2,1)} %bitcast.10), custom_call_target="tpu_custom_call" | custom-call | flops 2147483648 | bytes 6291456 | tf_op jit(solution)/shard_map/turn/pallas_call | solution.py:401
  36.1 0.0 collective-permute-done.5.refs_5_
  36.1 0.0 collective-permute-done.4.refs_4_
  36.1 0.4 collective-permute-done.2.refs_3_
  36.5 0.0 copy-done
  36.5 0.2 pack.1
  36.7 0.1 collective-permute-start.6
  36.8 5.1 %collective-permute-start.7 = (bf16[8,32,256]{2,1,0:T(8,128)(2,1)S(1)}, bf16[8,32,256]{2,1,0:T(8,128)(2,1)S(1)}, u32[]{:S(2)}, u32[]{:S(2)}) collective-permute-start(bf16[8,32,256]{2,1,0:T(8,128)(2,1)S(1)} %get-tuple-element.10), channel_id=1, source_target_pairs={{8,0},{16,8},{24,16},{32,24},{40,32},{48,40},{56,48},{64,56},{72,6... | collective-permute-start | bytes 393224 | tf_op jit(solution)/shard_map/ppermute | solution.py:372
  41.8 0.0 copy-done.3
  41.9 2.1 %inner.1.inner_ref = bf16[8,16,128]{2,1,0:T(8,128)(2,1)S(1)} custom-call(s32[9,32]{1,0:T(8,128)S(1)} %bitcast.7, bf16[32,32,256]{2,1,0:T(8,128)(2,1)S(1)} %get-tuple-element.8.own_ref, bf16[32,9,2,16,128]{4,3,2,1,0:T(8,128)(2,1)S(1)} %copy-done.3), custom_call_target="tpu_custom_call" | custom-call | flops 2147483648 | bytes 2097152 | tf_op jit(solution)/shard_map/inner/pallas_call | solution.py:376
  44.0 0.6 collective-permute-done.6.before_ref
  44.6 0.0 collective-permute-done.7.after_ref
  44.6 2.8 %outer.1 = bf16[8,32,128]{2,1,0:T(8,128)(2,1)} custom-call(s32[9,32]{1,0:T(8,128)S(1)} %bitcast.8, bf16[32,32,256]{2,1,0:T(8,128)(2,1)S(1)} %get-tuple-element.8.own_ref, bf16[8,32,256]{2,1,0:T(8,128)(2,1)S(1)} %collective-permute-done.6.before_ref, bf16[8,32,256]{2,1,0:T(8,128)(2,1)S(1)} %collective-permute-done.7.after_ref, ...), custom_call_target="tpu_custom_call" | custom-call | flops 68719476736 | bytes 2097152 | tf_op jit(solution)/shard_map/outer/pallas_call | solution.py:386
  47.5 0.0 all-to-all-done.1
  47.5 6.7 %all-to-all-start = ((bf16[8,32,128]{2,1,0:T(8,128)(2,1)}), bf16[8,32,128]{2,1,0:T(8,128)(2,1)S(1)}, u32[]{:S(2)}, u32[]{:S(2)}) async-start(bf16[8,32,128]{2,1,0:T(8,128)(2,1)} %outer.1), calls=%async_computation | async-start | bytes 131072 | tf_op jit(solution)/shard_map/all_to_all | solution.py:399
  54.1 10.2 %far.1.far_ref = f32[2,128,128]{2,1,0:T(8,128)} custom-call(s32[32,1024]{1,0:T(8,128)} %bitcast.13, bf16[1024,512]{1,0:T(8,128)(2,1)} %bitcast.4.pieces_ref, bf16[128,128,128]{2,1,0:T(8,128)(2,1)} %turn.1.kernels_hbm, bf16[32,2,64,128]{3,2,1,0:T(8,128)(2,1)} %bitcast.12), custom_call_target="tpu_custom_call" | custom-call | flops 8589934592 | bytes 8388608 | tf_op jit(solution)/shard_map/far/pallas_call | solution.py:412
  64.4 0.0 all-to-all-done.near_ref
  64.4 0.0 copy-start.1
  64.4 0.9 %copy-done.1 = f32[2,128,128]{2,1,0:T(8,128)S(1)} copy-done((f32[2,128,128]{2,1,0:T(8,128)S(1)}, f32[2,128,128]{2,1,0:T(8,128)}, u32[]{:S(2)}) %copy-start.1) | copy-done | bytes 131096
  65.3 1.4 %finish.1 = f32[4,32,256]{2,1,0:T(8,128)} custom-call(s32[32]{0:T(128)S(1)} %copy-done.2, bf16[8,32,128]{2,1,0:T(8,128)(2,1)S(1)} %all-to-all-done.near_ref, f32[2,128,128]{2,1,0:T(8,128)S(1)} %copy-done.1), custom_call_target="tpu_custom_call" | custom-call | tf_op jit(solution)/shard_map/finish/pallas_call | solution.py:429
  (7 shorter events, 0.0 us)
Async XLA Ops:
  1.5 34.6 %collective-permute-start.5 = (bf16[4,32,256]{2,1,0:T(8,128)(2,1)}, bf16[4,32,256]{2,1,0:T(8,128)(2,1)S(1)}, u32[]{:S(2)}, u32[]{:S(2)}) collective-permute-start(bf16[4,32,256]{2,1,0:T(8,128)(2,1)} %mask.1.refs_0_.masked_ref), channel_id=1, source_target_pairs={{0,6},{1,7},{2,0},{3,1},{4,2},{5,3},{6,4},{7,5},{8,14},{9,15},{10,... | collective-permute-start | bytes 196616 | tf_op jit(solution)/shard_map/ppermute | solution.py:328
  6.9 20.8 %collective-permute-start.3 = (bf16[4,32,256]{2,1,0:T(8,128)(2,1)}, bf16[4,32,256]{2,1,0:T(8,128)(2,1)S(1)}, u32[]{:S(2)}, u32[]{:S(2)}) collective-permute-start(bf16[4,32,256]{2,1,0:T(8,128)(2,1)} %mask.1.refs_0_.masked_ref), channel_id=1, source_target_pairs={{0,7},{1,0},{2,1},{3,2},{4,3},{5,4},{6,5},{7,6},{8,15},{9,8},{10,9... | collective-permute-start | bytes 196616 | tf_op jit(solution)/shard_map/ppermute | solution.py:328
  7.9 17.7 %collective-permute-start.1 = (bf16[4,32,256]{2,1,0:T(8,128)(2,1)}, bf16[4,32,256]{2,1,0:T(8,128)(2,1)S(1)}, u32[]{:S(2)}, u32[]{:S(2)}) collective-permute-start(bf16[4,32,256]{2,1,0:T(8,128)(2,1)} %mask.1.refs_0_.masked_ref), channel_id=1, source_target_pairs={{0,2},{1,3},{2,4},{3,5},{4,6},{5,7},{6,0},{7,1},{8,10},{9,11},{10,... | collective-permute-start | bytes 196616 | tf_op jit(solution)/shard_map/ppermute | solution.py:328
  7.9 17.7 %collective-permute-start = (bf16[4,32,256]{2,1,0:T(8,128)(2,1)}, bf16[4,32,256]{2,1,0:T(8,128)(2,1)S(1)}, u32[]{:S(2)}, u32[]{:S(2)}) collective-permute-start(bf16[4,32,256]{2,1,0:T(8,128)(2,1)} %mask.1.refs_0_.masked_ref), channel_id=1, source_target_pairs={{0,1},{1,2},{2,3},{3,4},{4,5},{5,6},{6,7},{7,0},{8,9},{9,10},{10,1... | collective-permute-start | bytes 196616 | tf_op jit(solution)/shard_map/ppermute | solution.py:328
  18.1 29.4 %all-to-all-start.1 = ((bf16[32,32,512]{2,1,0:T(8,128)(2,1)}), bf16[32,32,512]{2,1,0:T(8,128)(2,1)}, u32[]{:S(2)}, u32[]{:S(2)}) async-start(bf16[32,32,512]{2,1,0:T(8,128)(2,1)} %lift.1), calls=%async_computation.1 | async-start | bytes 2097152 | tf_op jit(solution)/shard_map/all_to_all | solution.py:355
  25.6 10.9 %collective-permute-start.2 = (bf16[8,32,256]{2,1,0:T(8,128)(2,1)S(1)}, bf16[8,32,256]{2,1,0:T(8,128)(2,1)S(1)}, u32[]{:S(2)}, u32[]{:S(2)}) collective-permute-start(bf16[8,32,256]{2,1,0:T(8,128)(2,1)S(1)} %pad_maximum_fusion), channel_id=1, source_target_pairs={{0,2},{1,3},{2,4},{3,5},{4,6},{5,7},{6,0},{7,1},{8,10},{9,11},{10,... | collective-permute-start | bytes 393224 | tf_op jit(solution)/shard_map/ppermute | solution.py:328
  27.7 8.4 %collective-permute-start.4 = (bf16[4,32,256]{2,1,0:T(8,128)(2,1)S(1)}, bf16[4,32,256]{2,1,0:T(8,128)(2,1)S(1)}, u32[]{:S(2)}, u32[]{:S(2)}) collective-permute-start(bf16[4,32,256]{2,1,0:T(8,128)(2,1)S(1)} %collective-permute-done.3.refs_6_), channel_id=1, source_target_pairs={{0,6},{1,7},{2,0},{3,1},{4,2},{5,3},{6,4},{7,5},{8,14},{9,15},{10,... | collective-permute-start | bytes 196616 | tf_op jit(solution)/shard_map/ppermute | solution.py:328
  29.9 6.6 %copy-start = (bf16[4,32,256]{2,1,0:T(8,128)(2,1)S(1)}, bf16[4,32,256]{2,1,0:T(8,128)(2,1)}, u32[]{:S(2)}) copy-start(bf16[4,32,256]{2,1,0:T(8,128)(2,1)} %mask.1.refs_0_.masked_ref) | copy-start | bytes 196612
  29.9 11.9 %copy-start.3 = (bf16[32,9,2,16,128]{4,3,2,1,0:T(8,128)(2,1)S(1)}, bf16[32,9,2,16,128]{4,3,2,1,0:T(8,128)(2,1)}, u32[]{:S(2)}) copy-start(bf16[32,9,2,16,128]{4,3,2,1,0:T(8,128)(2,1)} %blocks_ref.3) | copy-start | bytes 7077892
  30.0 11.9 %copy-start.4 = (s32[32,9]{0,1:T(8,128)S(1)}, s32[32,9]{0,1:T(8,128)}, u32[]{:S(2)}) copy-start(s32[32,9]{0,1:T(8,128)} %param.12) | copy-start | bytes 3460
  36.7 7.9 %collective-permute-start.6 = (bf16[8,32,256]{2,1,0:T(8,128)(2,1)S(1)}, bf16[8,32,256]{2,1,0:T(8,128)(2,1)S(1)}, u32[]{:S(2)}, u32[]{:S(2)}) collective-permute-start(bf16[8,32,256]{2,1,0:T(8,128)(2,1)S(1)} %get-tuple-element.9), channel_id=1, source_target_pairs={{0,8},{8,16},{16,24},{24,32},{32,40},{40,48},{48,56},{56,64},{64,7... | collective-permute-start | bytes 393224 | tf_op jit(solution)/shard_map/ppermute | solution.py:371
  36.8 7.8 %collective-permute-start.7 = (bf16[8,32,256]{2,1,0:T(8,128)(2,1)S(1)}, bf16[8,32,256]{2,1,0:T(8,128)(2,1)S(1)}, u32[]{:S(2)}, u32[]{:S(2)}) collective-permute-start(bf16[8,32,256]{2,1,0:T(8,128)(2,1)S(1)} %get-tuple-element.10), channel_id=1, source_target_pairs={{8,0},{16,8},{24,16},{32,24},{40,32},{48,40},{56,48},{64,56},{72,6... | collective-permute-start | bytes 393224 | tf_op jit(solution)/shard_map/ppermute | solution.py:372
  47.5 16.9 %all-to-all-start = ((bf16[8,32,128]{2,1,0:T(8,128)(2,1)}), bf16[8,32,128]{2,1,0:T(8,128)(2,1)S(1)}, u32[]{:S(2)}, u32[]{:S(2)}) async-start(bf16[8,32,128]{2,1,0:T(8,128)(2,1)} %outer.1), calls=%async_computation | async-start | bytes 131072 | tf_op jit(solution)/shard_map/all_to_all | solution.py:399
  54.1 10.3 %copy-start.2 = (s32[32]{0:T(128)S(1)}, s32[32]{0:T(128)}, u32[]{:S(2)}) copy-start(s32[32]{0:T(128)} %counts_ref.3) | copy-start | bytes 388
  64.4 0.9 %copy-start.1 = (f32[2,128,128]{2,1,0:T(8,128)S(1)}, f32[2,128,128]{2,1,0:T(8,128)}, u32[]{:S(2)}) copy-start(f32[2,128,128]{2,1,0:T(8,128)} %far.1.far_ref) | copy-start | bytes 393220

commit v3 on v2

--- a/solution.py
+++ b/solution.py
@@ -56,16 +56,34 @@
         turned[pl.ds(rank + r, kernel_count, stride=PITCH), :] = above(-imag, real).T.astype(F32)
         return 0
 
-    lax.fori_loop(0, rank, one, 0, unroll=4)
+    lax.fori_loop(0, rank, one, 0, unroll=16)
 
 
 def lift_kernel(
-    maps_ref, masked_ref, bases_hbm, kernels_hbm, out_ref, bases_ref, kernels_ref, rows, raws, turned, lifted, staged, arrived
+    maps_ref,
+    masked_hbm,
+    bases_hbm,
+    kernels_hbm,
+    out_hbm,
+    masked_ref,
+    bases_ref,
+    kernels_ref,
+    out_ref,
+    rows,
+    raws,
+    turned,
+    lifted,
+    staged,
+    arrived,
+    sent,
 ):
+    load_masked = pltpu.make_async_copy(masked_hbm, masked_ref, arrived.at[2])
+    load_masked.start()
     load_bases = pltpu.make_async_copy(bases_hbm, bases_ref, arrived.at[0])
     load_kernels = pltpu.make_async_copy(kernels_hbm, kernels_ref, arrived.at[1])
     load_bases.start()
     load_kernels.start()
+    load_masked.wait()
     angles, boxes, doubled = masked_ref.shape
     points = doubled // 2
     _, rank, _, kernel_count = kernels_ref.shape
@@ -99,7 +117,7 @@
         lifted[k + 1] = both[:, wide:]
         return 0
 
-    lax.fori_loop(0, kernel_count // 2, pair, 0, unroll=16)
+    lax.fori_loop(0, kernel_count // 2, pair, 0, unroll=True)
     pitch = boxes + 1
 
     def one_group(g, slot):
@@ -113,12 +131,19 @@
                 slot, a * pitch : a * pitch + boxes, :
             ].astype(BF16)
 
-    def two_groups(step, _):
-        one_group(2 * step, 0)
-        one_group(2 * step + 1, 1)
-        return 0
-
-    lax.fori_loop(0, groups // 2, two_groups, 0)
+    def send(step):
+        part = pl.ds(step * 4, 4)
+        return pltpu.make_async_copy(out_ref.at[part], out_hbm.at[part], sent.at[step])
+
+    def four_groups(step, _):
+        for i in range(4):
+            one_group(4 * step + i, i)
+        send(step).start()
+        return 0
+
+    lax.fori_loop(0, groups // 4, four_groups, 0)
+    for step in range(groups // 4):
+        send(step).wait()
 
 
 def pack_kernel(*refs):
@@ -174,7 +199,7 @@
         rows[pl.ds(step, parts, stride=pitch), :] = near_rows(own_ref, ids, blocks_ref, t, total, angles)
         return 0
 
-    lax.fori_loop(0, inner, target, 0, unroll=4)
+    lax.fori_loop(0, inner, target, 0, unroll=True)
     for z in range(parts):
         out_ref[z] = rows[z * pitch : z * pitch + inner, :].astype(BF16)
 
@@ -197,7 +222,7 @@
         rows[pl.ds(t, parts, stride=pitch), :] = near_rows(window, ids, blocks_ref, t, total, angles)
         return 0
 
-    lax.fori_loop(0, 2 * SPAN, target, 0, unroll=4)
+    lax.fori_loop(0, 2 * SPAN, target, 0, unroll=True)
     for z in range(parts):
         out_ref[z, :SPAN] = rows[z * pitch : z * pitch + SPAN, :].astype(BF16)
         out_ref[z, SPAN : boxes - SPAN] = inner_ref[z]
@@ -212,16 +237,27 @@
         out_ref[k] = turned[pl.ds(k * PITCH, wide), :].astype(BF16)
         return 0
 
-    lax.fori_loop(0, out_ref.shape[0], one, 0, unroll=8)
+    lax.fori_loop(0, out_ref.shape[0], one, 0, unroll=32)
 
 
 CHUNK = 32
 
 
 def far_kernel(
-    maps_ref, pieces_ref, kernels_hbm, bases_hbm, out_ref, table, kernels_ref, bases_ref, total_ref, arrived
+    maps_hbm,
+    pieces_hbm,
+    kernels_hbm,
+    bases_hbm,
+    out_ref,
+    maps_ref,
+    pieces_ref,
+    kernels_ref,
+    bases_ref,
+    table,
+    total_ref,
+    arrived,
 ):
-    sources, lanes = pieces_ref.shape
+    sources, lanes = pieces_hbm.shape
     kernel_count, wide, _ = kernels_hbm.shape
     boxes, _, _, points = bases_hbm.shape
     angles = lanes // wide
@@ -232,32 +268,34 @@
         return pltpu.make_async_copy(kernels_hbm.at[part], kernels_ref.at[part], arrived.at[step])
 
     load_bases = pltpu.make_async_copy(bases_hbm, bases_ref, arrived.at[chunks])
+    load_maps = pltpu.make_async_copy(maps_hbm, maps_ref, arrived.at[chunks + 1])
+    load_pieces = pltpu.make_async_copy(pieces_hbm, pieces_ref, arrived.at[chunks + 2])
+    load_maps.start()
+    load_pieces.start()
     for step in range(chunks):
         load_kernels(step).start()
     load_bases.start()
+    load_maps.wait()
     table[...] = maps_ref[...].astype(F32).astype(BF16)
-    total_ref[...] = jnp.zeros_like(total_ref)
     one, zero = jnp.ones((), BF16), jnp.zeros((), BF16)
-
-    def chunk(step, _):
+    load_pieces.wait()
+    total = None
+    for step in range(chunks):
         first = step * CHUNK
         maps = table[...]
-        chosen = above(*[jnp.where(maps == (first + i).astype(BF16), one, zero) for i in range(CHUNK)])
+        chosen = above(*[jnp.where(maps == jnp.asarray(first + i, BF16), one, zero) for i in range(CHUNK)])
         summed = jnp.dot(chosen, pieces_ref[...], preferred_element_type=F32)
         load_kernels(step).wait()
-        xs, weights = [], []
-        for i in range(CHUNK):
-            x = above(
+        xs = [
+            above(
                 *[summed[i * boxes : (i + 1) * boxes, a * wide : (a + 1) * wide] for a in range(angles)]
-            )
-            w = kernels_ref[first + i]
-            high = x.astype(BF16)
-            xs += [high, (x - high.astype(F32)).astype(BF16)]
-            weights += [w, w]
-        total_ref[...] += jnp.dot(beside(*xs), above(*weights), preferred_element_type=F32)
-        return 0
-
-    lax.fori_loop(0, chunks, chunk, 0)
+            ).astype(BF16)
+            for i in range(CHUNK)
+        ]
+        weights = kernels_ref[first : first + CHUNK].reshape(CHUNK * wide, wide)
+        add = jnp.dot(beside(*xs), weights, preferred_element_type=F32)
+        total = add if total is None else total + add
+    total_ref[...] = total
     load_bases.wait()
     for t in range(boxes):
         x = total_ref[pl.ds(t, angles, stride=boxes), :]
@@ -336,17 +374,20 @@
     pieces = pl.pallas_call(
         lift_kernel,
         out_shape=jax.ShapeDtypeStruct((leaves, boxes, angles * wide), BF16),
-        in_specs=[SMEM, VMEM, ANY, ANY],
-        out_specs=VMEM,
+        in_specs=[SMEM, ANY, ANY, ANY],
+        out_specs=ANY,
         scratch_shapes=[
+            pltpu.VMEM((angles, boxes, doubled), BF16),
             pltpu.VMEM((boxes, 2, rank, points), BF16),
             pltpu.VMEM((2, rank, rank, kernel_count), BF16),
+            pltpu.VMEM((leaves, boxes, angles * wide), BF16),
             pltpu.VMEM((boxes * 2 * angles, points), F32),
             pltpu.VMEM((boxes * 2 * angles, wide), F32),
             pltpu.VMEM((kernel_count * PITCH, wide), F32),
             pltpu.VMEM((kernel_count, boxes * angles, wide), F32),
-            pltpu.VMEM((2, angles * (boxes + 1) + angles, wide), F32),
-            pltpu.SemaphoreType.DMA((2,)),
+            pltpu.VMEM((4, angles * (boxes + 1) + angles, wide), F32),
+            pltpu.SemaphoreType.DMA((3,)),
+            pltpu.SemaphoreType.DMA((leaves // 4,)),
         ],
         compiler_params=params(60),
         cost_estimate=pl.CostEstimate(flops=2**33, bytes_accessed=8 * 2**20, transcendentals=0),
@@ -404,7 +445,7 @@
         in_specs=[VMEM],
         out_specs=VMEM,
         scratch_shapes=[pltpu.VMEM((kernel_count * PITCH, wide), F32)],
-        compiler_params=params(60),
+        compiler_params=params(12),
         cost_estimate=pl.CostEstimate(flops=2**31, bytes_accessed=6 * 2**20, transcendentals=0),
         name="turn",
     )(kernels_two)
@@ -412,14 +453,16 @@
     far = pl.pallas_call(
         far_kernel,
         out_shape=jax.ShapeDtypeStruct((2, angles * boxes, points), F32),
-        in_specs=[VMEM, VMEM, ANY, ANY],
+        in_specs=[ANY, ANY, ANY, ANY],
         out_specs=VMEM,
         scratch_shapes=[
-            pltpu.VMEM((boxes, leaves * boxes), BF16),
+            pltpu.VMEM((boxes, leaves * boxes), jnp.int32),
+            pltpu.VMEM((leaves * boxes, angles * wide), BF16),
             pltpu.VMEM((kernel_count, wide, wide), BF16),
             pltpu.VMEM((boxes, 2, rank, points), BF16),
+            pltpu.VMEM((boxes, leaves * boxes), BF16),
             pltpu.VMEM((angles * boxes, wide), F32),
-            pltpu.SemaphoreType.DMA((kernel_count // CHUNK + 1,)),
+            pltpu.SemaphoreType.DMA((kernel_count // CHUNK + 3,)),
         ],
         compiler_params=params(60),
         cost_estimate=pl.CostEstimate(flops=2**33, bytes_accessed=8 * 2**20, transcendentals=0),

time: 67.1 us -> 63.7 us (0.949)
  Pallas kernels: 33.6 us -> 25 us
  waiting for transfers between devices: 1.06 us -> 6.23 us
    ppermute x6, waiting for transfers between devices: 0.41 us -> 4.89 us  [passed(): lax.ppermute(x, 'rhs', [(i, (i + steps) % parts) for i in range(parts)])]
    pallas_call x1, Pallas kernels: 6.16 us -> 1.72 us  [shards(): pl.pallas_call(turn_kernel, out_shape=jax.ShapeDtypeStruct((kernel_count,...]
    pallas_call x1, Pallas kernels: 10.2 us -> 8.78 us  [shards(): pl.pallas_call(far_kernel, out_shape=jax.ShapeDtypeStruct((2, angles * bo...]
    pallas_call x1, Pallas kernels: 9.18 us -> 7.76 us  [shards(): pl.pallas_call(lift_kernel, out_shape=jax.ShapeDtypeStruct((leaves, boxes...]
    ppermute x1, waiting for transfers between devices: 0.64 us -> 1.33 us  [shards(): lax.ppermute(tail, 'leaf', [(i, (i + 1) % leaves) for i in range(leaves)])]
  transfers between devices with their start and end apart: 10 -> 10, of which waited for: 2 -> 3; matrix products, arithmetic and copies ran while one was open for 0% -> 0% of each run, Pallas kernels for 46% -> 35%
where the time goes in v3:
time: 63.7 us; the launch traced here: 63.3 us
  starting transfers between devices  31 us (49%)
  Pallas kernels  25 us (39%)
  waiting for transfers between devices  6.23 us (10%)
  local copies, waits for them, and re-layouts  0.93 us (1%)
    ppermute x6, starting transfers between devices, passed(): lax.ppermute(x, 'rhs', [(i, (i + steps) % parts) for i in range(parts)])  11.7 us
    pallas_call x1, Pallas kernels, shards(): pl.pallas_call(far_kernel, out_shape=jax.ShapeDtypeStruct((2, angles * bo...  8.78 us
    pallas_call x1, Pallas kernels, shards(): pl.pallas_call(lift_kernel, out_shape=jax.ShapeDtypeStruct((leaves, boxes...  7.76 us
    all_to_all x1, starting transfers between devices, shards(): lax.all_to_all(pieces, 'leaf', split_axis=0, concat_axis=0, tiled=True)  7.46 us
    all_to_all x1, starting transfers between devices, shards(): near = lax.all_to_all(rows, 'rhs', split_axis=0, concat_axis=0, tiled=True)  6.62 us
    ppermute x1, starting transfers between devices, shards(): lax.ppermute(head, 'leaf', [((i + 1) % leaves, i) for i in range(leaves)])  5.05 us
    ppermute x6, waiting for transfers between devices, passed(): lax.ppermute(x, 'rhs', [(i, (i + steps) % parts) for i in range(parts)])  4.89 us
    pallas_call x1, Pallas kernels, shards(): pl.pallas_call(outer_kernel, out_shape=jax.ShapeDtypeStruct((parts, boxes...  2.2 us
  transfers between devices with their start and end apart: 10, of which 3 were waited for; matrix products, arithmetic and copies ran while one was open for 0% of the time, Pallas kernels for 35%

profile of v3, /device:TPU:32, one launch (start us, length us, event | category | flops | bytes accessed | tf_op | source)
XLA Modules:
  0.0 63.3 jit_solution(8954177673236459649)
XLA Ops:
  0.0 1.5 %mask.1.refs_0_.masked_hbm = bf16[4,32,256]{2,1,0:T(8,128)(2,1)} custom-call(s32[32]{0:T(128)} %counts_ref.3, bf16[4,32,256]{2,1,0:T(8,128)(2,1)} %currents_ref.1), custom_call_target="tpu_custom_call" | custom-call | tf_op jit(solution)/shard_map/mask/pallas_call | solution.py:356
  1.5 5.4 %collective-permute-start.5 = (bf16[4,32,256]{2,1,0:T(8,128)(2,1)}, bf16[4,32,256]{2,1,0:T(8,128)(2,1)S(1)}, u32[]{:S(2)}, u32[]{:S(2)}) collective-permute-start(bf16[4,32,256]{2,1,0:T(8,128)(2,1)} %mask.1.refs_0_.masked_hbm), channel_id=1, source_target_pairs={{0,6},{1,7},{2,0},{3,1},{4,2},{5,3},{6,4},{7,5},{8,14},{9,15},{10,... | collective-permute-start | bytes 196616 | tf_op jit(solution)/shard_map/ppermute | solution.py:366
  6.9 1.0 %collective-permute-start.3 = (bf16[4,32,256]{2,1,0:T(8,128)(2,1)}, bf16[4,32,256]{2,1,0:T(8,128)(2,1)S(1)}, u32[]{:S(2)}, u32[]{:S(2)}) collective-permute-start(bf16[4,32,256]{2,1,0:T(8,128)(2,1)} %mask.1.refs_0_.masked_hbm), channel_id=1, source_target_pairs={{0,7},{1,0},{2,1},{3,2},{4,3},{5,4},{6,5},{7,6},{8,15},{9,8},{10,9... | collective-permute-start | bytes 196616 | tf_op jit(solution)/shard_map/ppermute | solution.py:366
  7.9 0.0 collective-permute-start.1
  7.9 1.0 %collective-permute-start = (bf16[4,32,256]{2,1,0:T(8,128)(2,1)}, bf16[4,32,256]{2,1,0:T(8,128)(2,1)S(1)}, u32[]{:S(2)}, u32[]{:S(2)}) collective-permute-start(bf16[4,32,256]{2,1,0:T(8,128)(2,1)} %mask.1.refs_0_.masked_hbm), channel_id=1, source_target_pairs={{0,1},{1,2},{2,3},{3,4},{4,5},{5,6},{6,7},{7,0},{8,9},{9,10},{10,1... | collective-permute-start | bytes 196616 | tf_op jit(solution)/shard_map/ppermute | solution.py:366
  8.9 7.8 %lift.1 = bf16[32,32,512]{2,1,0:T(8,128)(2,1)} custom-call(s32[32,32]{1,0:T(8,128)} %maps_ref.1, bf16[4,32,256]{2,1,0:T(8,128)(2,1)} %mask.1.refs_0_.masked_hbm, bf16[32,2,64,128]{3,2,1,0:T(8,128)(2,1)} %bitcast.12, bf16[2,64,64,128]{3,2,1,0:T(8,128)(2,1)} %bitcast.11), custom_call_target="tpu_custom_call" | custom-call | flops 8589934592 | bytes 8388608 | tf_op jit(solution)/shard_map/lift/pallas_call | solution.py:374
  16.7 0.0 copy-start.4
  16.7 7.5 %all-to-all-start.1 = ((bf16[32,32,512]{2,1,0:T(8,128)(2,1)}), bf16[32,32,512]{2,1,0:T(8,128)(2,1)S(1)}, u32[]{:S(2)}, u32[]{:S(2)}) async-start(bf16[32,32,512]{2,1,0:T(8,128)(2,1)} %lift.1), calls=%async_computation.1 | async-start | bytes 2097152 | tf_op jit(solution)/shard_map/all_to_all | solution.py:396
  24.2 0.0 collective-permute-done.1.refs_2_
  24.2 0.0 collective-permute-done.refs_1_
  24.2 2.1 %collective-permute-start.2 = (bf16[8,32,256]{2,1,0:T(8,128)(2,1)S(1)}, bf16[8,32,256]{2,1,0:T(8,128)(2,1)S(1)}, u32[]{:S(2)}, u32[]{:S(2)}) collective-permute-start(bf16[8,32,256]{2,1,0:T(8,128)(2,1)S(1)} %pad_maximum_fusion), channel_id=1, source_target_pairs={{0,2},{1,3},{2,4},{3,5},{4,6},{5,7},{6,0},{7,1},{8,10},{9,11},{10,... | collective-permute-start | bytes 393224 | tf_op jit(solution)/shard_map/ppermute | solution.py:366
  26.3 0.0 collective-permute-done.3.refs_6_
  26.3 2.2 %collective-permute-start.4 = (bf16[4,32,256]{2,1,0:T(8,128)(2,1)S(1)}, bf16[4,32,256]{2,1,0:T(8,128)(2,1)S(1)}, u32[]{:S(2)}, u32[]{:S(2)}) collective-permute-start(bf16[4,32,256]{2,1,0:T(8,128)(2,1)S(1)} %collective-permute-done.3.refs_6_), channel_id=1, source_target_pairs={{0,6},{1,7},{2,0},{3,1},{4,2},{5,3},{6,4},{7,5},{8,14},{9,15},{10,... | collective-permute-start | bytes 196616 | tf_op jit(solution)/shard_map/ppermute | solution.py:366
  28.6 1.7 %turn.1.kernels_hbm = bf16[128,128,128]{2,1,0:T(8,128)(2,1)S(1)} custom-call(bf16[2,64,64,128]{3,2,1,0:T(8,128)(2,1)S(1)} %bitcast.7), custom_call_target="tpu_custom_call" | custom-call | flops 2147483648 | bytes 6291456 | tf_op jit(solution)/shard_map/turn/pallas_call | solution.py:442
  30.3 0.0 collective-permute-done.5.refs_5_
  30.3 1.8 %collective-permute-done.4.refs_4_ = bf16[4,32,256]{2,1,0:T(8,128)(2,1)S(1)} collective-permute-done((bf16[4,32,256]{2,1,0:T(8,128)(2,1)S(1)}, bf16[4,32,256]{2,1,0:T(8,128)(2,1)S(1)}, u32[]{:S(2)}, u32[]{:S(2)}) %collective-permute-start.4) | collective-permute-done | bytes 65568 | tf_op jit(solution)/shard_map/ppermute | solution.py:366
  32.1 3.0 %collective-permute-done.2.refs_3_ = bf16[8,32,256]{2,1,0:T(8,128)(2,1)S(1)} collective-permute-done((bf16[8,32,256]{2,1,0:T(8,128)(2,1)S(1)}, bf16[8,32,256]{2,1,0:T(8,128)(2,1)S(1)}, u32[]{:S(2)}, u32[]{:S(2)}) %collective-permute-start.2) | collective-permute-done | bytes 131104 | tf_op jit(solution)/shard_map/ppermute | solution.py:366
  35.2 0.2 pack.1
  35.4 0.1 collective-permute-start.6
  35.5 5.1 %collective-permute-start.7 = (bf16[8,32,256]{2,1,0:T(8,128)(2,1)S(1)}, bf16[8,32,256]{2,1,0:T(8,128)(2,1)S(1)}, u32[]{:S(2)}, u32[]{:S(2)}) collective-permute-start(bf16[8,32,256]{2,1,0:T(8,128)(2,1)S(1)} %get-tuple-element.10), channel_id=1, source_target_pairs={{8,0},{16,8},{24,16},{32,24},{40,32},{48,40},{56,48},{64,56},{72,6... | collective-permute-start | bytes 393224 | tf_op jit(solution)/shard_map/ppermute | solution.py:413
  40.5 0.0 copy-done.3
  40.5 1.5 %inner.1.inner_ref = bf16[8,16,128]{2,1,0:T(8,128)(2,1)S(1)} custom-call(s32[9,32]{1,0:T(8,128)S(1)} %bitcast.8, bf16[32,32,256]{2,1,0:T(8,128)(2,1)S(1)} %get-tuple-element.8.own_ref, bf16[32,9,2,16,128]{4,3,2,1,0:T(8,128)(2,1)S(1)} %copy-done.3), custom_call_target="tpu_custom_call" | custom-call | flops 2147483648 | bytes 2097152 | tf_op jit(solution)/shard_map/inner/pallas_call | solution.py:417
  42.0 1.3 %collective-permute-done.6.before_ref = bf16[8,32,256]{2,1,0:T(8,128)(2,1)S(1)} collective-permute-done((bf16[8,32,256]{2,1,0:T(8,128)(2,1)S(1)}, bf16[8,32,256]{2,1,0:T(8,128)(2,1)S(1)}, u32[]{:S(2)}, u32[]{:S(2)}) %collective-permute-start.6) | collective-permute-done | bytes 131104 | tf_op jit(solution)/shard_map/ppermute | solution.py:412
  43.4 0.0 collective-permute-done.7.after_ref
  43.4 2.2 %outer.1 = bf16[8,32,128]{2,1,0:T(8,128)(2,1)} custom-call(s32[9,32]{1,0:T(8,128)S(1)} %bitcast.9, bf16[32,32,256]{2,1,0:T(8,128)(2,1)S(1)} %get-tuple-element.8.own_ref, bf16[8,32,256]{2,1,0:T(8,128)(2,1)S(1)} %collective-permute-done.6.before_ref, bf16[8,32,256]{2,1,0:T(8,128)(2,1)S(1)} %collective-permute-done.7.after_ref, ...), custom_call_target="tpu_custom_call" | custom-call | flops 68719476736 | bytes 2097152 | tf_op jit(solution)/shard_map/outer/pallas_call | solution.py:427
  45.6 0.0 all-to-all-done.1
  45.6 6.6 %all-to-all-start = ((bf16[8,32,128]{2,1,0:T(8,128)(2,1)}), bf16[8,32,128]{2,1,0:T(8,128)(2,1)S(1)}, u32[]{:S(2)}, u32[]{:S(2)}) async-start(bf16[8,32,128]{2,1,0:T(8,128)(2,1)} %outer.1), calls=%async_computation | async-start | bytes 131072 | tf_op jit(solution)/shard_map/all_to_all | solution.py:440
  52.2 8.8 %far.1.far_ref = f32[2,128,128]{2,1,0:T(8,128)} custom-call(s32[32,1024]{1,0:T(8,128)} %bitcast.14, bf16[1024,512]{1,0:T(8,128)(2,1)} %bitcast.10, bf16[128,128,128]{2,1,0:T(8,128)(2,1)} %copy-done.6, bf16[32,2,64,128]{3,2,1,0:T(8,128)(2,1)} %bitcast.13), custom_call_target="tpu_custom_call" | custom-call | flops 8589934592 | bytes 8388608 | tf_op jit(solution)/shard_map/far/pallas_call | solution.py:453
  61.0 0.0 all-to-all-done.near_ref
  61.0 0.0 copy-start.1
  61.0 0.9 %copy-done.1 = f32[2,128,128]{2,1,0:T(8,128)S(1)} copy-done((f32[2,128,128]{2,1,0:T(8,128)S(1)}, f32[2,128,128]{2,1,0:T(8,128)}, u32[]{:S(2)}) %copy-start.1) | copy-done | bytes 131096
  61.9 1.4 %finish.1 = f32[4,32,256]{2,1,0:T(8,128)} custom-call(s32[32]{0:T(128)S(1)} %copy-done.2, bf16[8,32,128]{2,1,0:T(8,128)(2,1)S(1)} %all-to-all-done.near_ref, f32[2,128,128]{2,1,0:T(8,128)S(1)} %copy-done.1), custom_call_target="tpu_custom_call" | custom-call | tf_op jit(solution)/shard_map/finish/pallas_call | solution.py:472
  (13 shorter events, 0.0 us)
Async XLA Ops:
  1.5 28.8 %collective-permute-start.5 = (bf16[4,32,256]{2,1,0:T(8,128)(2,1)}, bf16[4,32,256]{2,1,0:T(8,128)(2,1)S(1)}, u32[]{:S(2)}, u32[]{:S(2)}) collective-permute-start(bf16[4,32,256]{2,1,0:T(8,128)(2,1)} %mask.1.refs_0_.masked_hbm), channel_id=1, source_target_pairs={{0,6},{1,7},{2,0},{3,1},{4,2},{5,3},{6,4},{7,5},{8,14},{9,15},{10,... | collective-permute-start | bytes 196616 | tf_op jit(solution)/shard_map/ppermute | solution.py:366
  6.9 19.4 %collective-permute-start.3 = (bf16[4,32,256]{2,1,0:T(8,128)(2,1)}, bf16[4,32,256]{2,1,0:T(8,128)(2,1)S(1)}, u32[]{:S(2)}, u32[]{:S(2)}) collective-permute-start(bf16[4,32,256]{2,1,0:T(8,128)(2,1)} %mask.1.refs_0_.masked_hbm), channel_id=1, source_target_pairs={{0,7},{1,0},{2,1},{3,2},{4,3},{5,4},{6,5},{7,6},{8,15},{9,8},{10,9... | collective-permute-start | bytes 196616 | tf_op jit(solution)/shard_map/ppermute | solution.py:366
  7.9 16.3 %collective-permute-start.1 = (bf16[4,32,256]{2,1,0:T(8,128)(2,1)}, bf16[4,32,256]{2,1,0:T(8,128)(2,1)S(1)}, u32[]{:S(2)}, u32[]{:S(2)}) collective-permute-start(bf16[4,32,256]{2,1,0:T(8,128)(2,1)} %mask.1.refs_0_.masked_hbm), channel_id=1, source_target_pairs={{0,2},{1,3},{2,4},{3,5},{4,6},{5,7},{6,0},{7,1},{8,10},{9,11},{10,... | collective-permute-start | bytes 196616 | tf_op jit(solution)/shard_map/ppermute | solution.py:366
  7.9 16.3 %collective-permute-start = (bf16[4,32,256]{2,1,0:T(8,128)(2,1)}, bf16[4,32,256]{2,1,0:T(8,128)(2,1)S(1)}, u32[]{:S(2)}, u32[]{:S(2)}) collective-permute-start(bf16[4,32,256]{2,1,0:T(8,128)(2,1)} %mask.1.refs_0_.masked_hbm), channel_id=1, source_target_pairs={{0,1},{1,2},{2,3},{3,4},{4,5},{5,6},{6,7},{7,0},{8,9},{9,10},{10,1... | collective-permute-start | bytes 196616 | tf_op jit(solution)/shard_map/ppermute | solution.py:366
  16.7 11.8 %copy-start.4 = (bf16[128,2,64,64]{0,3,2,1:T(8,128)(2,1)S(1)}, bf16[128,2,64,64]{0,3,2,1:T(8,128)(2,1)}, u32[]{:S(2)}) copy-start(bf16[128,2,64,64]{0,3,2,1:T(8,128)(2,1)} %param.17) | copy-start | bytes 6291460
  16.7 28.8 %all-to-all-start.1 = ((bf16[32,32,512]{2,1,0:T(8,128)(2,1)}), bf16[32,32,512]{2,1,0:T(8,128)(2,1)S(1)}, u32[]{:S(2)}, u32[]{:S(2)}) async-start(bf16[32,32,512]{2,1,0:T(8,128)(2,1)} %lift.1), calls=%async_computation.1 | async-start | bytes 2097152 | tf_op jit(solution)/shard_map/all_to_all | solution.py:396
  24.2 11.0 %collective-permute-start.2 = (bf16[8,32,256]{2,1,0:T(8,128)(2,1)S(1)}, bf16[8,32,256]{2,1,0:T(8,128)(2,1)S(1)}, u32[]{:S(2)}, u32[]{:S(2)}) collective-permute-start(bf16[8,32,256]{2,1,0:T(8,128)(2,1)S(1)} %pad_maximum_fusion), channel_id=1, source_target_pairs={{0,2},{1,3},{2,4},{3,5},{4,6},{5,7},{6,0},{7,1},{8,10},{9,11},{10,... | collective-permute-start | bytes 393224 | tf_op jit(solution)/shard_map/ppermute | solution.py:366
  26.3 5.8 %collective-permute-start.4 = (bf16[4,32,256]{2,1,0:T(8,128)(2,1)S(1)}, bf16[4,32,256]{2,1,0:T(8,128)(2,1)S(1)}, u32[]{:S(2)}, u32[]{:S(2)}) collective-permute-start(bf16[4,32,256]{2,1,0:T(8,128)(2,1)S(1)} %collective-permute-done.3.refs_6_), channel_id=1, source_target_pairs={{0,6},{1,7},{2,0},{3,1},{4,2},{5,3},{6,4},{7,5},{8,14},{9,15},{10,... | collective-permute-start | bytes 196616 | tf_op jit(solution)/shard_map/ppermute | solution.py:366
  28.5 6.6 %copy-start = (bf16[4,32,256]{2,1,0:T(8,128)(2,1)S(1)}, bf16[4,32,256]{2,1,0:T(8,128)(2,1)}, u32[]{:S(2)}) copy-start(bf16[4,32,256]{2,1,0:T(8,128)(2,1)} %mask.1.refs_0_.masked_hbm) | copy-start | bytes 196612
  28.5 12.0 %copy-start.3 = (bf16[32,9,2,16,128]{4,3,2,1,0:T(8,128)(2,1)S(1)}, bf16[32,9,2,16,128]{4,3,2,1,0:T(8,128)(2,1)}, u32[]{:S(2)}) copy-start(bf16[32,9,2,16,128]{4,3,2,1,0:T(8,128)(2,1)} %blocks_ref.3) | copy-start | bytes 7077892
  28.5 12.0 %copy-start.5 = (s32[32,9]{0,1:T(8,128)S(1)}, s32[32,9]{0,1:T(8,128)}, u32[]{:S(2)}) copy-start(s32[32,9]{0,1:T(8,128)} %param.12) | copy-start | bytes 3460
  30.3 11.7 %copy-start.6 = (bf16[128,128,128]{2,1,0:T(8,128)(2,1)}, bf16[128,128,128]{2,1,0:T(8,128)(2,1)S(1)}, u32[]{:S(2)}) copy-start(bf16[128,128,128]{2,1,0:T(8,128)(2,1)S(1)} %turn.1.kernels_hbm) | copy-start | bytes 12582916
  35.4 8.0 %collective-permute-start.6 = (bf16[8,32,256]{2,1,0:T(8,128)(2,1)S(1)}, bf16[8,32,256]{2,1,0:T(8,128)(2,1)S(1)}, u32[]{:S(2)}, u32[]{:S(2)}) collective-permute-start(bf16[8,32,256]{2,1,0:T(8,128)(2,1)S(1)} %get-tuple-element.9), channel_id=1, source_target_pairs={{0,8},{8,16},{16,24},{24,32},{32,40},{40,48},{48,56},{56,64},{64,7... | collective-permute-start | bytes 393224 | tf_op jit(solution)/shard_map/ppermute | solution.py:412
  35.5 7.9 %collective-permute-start.7 = (bf16[8,32,256]{2,1,0:T(8,128)(2,1)S(1)}, bf16[8,32,256]{2,1,0:T(8,128)(2,1)S(1)}, u32[]{:S(2)}, u32[]{:S(2)}) collective-permute-start(bf16[8,32,256]{2,1,0:T(8,128)(2,1)S(1)} %get-tuple-element.10), channel_id=1, source_target_pairs={{8,0},{16,8},{24,16},{32,24},{40,32},{48,40},{56,48},{64,56},{72,6... | collective-permute-start | bytes 393224 | tf_op jit(solution)/shard_map/ppermute | solution.py:413
  45.6 6.6 %copy-start.7 = (bf16[32,32,512]{2,1,0:T(8,128)(2,1)}, bf16[32,32,512]{2,1,0:T(8,128)(2,1)S(1)}, u32[]{:S(2)}) copy-start(bf16[32,32,512]{2,1,0:T(8,128)(2,1)S(1)} %all-to-all-done.1) | copy-start | bytes 3145732
  45.6 15.4 %all-to-all-start = ((bf16[8,32,128]{2,1,0:T(8,128)(2,1)}), bf16[8,32,128]{2,1,0:T(8,128)(2,1)S(1)}, u32[]{:S(2)}, u32[]{:S(2)}) async-start(bf16[8,32,128]{2,1,0:T(8,128)(2,1)} %outer.1), calls=%async_computation | async-start | bytes 131072 | tf_op jit(solution)/shard_map/all_to_all | solution.py:440
  52.2 8.8 %copy-start.2 = (s32[32]{0:T(128)S(1)}, s32[32]{0:T(128)}, u32[]{:S(2)}) copy-start(s32[32]{0:T(128)} %counts_ref.3) | copy-start | bytes 388
  61.0 0.9 %copy-start.1 = (f32[2,128,128]{2,1,0:T(8,128)S(1)}, f32[2,128,128]{2,1,0:T(8,128)}, u32[]{:S(2)}) copy-start(f32[2,128,128]{2,1,0:T(8,128)} %far.1.far_ref) | copy-start | bytes 393220

commit v4 on v3

--- a/solution.py
+++ b/solution.py
@@ -47,24 +47,26 @@
     return jnp.concatenate(parts, axis=0)
 
 
-def turn_kernels(kernels_ref, turned):
+def turn_kernels(kernels_ref, turned, first, count):
     _, rank, _, kernel_count = kernels_ref.shape
 
-    def one(r, _):
+    def one(step, _):
+        r = first + step
         real, imag = kernels_ref[0, r], kernels_ref[1, r]
         turned[pl.ds(r, kernel_count, stride=PITCH), :] = above(real, imag).T.astype(F32)
         turned[pl.ds(rank + r, kernel_count, stride=PITCH), :] = above(-imag, real).T.astype(F32)
         return 0
 
-    lax.fori_loop(0, rank, one, 0, unroll=16)
+    lax.fori_loop(0, count, one, 0, unroll=16)
 
 
 def lift_kernel(
-    maps_ref,
+    maps_hbm,
     masked_hbm,
     bases_hbm,
     kernels_hbm,
     out_hbm,
+    maps_ref,
     masked_ref,
     bases_ref,
     kernels_ref,
@@ -77,12 +79,23 @@
     arrived,
     sent,
 ):
-    load_masked = pltpu.make_async_copy(masked_hbm, masked_ref, arrived.at[2])
+    quarter = kernels_ref.shape[1] // 4
+
+    def load_kernels(i):
+        part = pl.ds(i * quarter, quarter)
+        return pltpu.make_async_copy(kernels_hbm.at[:, part], kernels_ref.at[:, part], arrived.at[i])
+
+    load_masked = pltpu.make_async_copy(masked_hbm, masked_ref, arrived.at[4])
+    load_bases = pltpu.make_async_copy(bases_hbm, bases_ref, arrived.at[5])
+    load_maps = pltpu.make_async_copy(maps_hbm, maps_ref, arrived.at[6])
+    for i in range(4):
+        load_kernels(i).start()
     load_masked.start()
-    load_bases = pltpu.make_async_copy(bases_hbm, bases_ref, arrived.at[0])
-    load_kernels = pltpu.make_async_copy(kernels_hbm, kernels_ref, arrived.at[1])
     load_bases.start()
-    load_kernels.start()
+    load_maps.start()
+    for i in range(4):
+        load_kernels(i).wait()
+        turn_kernels(kernels_ref, turned, i * quarter, quarter)
     load_masked.wait()
     angles, boxes, doubled = masked_ref.shape
     points = doubled // 2
@@ -106,8 +119,6 @@
     lane = lax.broadcasted_iota(jnp.int32, crossed.shape, 1)
     straight = raw[:, 0].reshape(boxes * angles, wide)
     coef = (straight + jnp.where(lane < rank, -crossed, crossed)).astype(BF16)
-    load_kernels.wait()
-    turn_kernels(kernels_ref, turned)
 
     def pair(step, _):
         k = 2 * step
@@ -119,6 +130,7 @@
 
     lax.fori_loop(0, kernel_count // 2, pair, 0, unroll=True)
     pitch = boxes + 1
+    load_maps.wait()
 
     def one_group(g, slot):
         for box in range(boxes):
@@ -230,7 +242,7 @@
 
 
 def turn_kernel(kernels_ref, out_ref, turned):
-    turn_kernels(kernels_ref, turned)
+    turn_kernels(kernels_ref, turned, 0, kernels_ref.shape[1])
     wide = out_ref.shape[1]
 
     def one(k, _):
@@ -374,9 +386,10 @@
     pieces = pl.pallas_call(
         lift_kernel,
         out_shape=jax.ShapeDtypeStruct((leaves, boxes, angles * wide), BF16),
-        in_specs=[SMEM, ANY, ANY, ANY],
+        in_specs=[ANY, ANY, ANY, ANY],
         out_specs=ANY,
         scratch_shapes=[
+            pltpu.SMEM((boxes, leaves), jnp.int32),
             pltpu.VMEM((angles, boxes, doubled), BF16),
             pltpu.VMEM((boxes, 2, rank, points), BF16),
             pltpu.VMEM((2, rank, rank, kernel_count), BF16),
@@ -386,7 +399,7 @@
             pltpu.VMEM((kernel_count * PITCH, wide), F32),
             pltpu.VMEM((kernel_count, boxes * angles, wide), F32),
             pltpu.VMEM((4, angles * (boxes + 1) + angles, wide), F32),
-            pltpu.SemaphoreType.DMA((3,)),
+            pltpu.SemaphoreType.DMA((7,)),
             pltpu.SemaphoreType.DMA((leaves // 4,)),
         ],
         compiler_params=params(60),

time: 63.7 us -> 62.5 us (0.981)
  Pallas kernels: 25 us -> 23.9 us
    pallas_call x1, Pallas kernels: 7.76 us -> 6.64 us  [shards(): pl.pallas_call(lift_kernel, out_shape=jax.ShapeDtypeStruct((leaves, boxes...]
  transfers between devices with their start and end apart: 10 -> 10, of which waited for: 3 -> 3; matrix products, arithmetic and copies ran while one was open for 0% -> 0% of each run, Pallas kernels for 35% -> 34%
where the time goes in v4:
time: 62.5 us; the launch traced here: 62.2 us
  starting transfers between devices  31 us (50%)
  Pallas kernels  23.9 us (38%)
  waiting for transfers between devices  6.23 us (10%)
  local copies, waits for them, and re-layouts  0.93 us (1%)
    ppermute x6, starting transfers between devices, passed(): lax.ppermute(x, 'rhs', [(i, (i + steps) % parts) for i in range(parts)])  11.7 us
    pallas_call x1, Pallas kernels, shards(): pl.pallas_call(far_kernel, out_shape=jax.ShapeDtypeStruct((2, angles * bo...  8.78 us
    all_to_all x1, starting transfers between devices, shards(): lax.all_to_all(pieces, 'leaf', split_axis=0, concat_axis=0, tiled=True)  7.47 us
    pallas_call x1, Pallas kernels, shards(): pl.pallas_call(lift_kernel, out_shape=jax.ShapeDtypeStruct((leaves, boxes...  6.64 us
    all_to_all x1, starting transfers between devices, shards(): near = lax.all_to_all(rows, 'rhs', split_axis=0, concat_axis=0, tiled=True)  6.62 us
    ppermute x1, starting transfers between devices, shards(): lax.ppermute(head, 'leaf', [((i + 1) % leaves, i) for i in range(leaves)])  5.05 us
    ppermute x6, waiting for transfers between devices, passed(): lax.ppermute(x, 'rhs', [(i, (i + steps) % parts) for i in range(parts)])  4.89 us
    pallas_call x1, Pallas kernels, shards(): pl.pallas_call(outer_kernel, out_shape=jax.ShapeDtypeStruct((parts, boxes...  2.2 us
  transfers between devices with their start and end apart: 10, of which 3 were waited for; matrix products, arithmetic and copies ran while one was open for 0% of the time, Pallas kernels for 34%

profile of v4, /device:TPU:32, one launch (start us, length us, event | category | flops | bytes accessed | tf_op | source)
XLA Modules:
  0.0 62.2 jit_solution(15866554690097496380)
XLA Ops:
  0.0 1.5 %mask.1.refs_0_.masked_hbm = bf16[4,32,256]{2,1,0:T(8,128)(2,1)} custom-call(s32[32]{0:T(128)} %counts_ref.3, bf16[4,32,256]{2,1,0:T(8,128)(2,1)} %currents_ref.1), custom_call_target="tpu_custom_call" | custom-call | tf_op jit(solution)/shard_map/mask/pallas_call | solution.py:368
  1.5 5.4 %collective-permute-start.5 = (bf16[4,32,256]{2,1,0:T(8,128)(2,1)}, bf16[4,32,256]{2,1,0:T(8,128)(2,1)S(1)}, u32[]{:S(2)}, u32[]{:S(2)}) collective-permute-start(bf16[4,32,256]{2,1,0:T(8,128)(2,1)} %mask.1.refs_0_.masked_hbm), channel_id=1, source_target_pairs={{0,6},{1,7},{2,0},{3,1},{4,2},{5,3},{6,4},{7,5},{8,14},{9,15},{10,... | collective-permute-start | bytes 196616 | tf_op jit(solution)/shard_map/ppermute | solution.py:378
  6.9 1.0 %collective-permute-start.3 = (bf16[4,32,256]{2,1,0:T(8,128)(2,1)}, bf16[4,32,256]{2,1,0:T(8,128)(2,1)S(1)}, u32[]{:S(2)}, u32[]{:S(2)}) collective-permute-start(bf16[4,32,256]{2,1,0:T(8,128)(2,1)} %mask.1.refs_0_.masked_hbm), channel_id=1, source_target_pairs={{0,7},{1,0},{2,1},{3,2},{4,3},{5,4},{6,5},{7,6},{8,15},{9,8},{10,9... | collective-permute-start | bytes 196616 | tf_op jit(solution)/shard_map/ppermute | solution.py:378
  7.9 0.0 collective-permute-start.1
  7.9 1.0 %collective-permute-start = (bf16[4,32,256]{2,1,0:T(8,128)(2,1)}, bf16[4,32,256]{2,1,0:T(8,128)(2,1)S(1)}, u32[]{:S(2)}, u32[]{:S(2)}) collective-permute-start(bf16[4,32,256]{2,1,0:T(8,128)(2,1)} %mask.1.refs_0_.masked_hbm), channel_id=1, source_target_pairs={{0,1},{1,2},{2,3},{3,4},{4,5},{5,6},{6,7},{7,0},{8,9},{9,10},{10,1... | collective-permute-start | bytes 196616 | tf_op jit(solution)/shard_map/ppermute | solution.py:378
  8.9 6.6 %lift.1 = bf16[32,32,512]{2,1,0:T(8,128)(2,1)} custom-call(s32[32,32]{1,0:T(8,128)} %maps_hbm.1, bf16[4,32,256]{2,1,0:T(8,128)(2,1)} %mask.1.refs_0_.masked_hbm, bf16[32,2,64,128]{3,2,1,0:T(8,128)(2,1)} %bitcast.12, bf16[2,64,64,128]{3,2,1,0:T(8,128)(2,1)} %bitcast.11), custom_call_target="tpu_custom_call" | custom-call | flops 8589934592 | bytes 8388608 | tf_op jit(solution)/shard_map/lift/pallas_call | solution.py:386
  15.6 0.0 copy-start.4
  15.6 7.5 %all-to-all-start.1 = ((bf16[32,32,512]{2,1,0:T(8,128)(2,1)}), bf16[32,32,512]{2,1,0:T(8,128)(2,1)S(1)}, u32[]{:S(2)}, u32[]{:S(2)}) async-start(bf16[32,32,512]{2,1,0:T(8,128)(2,1)} %lift.1), calls=%async_computation.1 | async-start | bytes 2097152 | tf_op jit(solution)/shard_map/all_to_all | solution.py:409
  23.1 0.0 collective-permute-done.1.refs_2_
  23.1 0.0 collective-permute-done.refs_1_
  23.1 2.1 %collective-permute-start.2 = (bf16[8,32,256]{2,1,0:T(8,128)(2,1)S(1)}, bf16[8,32,256]{2,1,0:T(8,128)(2,1)S(1)}, u32[]{:S(2)}, u32[]{:S(2)}) collective-permute-start(bf16[8,32,256]{2,1,0:T(8,128)(2,1)S(1)} %pad_maximum_fusion), channel_id=1, source_target_pairs={{0,2},{1,3},{2,4},{3,5},{4,6},{5,7},{6,0},{7,1},{8,10},{9,11},{10,... | collective-permute-start | bytes 393224 | tf_op jit(solution)/shard_map/ppermute | solution.py:378
  25.2 0.0 collective-permute-done.3.refs_6_
  25.2 2.2 %collective-permute-start.4 = (bf16[4,32,256]{2,1,0:T(8,128)(2,1)S(1)}, bf16[4,32,256]{2,1,0:T(8,128)(2,1)S(1)}, u32[]{:S(2)}, u32[]{:S(2)}) collective-permute-start(bf16[4,32,256]{2,1,0:T(8,128)(2,1)S(1)} %collective-permute-done.3.refs_6_), channel_id=1, source_target_pairs={{0,6},{1,7},{2,0},{3,1},{4,2},{5,3},{6,4},{7,5},{8,14},{9,15},{10,... | collective-permute-start | bytes 196616 | tf_op jit(solution)/shard_map/ppermute | solution.py:378
  27.4 1.7 %turn.1.kernels_hbm = bf16[128,128,128]{2,1,0:T(8,128)(2,1)S(1)} custom-call(bf16[2,64,64,128]{3,2,1,0:T(8,128)(2,1)S(1)} %bitcast.7), custom_call_target="tpu_custom_call" | custom-call | flops 2147483648 | bytes 6291456 | tf_op jit(solution)/shard_map/turn/pallas_call | solution.py:455
  29.2 0.0 collective-permute-done.5.refs_5_
  29.2 1.8 %collective-permute-done.4.refs_4_ = bf16[4,32,256]{2,1,0:T(8,128)(2,1)S(1)} collective-permute-done((bf16[4,32,256]{2,1,0:T(8,128)(2,1)S(1)}, bf16[4,32,256]{2,1,0:T(8,128)(2,1)S(1)}, u32[]{:S(2)}, u32[]{:S(2)}) %collective-permute-start.4) | collective-permute-done | bytes 65568 | tf_op jit(solution)/shard_map/ppermute | solution.py:378
  31.0 3.0 %collective-permute-done.2.refs_3_ = bf16[8,32,256]{2,1,0:T(8,128)(2,1)S(1)} collective-permute-done((bf16[8,32,256]{2,1,0:T(8,128)(2,1)S(1)}, bf16[8,32,256]{2,1,0:T(8,128)(2,1)S(1)}, u32[]{:S(2)}, u32[]{:S(2)}) %collective-permute-start.2) | collective-permute-done | bytes 131104 | tf_op jit(solution)/shard_map/ppermute | solution.py:378
  34.1 0.0 copy-done
  34.1 0.2 pack.1
  34.3 0.1 collective-permute-start.6
  34.3 5.1 %collective-permute-start.7 = (bf16[8,32,256]{2,1,0:T(8,128)(2,1)S(1)}, bf16[8,32,256]{2,1,0:T(8,128)(2,1)S(1)}, u32[]{:S(2)}, u32[]{:S(2)}) collective-permute-start(bf16[8,32,256]{2,1,0:T(8,128)(2,1)S(1)} %get-tuple-element.10), channel_id=1, source_target_pairs={{8,0},{16,8},{24,16},{32,24},{40,32},{48,40},{56,48},{64,56},{72,6... | collective-permute-start | bytes 393224 | tf_op jit(solution)/shard_map/ppermute | solution.py:426
  39.4 1.5 %inner.1.inner_ref = bf16[8,16,128]{2,1,0:T(8,128)(2,1)S(1)} custom-call(s32[9,32]{1,0:T(8,128)S(1)} %bitcast.8, bf16[32,32,256]{2,1,0:T(8,128)(2,1)S(1)} %get-tuple-element.8.own_ref, bf16[32,9,2,16,128]{4,3,2,1,0:T(8,128)(2,1)S(1)} %copy-done.3), custom_call_target="tpu_custom_call" | custom-call | flops 2147483648 | bytes 2097152 | tf_op jit(solution)/shard_map/inner/pallas_call | solution.py:430
  40.9 1.3 %collective-permute-done.6.before_ref = bf16[8,32,256]{2,1,0:T(8,128)(2,1)S(1)} collective-permute-done((bf16[8,32,256]{2,1,0:T(8,128)(2,1)S(1)}, bf16[8,32,256]{2,1,0:T(8,128)(2,1)S(1)}, u32[]{:S(2)}, u32[]{:S(2)}) %collective-permute-start.6) | collective-permute-done | bytes 131104 | tf_op jit(solution)/shard_map/ppermute | solution.py:425
  42.2 0.0 collective-permute-done.7.after_ref
  42.2 2.2 %outer.1 = bf16[8,32,128]{2,1,0:T(8,128)(2,1)} custom-call(s32[9,32]{1,0:T(8,128)S(1)} %bitcast.9, bf16[32,32,256]{2,1,0:T(8,128)(2,1)S(1)} %get-tuple-element.8.own_ref, bf16[8,32,256]{2,1,0:T(8,128)(2,1)S(1)} %collective-permute-done.6.before_ref, bf16[8,32,256]{2,1,0:T(8,128)(2,1)S(1)} %collective-permute-done.7.after_ref, ...), custom_call_target="tpu_custom_call" | custom-call | flops 68719476736 | bytes 2097152 | tf_op jit(solution)/shard_map/outer/pallas_call | solution.py:440
  44.4 0.0 all-to-all-done.1
  44.4 6.6 %all-to-all-start = ((bf16[8,32,128]{2,1,0:T(8,128)(2,1)}), bf16[8,32,128]{2,1,0:T(8,128)(2,1)S(1)}, u32[]{:S(2)}, u32[]{:S(2)}) async-start(bf16[8,32,128]{2,1,0:T(8,128)(2,1)} %outer.1), calls=%async_computation | async-start | bytes 131072 | tf_op jit(solution)/shard_map/all_to_all | solution.py:453
  51.1 8.8 %far.1.far_ref = f32[2,128,128]{2,1,0:T(8,128)} custom-call(s32[32,1024]{1,0:T(8,128)} %bitcast.14, bf16[1024,512]{1,0:T(8,128)(2,1)} %bitcast.10, bf16[128,128,128]{2,1,0:T(8,128)(2,1)} %copy-done.6, bf16[32,2,64,128]{3,2,1,0:T(8,128)(2,1)} %bitcast.13), custom_call_target="tpu_custom_call" | custom-call | flops 8589934592 | bytes 8388608 | tf_op jit(solution)/shard_map/far/pallas_call | solution.py:466
  59.9 0.0 all-to-all-done.near_ref
  59.9 0.0 copy-start.1
  59.9 0.9 %copy-done.1 = f32[2,128,128]{2,1,0:T(8,128)S(1)} copy-done((f32[2,128,128]{2,1,0:T(8,128)S(1)}, f32[2,128,128]{2,1,0:T(8,128)}, u32[]{:S(2)}) %copy-start.1) | copy-done | bytes 131096
  60.8 1.4 %finish.1 = f32[4,32,256]{2,1,0:T(8,128)} custom-call(s32[32]{0:T(128)S(1)} %copy-done.2, bf16[8,32,128]{2,1,0:T(8,128)(2,1)S(1)} %all-to-all-done.near_ref, f32[2,128,128]{2,1,0:T(8,128)S(1)} %copy-done.1), custom_call_target="tpu_custom_call" | custom-call | tf_op jit(solution)/shard_map/finish/pallas_call | solution.py:485
  (13 shorter events, 0.0 us)
Async XLA Ops:
  1.5 27.7 %collective-permute-start.5 = (bf16[4,32,256]{2,1,0:T(8,128)(2,1)}, bf16[4,32,256]{2,1,0:T(8,128)(2,1)S(1)}, u32[]{:S(2)}, u32[]{:S(2)}) collective-permute-start(bf16[4,32,256]{2,1,0:T(8,128)(2,1)} %mask.1.refs_0_.masked_hbm), channel_id=1, source_target_pairs={{0,6},{1,7},{2,0},{3,1},{4,2},{5,3},{6,4},{7,5},{8,14},{9,15},{10,... | collective-permute-start | bytes 196616 | tf_op jit(solution)/shard_map/ppermute | solution.py:378
  6.9 18.3 %collective-permute-start.3 = (bf16[4,32,256]{2,1,0:T(8,128)(2,1)}, bf16[4,32,256]{2,1,0:T(8,128)(2,1)S(1)}, u32[]{:S(2)}, u32[]{:S(2)}) collective-permute-start(bf16[4,32,256]{2,1,0:T(8,128)(2,1)} %mask.1.refs_0_.masked_hbm), channel_id=1, source_target_pairs={{0,7},{1,0},{2,1},{3,2},{4,3},{5,4},{6,5},{7,6},{8,15},{9,8},{10,9... | collective-permute-start | bytes 196616 | tf_op jit(solution)/shard_map/ppermute | solution.py:378
  7.9 15.2 %collective-permute-start.1 = (bf16[4,32,256]{2,1,0:T(8,128)(2,1)}, bf16[4,32,256]{2,1,0:T(8,128)(2,1)S(1)}, u32[]{:S(2)}, u32[]{:S(2)}) collective-permute-start(bf16[4,32,256]{2,1,0:T(8,128)(2,1)} %mask.1.refs_0_.masked_hbm), channel_id=1, source_target_pairs={{0,2},{1,3},{2,4},{3,5},{4,6},{5,7},{6,0},{7,1},{8,10},{9,11},{10,... | collective-permute-start | bytes 196616 | tf_op jit(solution)/shard_map/ppermute | solution.py:378
  7.9 15.2 %collective-permute-start = (bf16[4,32,256]{2,1,0:T(8,128)(2,1)}, bf16[4,32,256]{2,1,0:T(8,128)(2,1)S(1)}, u32[]{:S(2)}, u32[]{:S(2)}) collective-permute-start(bf16[4,32,256]{2,1,0:T(8,128)(2,1)} %mask.1.refs_0_.masked_hbm), channel_id=1, source_target_pairs={{0,1},{1,2},{2,3},{3,4},{4,5},{5,6},{6,7},{7,0},{8,9},{9,10},{10,1... | collective-permute-start | bytes 196616 | tf_op jit(solution)/shard_map/ppermute | solution.py:378
  15.6 11.8 %copy-start.4 = (bf16[128,2,64,64]{0,3,2,1:T(8,128)(2,1)S(1)}, bf16[128,2,64,64]{0,3,2,1:T(8,128)(2,1)}, u32[]{:S(2)}) copy-start(bf16[128,2,64,64]{0,3,2,1:T(8,128)(2,1)} %param.17) | copy-start | bytes 6291460
  15.6 28.9 %all-to-all-start.1 = ((bf16[32,32,512]{2,1,0:T(8,128)(2,1)}), bf16[32,32,512]{2,1,0:T(8,128)(2,1)S(1)}, u32[]{:S(2)}, u32[]{:S(2)}) async-start(bf16[32,32,512]{2,1,0:T(8,128)(2,1)} %lift.1), calls=%async_computation.1 | async-start | bytes 2097152 | tf_op jit(solution)/shard_map/all_to_all | solution.py:409
  23.1 11.0 %collective-permute-start.2 = (bf16[8,32,256]{2,1,0:T(8,128)(2,1)S(1)}, bf16[8,32,256]{2,1,0:T(8,128)(2,1)S(1)}, u32[]{:S(2)}, u32[]{:S(2)}) collective-permute-start(bf16[8,32,256]{2,1,0:T(8,128)(2,1)S(1)} %pad_maximum_fusion), channel_id=1, source_target_pairs={{0,2},{1,3},{2,4},{3,5},{4,6},{5,7},{6,0},{7,1},{8,10},{9,11},{10,... | collective-permute-start | bytes 393224 | tf_op jit(solution)/shard_map/ppermute | solution.py:378
  25.2 5.8 %collective-permute-start.4 = (bf16[4,32,256]{2,1,0:T(8,128)(2,1)S(1)}, bf16[4,32,256]{2,1,0:T(8,128)(2,1)S(1)}, u32[]{:S(2)}, u32[]{:S(2)}) collective-permute-start(bf16[4,32,256]{2,1,0:T(8,128)(2,1)S(1)} %collective-permute-done.3.refs_6_), channel_id=1, source_target_pairs={{0,6},{1,7},{2,0},{3,1},{4,2},{5,3},{6,4},{7,5},{8,14},{9,15},{10,... | collective-permute-start | bytes 196616 | tf_op jit(solution)/shard_map/ppermute | solution.py:378
  27.4 6.6 %copy-start = (bf16[4,32,256]{2,1,0:T(8,128)(2,1)S(1)}, bf16[4,32,256]{2,1,0:T(8,128)(2,1)}, u32[]{:S(2)}) copy-start(bf16[4,32,256]{2,1,0:T(8,128)(2,1)} %mask.1.refs_0_.masked_hbm) | copy-start | bytes 196612
  27.4 12.0 %copy-start.3 = (bf16[32,9,2,16,128]{4,3,2,1,0:T(8,128)(2,1)S(1)}, bf16[32,9,2,16,128]{4,3,2,1,0:T(8,128)(2,1)}, u32[]{:S(2)}) copy-start(bf16[32,9,2,16,128]{4,3,2,1,0:T(8,128)(2,1)} %blocks_ref.3) | copy-start | bytes 7077892
  27.4 12.0 %copy-start.5 = (s32[32,9]{0,1:T(8,128)S(1)}, s32[32,9]{0,1:T(8,128)}, u32[]{:S(2)}) copy-start(s32[32,9]{0,1:T(8,128)} %param.12) | copy-start | bytes 3460
  29.2 11.7 %copy-start.6 = (bf16[128,128,128]{2,1,0:T(8,128)(2,1)}, bf16[128,128,128]{2,1,0:T(8,128)(2,1)S(1)}, u32[]{:S(2)}) copy-start(bf16[128,128,128]{2,1,0:T(8,128)(2,1)S(1)} %turn.1.kernels_hbm) | copy-start | bytes 12582916
  34.3 8.0 %collective-permute-start.6 = (bf16[8,32,256]{2,1,0:T(8,128)(2,1)S(1)}, bf16[8,32,256]{2,1,0:T(8,128)(2,1)S(1)}, u32[]{:S(2)}, u32[]{:S(2)}) collective-permute-start(bf16[8,32,256]{2,1,0:T(8,128)(2,1)S(1)} %get-tuple-element.9), channel_id=1, source_target_pairs={{0,8},{8,16},{16,24},{24,32},{32,40},{40,48},{48,56},{56,64},{64,7... | collective-permute-start | bytes 393224 | tf_op jit(solution)/shard_map/ppermute | solution.py:425
  34.3 7.9 %collective-permute-start.7 = (bf16[8,32,256]{2,1,0:T(8,128)(2,1)S(1)}, bf16[8,32,256]{2,1,0:T(8,128)(2,1)S(1)}, u32[]{:S(2)}, u32[]{:S(2)}) collective-permute-start(bf16[8,32,256]{2,1,0:T(8,128)(2,1)S(1)} %get-tuple-element.10), channel_id=1, source_target_pairs={{8,0},{16,8},{24,16},{32,24},{40,32},{48,40},{56,48},{64,56},{72,6... | collective-permute-start | bytes 393224 | tf_op jit(solution)/shard_map/ppermute | solution.py:426
  44.4 6.6 %copy-start.7 = (bf16[32,32,512]{2,1,0:T(8,128)(2,1)}, bf16[32,32,512]{2,1,0:T(8,128)(2,1)S(1)}, u32[]{:S(2)}) copy-start(bf16[32,32,512]{2,1,0:T(8,128)(2,1)S(1)} %all-to-all-done.1) | copy-start | bytes 3145732
  44.4 15.4 %all-to-all-start = ((bf16[8,32,128]{2,1,0:T(8,128)(2,1)}), bf16[8,32,128]{2,1,0:T(8,128)(2,1)S(1)}, u32[]{:S(2)}, u32[]{:S(2)}) async-start(bf16[8,32,128]{2,1,0:T(8,128)(2,1)} %outer.1), calls=%async_computation | async-start | bytes 131072 | tf_op jit(solution)/shard_map/all_to_all | solution.py:453
  51.1 8.8 %copy-start.2 = (s32[32]{0:T(128)S(1)}, s32[32]{0:T(128)}, u32[]{:S(2)}) copy-start(s32[32]{0:T(128)} %counts_ref.3) | copy-start | bytes 388
  59.9 0.9 %copy-start.1 = (f32[2,128,128]{2,1,0:T(8,128)S(1)}, f32[2,128,128]{2,1,0:T(8,128)}, u32[]{:S(2)}) copy-start(f32[2,128,128]{2,1,0:T(8,128)} %far.1.far_ref) | copy-start | bytes 393220

commit v5 on v4

--- a/solution.py
+++ b/solution.py
@@ -28,17 +28,6 @@
     return lane < limit
 
 
-def mask_kernel(counts_ref, currents_ref, masked_ref):
-    angles, boxes, doubled = currents_ref.shape
-    points = doubled // 2
-    live = live_lanes(counts_ref, boxes, points)
-    for a in range(angles):
-        for c in range(2):
-            lanes = slice(c * points, (c + 1) * points)
-            kept = jnp.where(live, currents_ref[a, :, lanes].astype(F32), 0.0).astype(BF16)
-            masked_ref[a, :, lanes] = kept
-
-
 def beside(*parts):
     return jnp.concatenate(parts, axis=1)
 
@@ -61,13 +50,15 @@
 
 
 def lift_kernel(
+    counts_hbm,
     maps_hbm,
-    masked_hbm,
+    currents_hbm,
     bases_hbm,
     kernels_hbm,
     out_hbm,
+    counts_ref,
     maps_ref,
-    masked_ref,
+    currents_ref,
     bases_ref,
     kernels_ref,
     out_ref,
@@ -85,29 +76,32 @@
         part = pl.ds(i * quarter, quarter)
         return pltpu.make_async_copy(kernels_hbm.at[:, part], kernels_ref.at[:, part], arrived.at[i])
 
-    load_masked = pltpu.make_async_copy(masked_hbm, masked_ref, arrived.at[4])
+    load_currents = pltpu.make_async_copy(currents_hbm, currents_ref, arrived.at[4])
+    load_counts = pltpu.make_async_copy(counts_hbm, counts_ref, arrived.at[7])
     load_bases = pltpu.make_async_copy(bases_hbm, bases_ref, arrived.at[5])
     load_maps = pltpu.make_async_copy(maps_hbm, maps_ref, arrived.at[6])
     for i in range(4):
         load_kernels(i).start()
-    load_masked.start()
+    load_currents.start()
+    load_counts.start()
     load_bases.start()
     load_maps.start()
     for i in range(4):
         load_kernels(i).wait()
         turn_kernels(kernels_ref, turned, i * quarter, quarter)
-    load_masked.wait()
-    angles, boxes, doubled = masked_ref.shape
+    load_currents.wait()
+    load_counts.wait()
+    angles, boxes, doubled = currents_ref.shape
     points = doubled // 2
     _, rank, _, kernel_count = kernels_ref.shape
     groups = out_ref.shape[0]
     wide = 2 * rank
     each = 2 * angles
+    live = live_lanes(counts_ref, boxes, points)
     for a in range(angles):
         for c in range(2):
-            rows[pl.ds(c * angles + a, boxes, stride=each), :] = masked_ref[
-                a, :, c * points : (c + 1) * points
-            ].astype(F32)
+            found = currents_ref[a, :, c * points : (c + 1) * points].astype(F32)
+            rows[pl.ds(c * angles + a, boxes, stride=each), :] = jnp.where(live, found, 0.0)
     load_bases.wait()
     for box in range(boxes):
         x = rows[each * box : each * (box + 1), :].astype(BF16)
@@ -158,13 +152,14 @@
         send(step).wait()
 
 
-def pack_kernel(*refs):
+def pack_kernel(counts_ref, *refs):
     every, (out_ref, head_ref, tail_ref, spread) = refs[:7], refs[-4:]
     angles, boxes, doubled = every[0].shape
     points = doubled // 2
     total = out_ref.shape[1]
     parts = total // angles
     pitch = total + 1
+    live = live_lanes(counts_ref, boxes, points)
     me = lax.axis_index("rhs")
     back = 0
     for ref in every:
@@ -173,9 +168,8 @@
             back += 1
             for a in range(angles):
                 for c in range(2):
-                    spread[c, pl.ds(a * parts + z, boxes, stride=pitch), :] = ref[
-                        group * angles + a, :, c * points : (c + 1) * points
-                    ].astype(F32)
+                    found = ref[group * angles + a, :, c * points : (c + 1) * points].astype(F32)
+                    spread[c, pl.ds(a * parts + z, boxes, stride=pitch), :] = jnp.where(live, found, 0.0)
     for box in range(boxes):
         for c in range(2):
             lanes = slice(c * points, (c + 1) * points)
@@ -365,30 +359,22 @@
     kernels_one = level_one.transpose(1, 2, 3, 0)
     kernels_two = level_two.transpose(1, 2, 3, 0)
 
-    masked = pl.pallas_call(
-        mask_kernel,
-        out_shape=jax.ShapeDtypeStruct((angles, boxes, doubled), BF16),
-        in_specs=[SMEM, VMEM],
-        out_specs=VMEM,
-        compiler_params=params(60),
-        name="mask",
-    )(counts, currents)
-
     def passed(x, steps):
         return lax.ppermute(x, "rhs", [(i, (i + steps) % parts) for i in range(parts)])
 
-    back1, ahead1 = passed(masked, 1), passed(masked, -1)
-    back2, ahead2 = passed(masked, 2), passed(masked, -2)
+    back1, ahead1 = passed(currents, 1), passed(currents, -1)
+    back2, ahead2 = passed(currents, 2), passed(currents, -2)
     back34 = passed(jnp.concatenate([back1, back2], axis=0), 2)
     ahead3 = passed(ahead1, -2)
-    every = (masked, back1, back2, back34, ahead3, ahead2, ahead1)
+    every = (currents, back1, back2, back34, ahead3, ahead2, ahead1)
 
     pieces = pl.pallas_call(
         lift_kernel,
         out_shape=jax.ShapeDtypeStruct((leaves, boxes, angles * wide), BF16),
-        in_specs=[ANY, ANY, ANY, ANY],
+        in_specs=[ANY] * 5,
         out_specs=ANY,
         scratch_shapes=[
+            pltpu.SMEM((boxes,), jnp.int32),
             pltpu.SMEM((boxes, leaves), jnp.int32),
             pltpu.VMEM((angles, boxes, doubled), BF16),
             pltpu.VMEM((boxes, 2, rank, points), BF16),
@@ -399,13 +385,13 @@
             pltpu.VMEM((kernel_count * PITCH, wide), F32),
             pltpu.VMEM((kernel_count, boxes * angles, wide), F32),
             pltpu.VMEM((4, angles * (boxes + 1) + angles, wide), F32),
-            pltpu.SemaphoreType.DMA((7,)),
+            pltpu.SemaphoreType.DMA((8,)),
             pltpu.SemaphoreType.DMA((leaves // 4,)),
         ],
         compiler_params=params(60),
         cost_estimate=pl.CostEstimate(flops=2**33, bytes_accessed=8 * 2**20, transcendentals=0),
         name="lift",
-    )(source_maps, masked, lines(source_bases), kernels_one)
+    )(counts, source_maps, currents, lines(source_bases), kernels_one)
     incoming = lax.all_to_all(pieces, "leaf", split_axis=0, concat_axis=0, tiled=True)
 
     total = parts * angles
@@ -416,12 +402,12 @@
             jax.ShapeDtypeStruct((SPAN, total, doubled), BF16),
             jax.ShapeDtypeStruct((SPAN, total, doubled), BF16),
         ),
-        in_specs=[VMEM] * len(every),
+        in_specs=[SMEM] + [VMEM] * len(every),
         out_specs=(VMEM, VMEM, VMEM),
         scratch_shapes=[pltpu.VMEM((2, boxes * (total + 1) + total, points), F32)],
         compiler_params=params(6),
         name="pack",
-    )(*every)
+    )(counts, *every)
     before = lax.ppermute(tail, "leaf", [(i, (i + 1) % leaves) for i in range(leaves)])
     after = lax.ppermute(head, "leaf", [((i + 1) % leaves, i) for i in range(leaves)])
 

time: 62.5 us -> 61 us (0.976)
  Pallas kernels: 23.9 us -> 23 us
    pallas_call x1 -> x0, Pallas kernels: 1.51 us -> none  [shards(): pl.pallas_call(mask_kernel, out_shape=jax.ShapeDtypeStruct((angles, boxes...]
  transfers between devices with their start and end apart: 10 -> 10, of which waited for: 3 -> 3; matrix products, arithmetic and copies ran while one was open for 0% -> 0% of each run, Pallas kernels for 34% -> 36%
where the time goes in v5:
time: 61 us; the launch traced here: 60.7 us
  starting transfers between devices  30.6 us (50%)
  Pallas kernels  23 us (38%)
  waiting for transfers between devices  6.03 us (10%)
  local copies, waits for them, and re-layouts  0.93 us (2%)
    ppermute x6, starting transfers between devices, passed(): lax.ppermute(x, 'rhs', [(i, (i + steps) % parts) for i in range(parts)])  11.7 us
    pallas_call x1, Pallas kernels, shards(): pl.pallas_call(far_kernel, out_shape=jax.ShapeDtypeStruct((2, angles * bo...  8.77 us
    all_to_all x1, starting transfers between devices, shards(): lax.all_to_all(pieces, 'leaf', split_axis=0, concat_axis=0, tiled=True)  7.46 us
    pallas_call x1, Pallas kernels, shards(): pl.pallas_call(lift_kernel, out_shape=jax.ShapeDtypeStruct((leaves, boxes...  6.67 us
    all_to_all x1, starting transfers between devices, shards(): near = lax.all_to_all(rows, 'rhs', split_axis=0, concat_axis=0, tiled=True)  6.24 us
    ppermute x1, starting transfers between devices, shards(): lax.ppermute(head, 'leaf', [((i + 1) % leaves, i) for i in range(leaves)])  5.05 us
    ppermute x6, waiting for transfers between devices, passed(): lax.ppermute(x, 'rhs', [(i, (i + steps) % parts) for i in range(parts)])  4.88 us
    pallas_call x1, Pallas kernels, shards(): pl.pallas_call(outer_kernel, out_shape=jax.ShapeDtypeStruct((parts, boxes...  2.2 us
  transfers between devices with their start and end apart: 10, of which 3 were waited for; matrix products, arithmetic and copies ran while one was open for 0% of the time, Pallas kernels for 36%

profile of v5, /device:TPU:32, one launch (start us, length us, event | category | flops | bytes accessed | tf_op | source)
XLA Modules:
  0.0 60.7 jit_solution(5544387762776589647)
XLA Ops:
  0.0 5.4 %collective-permute-start.5 = (bf16[4,32,256]{2,1,0:T(8,128)(2,1)}, bf16[4,32,256]{2,1,0:T(8,128)(2,1)S(1)}, u32[]{:S(2)}, u32[]{:S(2)}) collective-permute-start(bf16[4,32,256]{2,1,0:T(8,128)(2,1)} %currents_hbm.1), channel_id=1, source_target_pairs={{0,6},{1,7},{2,0},{3,1},{4,2},{5,3},{6,4},{7,5},{8,14},{9,15},{10,... | collective-permute-start | bytes 196616 | tf_op jit(solution)/shard_map/ppermute | solution.py:363
  5.4 1.0 %collective-permute-start.3 = (bf16[4,32,256]{2,1,0:T(8,128)(2,1)}, bf16[4,32,256]{2,1,0:T(8,128)(2,1)S(1)}, u32[]{:S(2)}, u32[]{:S(2)}) collective-permute-start(bf16[4,32,256]{2,1,0:T(8,128)(2,1)} %currents_hbm.1), channel_id=1, source_target_pairs={{0,7},{1,0},{2,1},{3,2},{4,3},{5,4},{6,5},{7,6},{8,15},{9,8},{10,9... | collective-permute-start | bytes 196616 | tf_op jit(solution)/shard_map/ppermute | solution.py:363
  6.4 0.0 collective-permute-start.1
  6.4 1.0 %collective-permute-start = (bf16[4,32,256]{2,1,0:T(8,128)(2,1)}, bf16[4,32,256]{2,1,0:T(8,128)(2,1)S(1)}, u32[]{:S(2)}, u32[]{:S(2)}) collective-permute-start(bf16[4,32,256]{2,1,0:T(8,128)(2,1)} %currents_hbm.1), channel_id=1, source_target_pairs={{0,1},{1,2},{2,3},{3,4},{4,5},{5,6},{6,7},{7,0},{8,9},{9,10},{10,1... | collective-permute-start | bytes 196616 | tf_op jit(solution)/shard_map/ppermute | solution.py:363
  7.4 6.7 %lift.1 = bf16[32,32,512]{2,1,0:T(8,128)(2,1)} custom-call(s32[32]{0:T(128)} %counts_ref.3, s32[32,32]{1,0:T(8,128)} %maps_hbm.1, bf16[4,32,256]{2,1,0:T(8,128)(2,1)} %currents_hbm.1, bf16[32,2,64,128]{3,2,1,0:T(8,128)(2,1)} %bitcast.12, bf16[2,64,64,128]{3,2,1,0:T(8,128)(2,1)} %bitcast.11), custom_call_target="tpu_custom_call" | custom-call | flops 8589934592 | bytes 8388608 | tf_op jit(solution)/shard_map/lift/pallas_call | solution.py:371
  14.1 0.0 copy-start.4
  14.1 7.5 %all-to-all-start.1 = ((bf16[32,32,512]{2,1,0:T(8,128)(2,1)}), bf16[32,32,512]{2,1,0:T(8,128)(2,1)S(1)}, u32[]{:S(2)}, u32[]{:S(2)}) async-start(bf16[32,32,512]{2,1,0:T(8,128)(2,1)} %lift.1), calls=%async_computation.1 | async-start | bytes 2097152 | tf_op jit(solution)/shard_map/all_to_all | solution.py:395
  21.6 0.0 collective-permute-done.1.refs_2_
  21.6 0.0 collective-permute-done.refs_1_
  21.6 2.1 %collective-permute-start.2 = (bf16[8,32,256]{2,1,0:T(8,128)(2,1)S(1)}, bf16[8,32,256]{2,1,0:T(8,128)(2,1)S(1)}, u32[]{:S(2)}, u32[]{:S(2)}) collective-permute-start(bf16[8,32,256]{2,1,0:T(8,128)(2,1)S(1)} %pad_maximum_fusion), channel_id=1, source_target_pairs={{0,2},{1,3},{2,4},{3,5},{4,6},{5,7},{6,0},{7,1},{8,10},{9,11},{10,... | collective-permute-start | bytes 393224 | tf_op jit(solution)/shard_map/ppermute | solution.py:363
  23.7 0.0 collective-permute-done.3.refs_6_
  23.7 2.2 %collective-permute-start.4 = (bf16[4,32,256]{2,1,0:T(8,128)(2,1)S(1)}, bf16[4,32,256]{2,1,0:T(8,128)(2,1)S(1)}, u32[]{:S(2)}, u32[]{:S(2)}) collective-permute-start(bf16[4,32,256]{2,1,0:T(8,128)(2,1)S(1)} %collective-permute-done.3.refs_6_), channel_id=1, source_target_pairs={{0,6},{1,7},{2,0},{3,1},{4,2},{5,3},{6,4},{7,5},{8,14},{9,15},{10,... | collective-permute-start | bytes 196616 | tf_op jit(solution)/shard_map/ppermute | solution.py:363
  26.0 0.0 copy-start.5
  26.0 1.7 %turn.1.kernels_hbm = bf16[128,128,128]{2,1,0:T(8,128)(2,1)S(1)} custom-call(bf16[2,64,64,128]{3,2,1,0:T(8,128)(2,1)S(1)} %bitcast.7), custom_call_target="tpu_custom_call" | custom-call | flops 2147483648 | bytes 6291456 | tf_op jit(solution)/shard_map/turn/pallas_call | solution.py:441
  27.7 0.0 collective-permute-done.5.refs_5_
  27.7 1.8 %collective-permute-done.4.refs_4_ = bf16[4,32,256]{2,1,0:T(8,128)(2,1)S(1)} collective-permute-done((bf16[4,32,256]{2,1,0:T(8,128)(2,1)S(1)}, bf16[4,32,256]{2,1,0:T(8,128)(2,1)S(1)}, u32[]{:S(2)}, u32[]{:S(2)}) %collective-permute-start.4) | collective-permute-done | bytes 65568 | tf_op jit(solution)/shard_map/ppermute | solution.py:363
  29.6 3.0 %collective-permute-done.2.refs_3_ = bf16[8,32,256]{2,1,0:T(8,128)(2,1)S(1)} collective-permute-done((bf16[8,32,256]{2,1,0:T(8,128)(2,1)S(1)}, bf16[8,32,256]{2,1,0:T(8,128)(2,1)S(1)}, u32[]{:S(2)}, u32[]{:S(2)}) %collective-permute-start.2) | collective-permute-done | bytes 131104 | tf_op jit(solution)/shard_map/ppermute | solution.py:363
  32.6 0.7 %pack.1 = (bf16[32,32,256]{2,1,0:T(8,128)(2,1)S(1)}, bf16[8,32,256]{2,1,0:T(8,128)(2,1)S(1)}, bf16[8,32,256]{2,1,0:T(8,128)(2,1)S(1)}) custom-call(s32[32]{0:T(128)S(1)} %copy-done.2, bf16[4,32,256]{2,1,0:T(8,128)(2,1)S(1)} %copy-done.1, bf16[4,32,256]{2,1,0:T(8,128)(2,1)S(1)} %collective-permute-done.refs_1_, ...), custom_call_target="tpu_custom_call" | custom-call | tf_op jit(solution)/shard_map/pack/pallas_call | solution.py:398
  33.3 0.1 collective-permute-start.6
  33.4 5.1 %collective-permute-start.7 = (bf16[8,32,256]{2,1,0:T(8,128)(2,1)S(1)}, bf16[8,32,256]{2,1,0:T(8,128)(2,1)S(1)}, u32[]{:S(2)}, u32[]{:S(2)}) collective-permute-start(bf16[8,32,256]{2,1,0:T(8,128)(2,1)S(1)} %get-tuple-element.10), channel_id=1, source_target_pairs={{8,0},{16,8},{24,16},{32,24},{40,32},{48,40},{56,48},{64,56},{72,6... | collective-permute-start | bytes 393224 | tf_op jit(solution)/shard_map/ppermute | solution.py:412
  38.5 0.0 copy-done.3
  38.5 1.5 %inner.1.inner_ref = bf16[8,16,128]{2,1,0:T(8,128)(2,1)S(1)} custom-call(s32[9,32]{1,0:T(8,128)S(1)} %bitcast.8, bf16[32,32,256]{2,1,0:T(8,128)(2,1)S(1)} %get-tuple-element.8.own_ref, bf16[32,9,2,16,128]{4,3,2,1,0:T(8,128)(2,1)S(1)} %copy-done.3), custom_call_target="tpu_custom_call" | custom-call | flops 2147483648 | bytes 2097152 | tf_op jit(solution)/shard_map/inner/pallas_call | solution.py:416
  40.0 1.1 %collective-permute-done.6.before_ref = bf16[8,32,256]{2,1,0:T(8,128)(2,1)S(1)} collective-permute-done((bf16[8,32,256]{2,1,0:T(8,128)(2,1)S(1)}, bf16[8,32,256]{2,1,0:T(8,128)(2,1)S(1)}, u32[]{:S(2)}, u32[]{:S(2)}) %collective-permute-start.6) | collective-permute-done | bytes 131104 | tf_op jit(solution)/shard_map/ppermute | solution.py:411
  41.1 0.0 collective-permute-done.7.after_ref
  41.1 2.2 %outer.1 = bf16[8,32,128]{2,1,0:T(8,128)(2,1)} custom-call(s32[9,32]{1,0:T(8,128)S(1)} %bitcast.9, bf16[32,32,256]{2,1,0:T(8,128)(2,1)S(1)} %get-tuple-element.8.own_ref, bf16[8,32,256]{2,1,0:T(8,128)(2,1)S(1)} %collective-permute-done.6.before_ref, bf16[8,32,256]{2,1,0:T(8,128)(2,1)S(1)} %collective-permute-done.7.after_ref, ...), custom_call_target="tpu_custom_call" | custom-call | flops 68719476736 | bytes 2097152 | tf_op jit(solution)/shard_map/outer/pallas_call | solution.py:426
  43.3 0.0 all-to-all-done.1
  43.3 6.2 %all-to-all-start = ((bf16[8,32,128]{2,1,0:T(8,128)(2,1)}), bf16[8,32,128]{2,1,0:T(8,128)(2,1)S(1)}, u32[]{:S(2)}, u32[]{:S(2)}) async-start(bf16[8,32,128]{2,1,0:T(8,128)(2,1)} %outer.1), calls=%async_computation | async-start | bytes 131072 | tf_op jit(solution)/shard_map/all_to_all | solution.py:439
  49.6 8.8 %far.1.far_ref = f32[2,128,128]{2,1,0:T(8,128)} custom-call(s32[32,1024]{1,0:T(8,128)} %bitcast.14, bf16[1024,512]{1,0:T(8,128)(2,1)} %bitcast.10, bf16[128,128,128]{2,1,0:T(8,128)(2,1)} %copy-done.6, bf16[32,2,64,128]{3,2,1,0:T(8,128)(2,1)} %bitcast.13), custom_call_target="tpu_custom_call" | custom-call | flops 8589934592 | bytes 8388608 | tf_op jit(solution)/shard_map/far/pallas_call | solution.py:452
  58.4 0.0 all-to-all-done.near_ref
  58.4 0.0 copy-start
  58.4 0.9 %copy-done = f32[2,128,128]{2,1,0:T(8,128)S(1)} copy-done((f32[2,128,128]{2,1,0:T(8,128)S(1)}, f32[2,128,128]{2,1,0:T(8,128)}, u32[]{:S(2)}) %copy-start) | copy-done | bytes 131096
  59.3 1.4 %finish.1 = f32[4,32,256]{2,1,0:T(8,128)} custom-call(s32[32]{0:T(128)S(1)} %copy-done.2, bf16[8,32,128]{2,1,0:T(8,128)(2,1)S(1)} %all-to-all-done.near_ref, f32[2,128,128]{2,1,0:T(8,128)S(1)} %copy-done), custom_call_target="tpu_custom_call" | custom-call | tf_op jit(solution)/shard_map/finish/pallas_call | solution.py:471
  (12 shorter events, 0.0 us)
Async XLA Ops:
  0.0 27.7 %collective-permute-start.5 = (bf16[4,32,256]{2,1,0:T(8,128)(2,1)}, bf16[4,32,256]{2,1,0:T(8,128)(2,1)S(1)}, u32[]{:S(2)}, u32[]{:S(2)}) collective-permute-start(bf16[4,32,256]{2,1,0:T(8,128)(2,1)} %currents_hbm.1), channel_id=1, source_target_pairs={{0,6},{1,7},{2,0},{3,1},{4,2},{5,3},{6,4},{7,5},{8,14},{9,15},{10,... | collective-permute-start | bytes 196616 | tf_op jit(solution)/shard_map/ppermute | solution.py:363
  5.4 18.3 %collective-permute-start.3 = (bf16[4,32,256]{2,1,0:T(8,128)(2,1)}, bf16[4,32,256]{2,1,0:T(8,128)(2,1)S(1)}, u32[]{:S(2)}, u32[]{:S(2)}) collective-permute-start(bf16[4,32,256]{2,1,0:T(8,128)(2,1)} %currents_hbm.1), channel_id=1, source_target_pairs={{0,7},{1,0},{2,1},{3,2},{4,3},{5,4},{6,5},{7,6},{8,15},{9,8},{10,9... | collective-permute-start | bytes 196616 | tf_op jit(solution)/shard_map/ppermute | solution.py:363
  6.4 15.2 %collective-permute-start.1 = (bf16[4,32,256]{2,1,0:T(8,128)(2,1)}, bf16[4,32,256]{2,1,0:T(8,128)(2,1)S(1)}, u32[]{:S(2)}, u32[]{:S(2)}) collective-permute-start(bf16[4,32,256]{2,1,0:T(8,128)(2,1)} %currents_hbm.1), channel_id=1, source_target_pairs={{0,2},{1,3},{2,4},{3,5},{4,6},{5,7},{6,0},{7,1},{8,10},{9,11},{10,... | collective-permute-start | bytes 196616 | tf_op jit(solution)/shard_map/ppermute | solution.py:363
  6.4 15.2 %collective-permute-start = (bf16[4,32,256]{2,1,0:T(8,128)(2,1)}, bf16[4,32,256]{2,1,0:T(8,128)(2,1)S(1)}, u32[]{:S(2)}, u32[]{:S(2)}) collective-permute-start(bf16[4,32,256]{2,1,0:T(8,128)(2,1)} %currents_hbm.1), channel_id=1, source_target_pairs={{0,1},{1,2},{2,3},{3,4},{4,5},{5,6},{6,7},{7,0},{8,9},{9,10},{10,1... | collective-permute-start | bytes 196616 | tf_op jit(solution)/shard_map/ppermute | solution.py:363
  14.1 11.8 %copy-start.4 = (bf16[128,2,64,64]{0,3,2,1:T(8,128)(2,1)S(1)}, bf16[128,2,64,64]{0,3,2,1:T(8,128)(2,1)}, u32[]{:S(2)}) copy-start(bf16[128,2,64,64]{0,3,2,1:T(8,128)(2,1)} %param.17) | copy-start | bytes 6291460
  14.1 29.2 %all-to-all-start.1 = ((bf16[32,32,512]{2,1,0:T(8,128)(2,1)}), bf16[32,32,512]{2,1,0:T(8,128)(2,1)S(1)}, u32[]{:S(2)}, u32[]{:S(2)}) async-start(bf16[32,32,512]{2,1,0:T(8,128)(2,1)} %lift.1), calls=%async_computation.1 | async-start | bytes 2097152 | tf_op jit(solution)/shard_map/all_to_all | solution.py:395
  21.6 11.0 %collective-permute-start.2 = (bf16[8,32,256]{2,1,0:T(8,128)(2,1)S(1)}, bf16[8,32,256]{2,1,0:T(8,128)(2,1)S(1)}, u32[]{:S(2)}, u32[]{:S(2)}) collective-permute-start(bf16[8,32,256]{2,1,0:T(8,128)(2,1)S(1)} %pad_maximum_fusion), channel_id=1, source_target_pairs={{0,2},{1,3},{2,4},{3,5},{4,6},{5,7},{6,0},{7,1},{8,10},{9,11},{10,... | collective-permute-start | bytes 393224 | tf_op jit(solution)/shard_map/ppermute | solution.py:363
  23.7 5.8 %collective-permute-start.4 = (bf16[4,32,256]{2,1,0:T(8,128)(2,1)S(1)}, bf16[4,32,256]{2,1,0:T(8,128)(2,1)S(1)}, u32[]{:S(2)}, u32[]{:S(2)}) collective-permute-start(bf16[4,32,256]{2,1,0:T(8,128)(2,1)S(1)} %collective-permute-done.3.refs_6_), channel_id=1, source_target_pairs={{0,6},{1,7},{2,0},{3,1},{4,2},{5,3},{6,4},{7,5},{8,14},{9,15},{10,... | collective-permute-start | bytes 196616 | tf_op jit(solution)/shard_map/ppermute | solution.py:363
  25.9 6.6 %copy-start.1 = (bf16[4,32,256]{2,1,0:T(8,128)(2,1)S(1)}, bf16[4,32,256]{2,1,0:T(8,128)(2,1)}, u32[]{:S(2)}) copy-start(bf16[4,32,256]{2,1,0:T(8,128)(2,1)} %currents_hbm.1) | copy-start | bytes 196612
  26.0 6.6 %copy-start.2 = (s32[32]{0:T(128)S(1)}, s32[32]{0:T(128)}, u32[]{:S(2)}) copy-start(s32[32]{0:T(128)} %counts_ref.3) | copy-start | bytes 388
  26.0 12.5 %copy-start.3 = (bf16[32,9,2,16,128]{4,3,2,1,0:T(8,128)(2,1)S(1)}, bf16[32,9,2,16,128]{4,3,2,1,0:T(8,128)(2,1)}, u32[]{:S(2)}) copy-start(bf16[32,9,2,16,128]{4,3,2,1,0:T(8,128)(2,1)} %blocks_ref.3) | copy-start | bytes 7077892
  26.0 12.5 %copy-start.5 = (s32[32,9]{0,1:T(8,128)S(1)}, s32[32,9]{0,1:T(8,128)}, u32[]{:S(2)}) copy-start(s32[32,9]{0,1:T(8,128)} %param.12) | copy-start | bytes 3460
  27.7 12.3 %copy-start.6 = (bf16[128,128,128]{2,1,0:T(8,128)(2,1)}, bf16[128,128,128]{2,1,0:T(8,128)(2,1)S(1)}, u32[]{:S(2)}) copy-start(bf16[128,128,128]{2,1,0:T(8,128)(2,1)S(1)} %turn.1.kernels_hbm) | copy-start | bytes 12582916
  33.3 7.8 %collective-permute-start.6 = (bf16[8,32,256]{2,1,0:T(8,128)(2,1)S(1)}, bf16[8,32,256]{2,1,0:T(8,128)(2,1)S(1)}, u32[]{:S(2)}, u32[]{:S(2)}) collective-permute-start(bf16[8,32,256]{2,1,0:T(8,128)(2,1)S(1)} %get-tuple-element.9), channel_id=1, source_target_pairs={{0,8},{8,16},{16,24},{24,32},{32,40},{40,48},{48,56},{56,64},{64,7... | collective-permute-start | bytes 393224 | tf_op jit(solution)/shard_map/ppermute | solution.py:411
  33.4 7.7 %collective-permute-start.7 = (bf16[8,32,256]{2,1,0:T(8,128)(2,1)S(1)}, bf16[8,32,256]{2,1,0:T(8,128)(2,1)S(1)}, u32[]{:S(2)}, u32[]{:S(2)}) collective-permute-start(bf16[8,32,256]{2,1,0:T(8,128)(2,1)S(1)} %get-tuple-element.10), channel_id=1, source_target_pairs={{8,0},{16,8},{24,16},{32,24},{40,32},{48,40},{56,48},{64,56},{72,6... | collective-permute-start | bytes 393224 | tf_op jit(solution)/shard_map/ppermute | solution.py:412
  43.3 6.2 %copy-start.7 = (bf16[32,32,512]{2,1,0:T(8,128)(2,1)}, bf16[32,32,512]{2,1,0:T(8,128)(2,1)S(1)}, u32[]{:S(2)}) copy-start(bf16[32,32,512]{2,1,0:T(8,128)(2,1)S(1)} %all-to-all-done.1) | copy-start | bytes 3145732
  43.3 15.0 %all-to-all-start = ((bf16[8,32,128]{2,1,0:T(8,128)(2,1)}), bf16[8,32,128]{2,1,0:T(8,128)(2,1)S(1)}, u32[]{:S(2)}, u32[]{:S(2)}) async-start(bf16[8,32,128]{2,1,0:T(8,128)(2,1)} %outer.1), calls=%async_computation | async-start | bytes 131072 | tf_op jit(solution)/shard_map/all_to_all | solution.py:439
  58.4 0.9 %copy-start = (f32[2,128,128]{2,1,0:T(8,128)S(1)}, f32[2,128,128]{2,1,0:T(8,128)}, u32[]{:S(2)}) copy-start(f32[2,128,128]{2,1,0:T(8,128)} %far.1.far_ref) | copy-start | bytes 393220

commit v6 on v5

--- a/solution.py
+++ b/solution.py
@@ -463,7 +463,7 @@
             pltpu.VMEM((angles * boxes, wide), F32),
             pltpu.SemaphoreType.DMA((kernel_count // CHUNK + 3,)),
         ],
-        compiler_params=params(60),
+        compiler_params=params(48),
         cost_estimate=pl.CostEstimate(flops=2**33, bytes_accessed=8 * 2**20, transcendentals=0),
         name="far",
     )(target_maps.T, incoming.reshape(leaves * boxes, angles * wide), turned, lines(target_bases))

time: 61 us -> 58.4 us (0.957)
  Pallas kernels: 23 us -> 21.3 us
  local copies, waits for them, and re-layouts: 0.93 us -> 0.04 us
    pallas_call x1, Pallas kernels: 8.77 us -> 7.14 us  [shards(): pl.pallas_call(far_kernel, out_shape=jax.ShapeDtypeStruct((2, angles * bo...]
    unnamed x16, local copies, waits for them, and re-layouts: 0.93 us -> 0.04 us
  transfers between devices with their start and end apart: 10 -> 10, of which waited for: 3 -> 3; matrix products, arithmetic and copies ran while one was open for 0% -> 0% of each run, Pallas kernels for 36% -> 34%
where the time goes in v6:
time: 58.4 us; the launch traced here: 58.1 us
  starting transfers between devices  30.6 us (52%)
  Pallas kernels  21.3 us (36%)
  waiting for transfers between devices  6.01 us (10%)
    ppermute x6, starting transfers between devices, passed(): lax.ppermute(x, 'rhs', [(i, (i + steps) % parts) for i in range(parts)])  11.7 us
    all_to_all x1, starting transfers between devices, shards(): lax.all_to_all(pieces, 'leaf', split_axis=0, concat_axis=0, tiled=True)  7.46 us
    pallas_call x1, Pallas kernels, shards(): pl.pallas_call(far_kernel, out_shape=jax.ShapeDtypeStruct((2, angles * bo...  7.14 us
    pallas_call x1, Pallas kernels, shards(): pl.pallas_call(lift_kernel, out_shape=jax.ShapeDtypeStruct((leaves, boxes...  6.67 us
    all_to_all x1, starting transfers between devices, shards(): near = lax.all_to_all(rows, 'rhs', split_axis=0, concat_axis=0, tiled=True)  6.24 us
    ppermute x1, starting transfers between devices, shards(): lax.ppermute(head, 'leaf', [((i + 1) % leaves, i) for i in range(leaves)])  5.05 us
    ppermute x6, waiting for transfers between devices, passed(): lax.ppermute(x, 'rhs', [(i, (i + steps) % parts) for i in range(parts)])  4.88 us
    pallas_call x1, Pallas kernels, shards(): pl.pallas_call(outer_kernel, out_shape=jax.ShapeDtypeStruct((parts, boxes...  2.18 us
  transfers between devices with their start and end apart: 10, of which 3 were waited for; matrix products, arithmetic and copies ran while one was open for 0% of the time, Pallas kernels for 34%

profile of v6, /device:TPU:32, one launch (start us, length us, event | category | flops | bytes accessed | tf_op | source)
XLA Modules:
  0.0 58.1 jit_solution(2414506299862105118)
XLA Ops:
  0.0 5.4 %collective-permute-start.5 = (bf16[4,32,256]{2,1,0:T(8,128)(2,1)}, bf16[4,32,256]{2,1,0:T(8,128)(2,1)S(1)}, u32[]{:S(2)}, u32[]{:S(2)}) collective-permute-start(bf16[4,32,256]{2,1,0:T(8,128)(2,1)} %currents_hbm.1), channel_id=1, source_target_pairs={{0,6},{1,7},{2,0},{3,1},{4,2},{5,3},{6,4},{7,5},{8,14},{9,15},{10,... | collective-permute-start | bytes 196616 | tf_op jit(solution)/shard_map/ppermute | solution.py:363
  5.4 1.0 %collective-permute-start.3 = (bf16[4,32,256]{2,1,0:T(8,128)(2,1)}, bf16[4,32,256]{2,1,0:T(8,128)(2,1)S(1)}, u32[]{:S(2)}, u32[]{:S(2)}) collective-permute-start(bf16[4,32,256]{2,1,0:T(8,128)(2,1)} %currents_hbm.1), channel_id=1, source_target_pairs={{0,7},{1,0},{2,1},{3,2},{4,3},{5,4},{6,5},{7,6},{8,15},{9,8},{10,9... | collective-permute-start | bytes 196616 | tf_op jit(solution)/shard_map/ppermute | solution.py:363
  6.4 0.0 collective-permute-start.1
  6.4 1.0 %collective-permute-start = (bf16[4,32,256]{2,1,0:T(8,128)(2,1)}, bf16[4,32,256]{2,1,0:T(8,128)(2,1)S(1)}, u32[]{:S(2)}, u32[]{:S(2)}) collective-permute-start(bf16[4,32,256]{2,1,0:T(8,128)(2,1)} %currents_hbm.1), channel_id=1, source_target_pairs={{0,1},{1,2},{2,3},{3,4},{4,5},{5,6},{6,7},{7,0},{8,9},{9,10},{10,1... | collective-permute-start | bytes 196616 | tf_op jit(solution)/shard_map/ppermute | solution.py:363
  7.4 6.7 %lift.1 = bf16[32,32,512]{2,1,0:T(8,128)(2,1)} custom-call(s32[32]{0:T(128)} %counts_ref.3, s32[32,32]{1,0:T(8,128)} %maps_hbm.1, bf16[4,32,256]{2,1,0:T(8,128)(2,1)} %currents_hbm.1, bf16[32,2,64,128]{3,2,1,0:T(8,128)(2,1)} %bitcast.14, bf16[2,64,64,128]{3,2,1,0:T(8,128)(2,1)} %bitcast.13), custom_call_target="tpu_custom_call" | custom-call | flops 8589934592 | bytes 8388608 | tf_op jit(solution)/shard_map/lift/pallas_call | solution.py:371
  14.1 0.0 copy-start.3
  14.1 7.5 %all-to-all-start.1 = ((bf16[32,32,512]{2,1,0:T(8,128)(2,1)}), bf16[32,32,512]{2,1,0:T(8,128)(2,1)S(1)}, u32[]{:S(2)}, u32[]{:S(2)}) async-start(bf16[32,32,512]{2,1,0:T(8,128)(2,1)} %lift.1), calls=%async_computation.1 | async-start | bytes 2097152 | tf_op jit(solution)/shard_map/all_to_all | solution.py:395
  21.6 0.0 collective-permute-done.1.refs_2_
  21.6 0.0 collective-permute-done.refs_1_
  21.6 2.1 %collective-permute-start.2 = (bf16[8,32,256]{2,1,0:T(8,128)(2,1)S(1)}, bf16[8,32,256]{2,1,0:T(8,128)(2,1)S(1)}, u32[]{:S(2)}, u32[]{:S(2)}) collective-permute-start(bf16[8,32,256]{2,1,0:T(8,128)(2,1)S(1)} %pad_maximum_fusion), channel_id=1, source_target_pairs={{0,2},{1,3},{2,4},{3,5},{4,6},{5,7},{6,0},{7,1},{8,10},{9,11},{10,... | collective-permute-start | bytes 393224 | tf_op jit(solution)/shard_map/ppermute | solution.py:363
  23.7 0.0 collective-permute-done.3.refs_6_
  23.7 2.2 %collective-permute-start.4 = (bf16[4,32,256]{2,1,0:T(8,128)(2,1)S(1)}, bf16[4,32,256]{2,1,0:T(8,128)(2,1)S(1)}, u32[]{:S(2)}, u32[]{:S(2)}) collective-permute-start(bf16[4,32,256]{2,1,0:T(8,128)(2,1)S(1)} %collective-permute-done.3.refs_6_), channel_id=1, source_target_pairs={{0,6},{1,7},{2,0},{3,1},{4,2},{5,3},{6,4},{7,5},{8,14},{9,15},{10,... | collective-permute-start | bytes 196616 | tf_op jit(solution)/shard_map/ppermute | solution.py:363
  26.0 0.0 copy-start.6
  26.0 1.7 %turn.1.kernels_hbm = bf16[128,128,128]{2,1,0:T(8,128)(2,1)S(1)} custom-call(bf16[2,64,64,128]{3,2,1,0:T(8,128)(2,1)S(1)} %bitcast.8), custom_call_target="tpu_custom_call" | custom-call | flops 2147483648 | bytes 6291456 | tf_op jit(solution)/shard_map/turn/pallas_call | solution.py:441
  27.7 0.0 collective-permute-done.5.refs_5_
  27.7 1.8 %collective-permute-done.4.refs_4_ = bf16[4,32,256]{2,1,0:T(8,128)(2,1)S(1)} collective-permute-done((bf16[4,32,256]{2,1,0:T(8,128)(2,1)S(1)}, bf16[4,32,256]{2,1,0:T(8,128)(2,1)S(1)}, u32[]{:S(2)}, u32[]{:S(2)}) %collective-permute-start.4) | collective-permute-done | bytes 65568 | tf_op jit(solution)/shard_map/ppermute | solution.py:363
  29.6 3.0 %collective-permute-done.2.refs_3_ = bf16[8,32,256]{2,1,0:T(8,128)(2,1)S(1)} collective-permute-done((bf16[8,32,256]{2,1,0:T(8,128)(2,1)S(1)}, bf16[8,32,256]{2,1,0:T(8,128)(2,1)S(1)}, u32[]{:S(2)}, u32[]{:S(2)}) %collective-permute-start.2) | collective-permute-done | bytes 131104 | tf_op jit(solution)/shard_map/ppermute | solution.py:363
  32.6 0.7 %pack.1 = (bf16[32,32,256]{2,1,0:T(8,128)(2,1)S(1)}, bf16[8,32,256]{2,1,0:T(8,128)(2,1)S(1)}, bf16[8,32,256]{2,1,0:T(8,128)(2,1)S(1)}) custom-call(s32[32]{0:T(128)S(1)} %copy-done.1, bf16[4,32,256]{2,1,0:T(8,128)(2,1)S(1)} %copy-done, bf16[4,32,256]{2,1,0:T(8,128)(2,1)S(1)} %collective-permute-done.refs_1_, ...), custom_call_target="tpu_custom_call" | custom-call | tf_op jit(solution)/shard_map/pack/pallas_call | solution.py:398
  33.3 0.1 collective-permute-start.6
  33.4 5.1 %collective-permute-start.7 = (bf16[8,32,256]{2,1,0:T(8,128)(2,1)S(1)}, bf16[8,32,256]{2,1,0:T(8,128)(2,1)S(1)}, u32[]{:S(2)}, u32[]{:S(2)}) collective-permute-start(bf16[8,32,256]{2,1,0:T(8,128)(2,1)S(1)} %get-tuple-element.10), channel_id=1, source_target_pairs={{8,0},{16,8},{24,16},{32,24},{40,32},{48,40},{56,48},{64,56},{72,6... | collective-permute-start | bytes 393224 | tf_op jit(solution)/shard_map/ppermute | solution.py:412
  38.5 0.0 copy-done.2
  38.5 1.5 %inner.1.inner_ref = bf16[8,16,128]{2,1,0:T(8,128)(2,1)S(1)} custom-call(s32[9,32]{1,0:T(8,128)S(1)} %bitcast.11, bf16[32,32,256]{2,1,0:T(8,128)(2,1)S(1)} %get-tuple-element.8.own_ref, bf16[32,9,2,16,128]{4,3,2,1,0:T(8,128)(2,1)S(1)} %copy-done.2), custom_call_target="tpu_custom_call" | custom-call | flops 2147483648 | bytes 2097152 | tf_op jit(solution)/shard_map/inner/pallas_call | solution.py:416
  40.0 0.0 copy-start.4
  40.0 0.0 copy-start.5
  40.0 1.1 %collective-permute-done.6.before_ref = bf16[8,32,256]{2,1,0:T(8,128)(2,1)S(1)} collective-permute-done((bf16[8,32,256]{2,1,0:T(8,128)(2,1)S(1)}, bf16[8,32,256]{2,1,0:T(8,128)(2,1)S(1)}, u32[]{:S(2)}, u32[]{:S(2)}) %collective-permute-start.6) | collective-permute-done | bytes 131104 | tf_op jit(solution)/shard_map/ppermute | solution.py:411
  41.1 0.0 collective-permute-done.7.after_ref
  41.1 2.2 %outer.1 = bf16[8,32,128]{2,1,0:T(8,128)(2,1)} custom-call(s32[9,32]{1,0:T(8,128)S(1)} %bitcast.12, bf16[32,32,256]{2,1,0:T(8,128)(2,1)S(1)} %get-tuple-element.8.own_ref, bf16[8,32,256]{2,1,0:T(8,128)(2,1)S(1)} %collective-permute-done.6.before_ref, bf16[8,32,256]{2,1,0:T(8,128)(2,1)S(1)} %collective-permute-done.7.after_ref, ...), custom_call_target="tpu_custom_call" | custom-call | flops 68719476736 | bytes 2097152 | tf_op jit(solution)/shard_map/outer/pallas_call | solution.py:426
  43.3 0.0 all-to-all-done.1
  43.3 6.2 %all-to-all-start = ((bf16[8,32,128]{2,1,0:T(8,128)(2,1)}), bf16[8,32,128]{2,1,0:T(8,128)(2,1)S(1)}, u32[]{:S(2)}, u32[]{:S(2)}) async-start(bf16[8,32,128]{2,1,0:T(8,128)(2,1)} %outer.1), calls=%async_computation | async-start | bytes 131072 | tf_op jit(solution)/shard_map/all_to_all | solution.py:439
  49.6 7.1 %far.1.far_ref = f32[2,128,128]{2,1,0:T(8,128)S(1)} custom-call(s32[32,1024]{1,0:T(8,128)S(1)} %bitcast.10, bf16[1024,512]{1,0:T(8,128)(2,1)S(1)} %bitcast.7, bf16[128,128,128]{2,1,0:T(8,128)(2,1)} %copy-done.7, bf16[32,2,64,128]{3,2,1,0:T(8,128)(2,1)S(1)} %bitcast.9), custom_call_target="tpu_custom_call" | custom-call | flops 8589934592 | bytes 8388608 | tf_op jit(solution)/shard_map/far/pallas_call | solution.py:452
  56.7 0.0 all-to-all-done.near_ref
  56.7 1.4 %finish.1 = f32[4,32,256]{2,1,0:T(8,128)} custom-call(s32[32]{0:T(128)S(1)} %copy-done.1, bf16[8,32,128]{2,1,0:T(8,128)(2,1)S(1)} %all-to-all-done.near_ref, f32[2,128,128]{2,1,0:T(8,128)S(1)} %far.1.far_ref), custom_call_target="tpu_custom_call" | custom-call | tf_op jit(solution)/shard_map/finish/pallas_call | solution.py:471
  (12 shorter events, 0.0 us)
Async XLA Ops:
  0.0 27.7 %collective-permute-start.5 = (bf16[4,32,256]{2,1,0:T(8,128)(2,1)}, bf16[4,32,256]{2,1,0:T(8,128)(2,1)S(1)}, u32[]{:S(2)}, u32[]{:S(2)}) collective-permute-start(bf16[4,32,256]{2,1,0:T(8,128)(2,1)} %currents_hbm.1), channel_id=1, source_target_pairs={{0,6},{1,7},{2,0},{3,1},{4,2},{5,3},{6,4},{7,5},{8,14},{9,15},{10,... | collective-permute-start | bytes 196616 | tf_op jit(solution)/shard_map/ppermute | solution.py:363
  5.4 18.3 %collective-permute-start.3 = (bf16[4,32,256]{2,1,0:T(8,128)(2,1)}, bf16[4,32,256]{2,1,0:T(8,128)(2,1)S(1)}, u32[]{:S(2)}, u32[]{:S(2)}) collective-permute-start(bf16[4,32,256]{2,1,0:T(8,128)(2,1)} %currents_hbm.1), channel_id=1, source_target_pairs={{0,7},{1,0},{2,1},{3,2},{4,3},{5,4},{6,5},{7,6},{8,15},{9,8},{10,9... | collective-permute-start | bytes 196616 | tf_op jit(solution)/shard_map/ppermute | solution.py:363
  6.4 15.2 %collective-permute-start.1 = (bf16[4,32,256]{2,1,0:T(8,128)(2,1)}, bf16[4,32,256]{2,1,0:T(8,128)(2,1)S(1)}, u32[]{:S(2)}, u32[]{:S(2)}) collective-permute-start(bf16[4,32,256]{2,1,0:T(8,128)(2,1)} %currents_hbm.1), channel_id=1, source_target_pairs={{0,2},{1,3},{2,4},{3,5},{4,6},{5,7},{6,0},{7,1},{8,10},{9,11},{10,... | collective-permute-start | bytes 196616 | tf_op jit(solution)/shard_map/ppermute | solution.py:363
  6.4 15.2 %collective-permute-start = (bf16[4,32,256]{2,1,0:T(8,128)(2,1)}, bf16[4,32,256]{2,1,0:T(8,128)(2,1)S(1)}, u32[]{:S(2)}, u32[]{:S(2)}) collective-permute-start(bf16[4,32,256]{2,1,0:T(8,128)(2,1)} %currents_hbm.1), channel_id=1, source_target_pairs={{0,1},{1,2},{2,3},{3,4},{4,5},{5,6},{6,7},{7,0},{8,9},{9,10},{10,1... | collective-permute-start | bytes 196616 | tf_op jit(solution)/shard_map/ppermute | solution.py:363
  14.1 11.8 %copy-start.3 = (bf16[128,2,64,64]{0,3,2,1:T(8,128)(2,1)S(1)}, bf16[128,2,64,64]{0,3,2,1:T(8,128)(2,1)}, u32[]{:S(2)}) copy-start(bf16[128,2,64,64]{0,3,2,1:T(8,128)(2,1)} %param.17) | copy-start | bytes 6291460
  14.1 29.2 %all-to-all-start.1 = ((bf16[32,32,512]{2,1,0:T(8,128)(2,1)}), bf16[32,32,512]{2,1,0:T(8,128)(2,1)S(1)}, u32[]{:S(2)}, u32[]{:S(2)}) async-start(bf16[32,32,512]{2,1,0:T(8,128)(2,1)} %lift.1), calls=%async_computation.1 | async-start | bytes 2097152 | tf_op jit(solution)/shard_map/all_to_all | solution.py:395
  21.6 11.0 %collective-permute-start.2 = (bf16[8,32,256]{2,1,0:T(8,128)(2,1)S(1)}, bf16[8,32,256]{2,1,0:T(8,128)(2,1)S(1)}, u32[]{:S(2)}, u32[]{:S(2)}) collective-permute-start(bf16[8,32,256]{2,1,0:T(8,128)(2,1)S(1)} %pad_maximum_fusion), channel_id=1, source_target_pairs={{0,2},{1,3},{2,4},{3,5},{4,6},{5,7},{6,0},{7,1},{8,10},{9,11},{10,... | collective-permute-start | bytes 393224 | tf_op jit(solution)/shard_map/ppermute | solution.py:363
  23.7 5.8 %collective-permute-start.4 = (bf16[4,32,256]{2,1,0:T(8,128)(2,1)S(1)}, bf16[4,32,256]{2,1,0:T(8,128)(2,1)S(1)}, u32[]{:S(2)}, u32[]{:S(2)}) collective-permute-start(bf16[4,32,256]{2,1,0:T(8,128)(2,1)S(1)} %collective-permute-done.3.refs_6_), channel_id=1, source_target_pairs={{0,6},{1,7},{2,0},{3,1},{4,2},{5,3},{6,4},{7,5},{8,14},{9,15},{10,... | collective-permute-start | bytes 196616 | tf_op jit(solution)/shard_map/ppermute | solution.py:363
  25.9 6.6 %copy-start = (bf16[4,32,256]{2,1,0:T(8,128)(2,1)S(1)}, bf16[4,32,256]{2,1,0:T(8,128)(2,1)}, u32[]{:S(2)}) copy-start(bf16[4,32,256]{2,1,0:T(8,128)(2,1)} %currents_hbm.1) | copy-start | bytes 196612
  26.0 6.6 %copy-start.1 = (s32[32]{0:T(128)S(1)}, s32[32]{0:T(128)}, u32[]{:S(2)}) copy-start(s32[32]{0:T(128)} %counts_ref.3) | copy-start | bytes 388
  26.0 12.5 %copy-start.2 = (bf16[32,9,2,16,128]{4,3,2,1,0:T(8,128)(2,1)S(1)}, bf16[32,9,2,16,128]{4,3,2,1,0:T(8,128)(2,1)}, u32[]{:S(2)}) copy-start(bf16[32,9,2,16,128]{4,3,2,1,0:T(8,128)(2,1)} %blocks_ref.3) | copy-start | bytes 7077892
  26.0 12.5 %copy-start.6 = (s32[32,9]{0,1:T(8,128)S(1)}, s32[32,9]{0,1:T(8,128)}, u32[]{:S(2)}) copy-start(s32[32,9]{0,1:T(8,128)} %param.12) | copy-start | bytes 3460
  27.7 12.3 %copy-start.7 = (bf16[128,128,128]{2,1,0:T(8,128)(2,1)}, bf16[128,128,128]{2,1,0:T(8,128)(2,1)S(1)}, u32[]{:S(2)}) copy-start(bf16[128,128,128]{2,1,0:T(8,128)(2,1)S(1)} %turn.1.kernels_hbm) | copy-start | bytes 12582916
  33.3 7.8 %collective-permute-start.6 = (bf16[8,32,256]{2,1,0:T(8,128)(2,1)S(1)}, bf16[8,32,256]{2,1,0:T(8,128)(2,1)S(1)}, u32[]{:S(2)}, u32[]{:S(2)}) collective-permute-start(bf16[8,32,256]{2,1,0:T(8,128)(2,1)S(1)} %get-tuple-element.9), channel_id=1, source_target_pairs={{0,8},{8,16},{16,24},{24,32},{32,40},{40,48},{48,56},{56,64},{64,7... | collective-permute-start | bytes 393224 | tf_op jit(solution)/shard_map/ppermute | solution.py:411
  33.4 7.7 %collective-permute-start.7 = (bf16[8,32,256]{2,1,0:T(8,128)(2,1)S(1)}, bf16[8,32,256]{2,1,0:T(8,128)(2,1)S(1)}, u32[]{:S(2)}, u32[]{:S(2)}) collective-permute-start(bf16[8,32,256]{2,1,0:T(8,128)(2,1)S(1)} %get-tuple-element.10), channel_id=1, source_target_pairs={{8,0},{16,8},{24,16},{32,24},{40,32},{48,40},{56,48},{64,56},{72,6... | collective-permute-start | bytes 393224 | tf_op jit(solution)/shard_map/ppermute | solution.py:412
  40.0 9.6 %copy-start.4 = (bf16[32,2,128,64]{2,3,1,0:T(8,128)(2,1)S(1)}, bf16[32,2,128,64]{2,3,1,0:T(8,128)(2,1)}, u32[]{:S(2)}) copy-start(bf16[32,2,128,64]{2,3,1,0:T(8,128)(2,1)} %param.18) | copy-start | bytes 3145732
  40.0 9.6 %copy-start.5 = (s32[1024,32]{0,1:T(8,128)S(1)}, s32[1024,32]{0,1:T(8,128)}, u32[]{:S(2)}) copy-start(s32[1024,32]{0,1:T(8,128)} %param.14) | copy-start | bytes 393220
  43.3 13.4 %all-to-all-start = ((bf16[8,32,128]{2,1,0:T(8,128)(2,1)}), bf16[8,32,128]{2,1,0:T(8,128)(2,1)S(1)}, u32[]{:S(2)}, u32[]{:S(2)}) async-start(bf16[8,32,128]{2,1,0:T(8,128)(2,1)} %outer.1), calls=%async_computation | async-start | bytes 131072 | tf_op jit(solution)/shard_map/all_to_all | solution.py:439
